TPU v7x, 256 devices: a whole 4x4x8 slice. The times are simulated.
256 devices in a mesh: tm: 32 (over y, z), chan: 8 (over x, core).
Axes of the slice: x: 4, y: 4, z: 8, core: 2. Of those that a mesh axis runs over, the one named last changes fastest.
Arguments:
- observations: bfloat16 [8192, 8192], P('tm', 'chan'), may hold values from -6 to 6
- emission: bfloat16 [8192, 256], P('chan'), may hold values from -0.0625 to 0.0625
- noise_precision: float32 [8192], P('chan'), may hold values from 0.3 to 3
- transition: float32 [256, 256], replicated, may hold values from -1 to 1
- info_gain: float32 [256, 256], replicated, may hold values from -2 to 2
- smoother_gain: float32 [256, 256], replicated, may hold values from -1 to 1
- smoother_input: float32 [256, 256], replicated, may hold values from -0.1 to 0.1
Outputs:
- smoothed: float32 [8192, 256], P('tm')
- cross_stat: float32 [8192, 256], P('chan')
- noise_var: float32 [8192], P('chan')
- state_moment: float32 [256, 256], replicated
All inputs are finite; a program needn't handle non-finite values.
Results may differ from a plain program's by a relative error of at most 0.0039.
Values sent between devices are 32-bit elements; how exact they have to be, the bound alone decides.
No kernel may reach another device: no remote copies, remote signals or barrier semaphores. Data moves between devices by JAX's collectives and lax.ppermute only.
A program may use at most 256 MiB of HBM per device.

v0:
```python
import functools
import math

import jax
import jax.numpy as jnp
import numpy as np
from jax import lax
from jax.experimental import pallas as pl
from jax.experimental.pallas import tpu as pltpu
from jax.sharding import Mesh, PartitionSpec as P

N_Y, N_Z, N_X, N_CORE = 4, 8, 4, 2
BLOCKS = N_Y * N_Z
SUB = 8
F32, BF16 = jnp.float32, jnp.bfloat16
KERNELS = True


class Late:
    def __init__(self, buffer, copies):
        self.buffer, self.copies, self.shape = buffer, copies, buffer.shape

    def __getitem__(self, key):
        while self.copies:
            self.copies.pop().wait()
        return self.buffer[key]


def pieces_of(shape):
    count = 4 if shape[0] >= 256 else 1
    return [(i * (shape[0] // count), shape[0] // count) for i in range(count)]


def call(body, outs, *args, large=(), sent=(), limit=16):
    if not KERNELS:
        results = [jnp.zeros(shape, dtype) for shape, dtype in outs]
        for i, place, value in body(*args):
            if place is None:
                results[i] = value
            elif isinstance(place, int):
                results[i] = results[i].at[place].set(value)
            else:
                results[i] = results[i].at[place[0] : place[0] + place[1]].set(value)
        return results

    n_in, n_out = len(args), len(outs)

    def kernel(*refs):
        values, out_refs, rest = list(refs[:n_in]), refs[n_in : n_in + n_out], refs[n_in + n_out :]
        targets = dict(zip(sent, rest[len(large) : -2]))
        in_sems, out_sems = rest[-2:]
        number = 0
        for i, buffer in zip(large, rest[: len(large)]):
            copies = []
            for start, size in pieces_of(buffer.shape):
                rows = pl.ds(start, size)
                copies.append(
                    pltpu.make_async_copy(refs[i].at[rows], buffer.at[rows], in_sems.at[number])
                )
                copies[-1].start()
                number += 1
            values[i] = Late(buffer, copies)
        leaving = []
        for i, place, value in body(*values):
            index = Ellipsis if place is None else place
            if isinstance(place, tuple):
                index = pl.ds(place[0], place[1])
            if i not in sent:
                out_refs[i][index] = value
                continue
            buffer = targets[i]
            buffer[index] = value
            spans = pieces_of(value.shape) if place is None else [place]
            for start, size in spans:
                rows = pl.ds(start, size)
                leaving.append(
                    pltpu.make_async_copy(
                        buffer.at[rows], out_refs[i].at[rows], out_sems.at[len(leaving)]
                    )
                )
                leaving[-1].start()
        for copy in leaving:
            copy.wait()

    args = [
        pltpu.with_memory_space_constraint(arg, pltpu.HBM if i in large else pltpu.VMEM)
        for i, arg in enumerate(args)
    ]
    vmem, far = pl.BlockSpec(memory_space=pltpu.VMEM), pl.BlockSpec(memory_space=pltpu.HBM)
    return pl.pallas_call(
        kernel,
        out_shape=[(pltpu.HBM if i in sent else pltpu.VMEM)(*kind) for i, kind in enumerate(outs)],
        in_specs=[far if i in large else vmem for i in range(n_in)],
        out_specs=[far if i in sent else vmem for i in range(n_out)],
        scratch_shapes=[pltpu.VMEM(args[i].shape, args[i].dtype) for i in large]
        + [pltpu.VMEM(*outs[i]) for i in sent]
        + [pltpu.SemaphoreType.DMA((32,)), pltpu.SemaphoreType.DMA((32,))],
        compiler_params=pltpu.CompilerParams(vmem_limit_bytes=limit * 2**20),
        name=body.__name__,
    )(*args)


def roll(rows, by):
    if KERNELS:
        return pltpu.roll(rows, by % rows.shape[0], 0)
    return jnp.roll(rows, by, 0)


def roll_lanes(rows, by):
    if KERNELS:
        return pltpu.roll(rows, by, 1)
    return jnp.roll(rows, by, 1)


def row_index(rows):
    return lax.broadcasted_iota(jnp.int32, rows.shape, 0)


def dot(left, right, dims=((1,), (0,))):
    return lax.dot_general(left, right, (dims, ((), ())), preferred_element_type=F32)


def dot_full(left, right):
    return jnp.dot(left, right, precision=lax.Precision.HIGHEST, preferred_element_type=F32)


def cut(value):
    high = value.astype(BF16)
    return high, (value - high.astype(F32)).astype(BF16)


def mul(rows, high, low):
    rows_high, rows_low = cut(rows)
    return dot(rows_high, high) + (dot(rows_low, high) + dot(rows_high, low))


def put(first, place, value):
    high, low = cut(value)
    yield first, place, high
    yield first + 1, place, low


def small_powers(transition, info_gain, smoother_gain, smoother_input):
    a, g = transition[...].T, smoother_input[...].T
    b, k = smoother_gain[...].T, info_gain[...].T
    ag = dot_full(a, g)
    m = dot_full(ag, b)
    for level in range(8):
        yield from put(2, level, a)
        yield from put(4, level, b)
        yield from put(6, level, m)
        n = mul(a, *cut(m))
        m = m + mul(n, *cut(b))
        a, b = dot_full(a, a), dot_full(b, b)
        yield from put(8, level, n)
        if level == 0:
            kg = dot_full(k, g)
            for i, value in enumerate([k, kg, dot_full(kg, smoother_gain[...].T), ag, g]):
                yield from put(0, i, value)
    yield 10, None, a
    yield 11, None, b
    yield 12, None, m


def big_powers(a, b, m):
    yield from put(4, None, m[...])
    a, b = a[...], b[...]
    for level in range(5):
        if level:
            a, b = dot_full(a, a), dot_full(b, b)
        yield from put(0, level, a)
        yield from put(2, level, b)


def information_part(order, noise_precision, emission, observations):
    scale = jnp.broadcast_to(noise_precision[...], (128, noise_precision.shape[1])).T
    scale = jnp.concatenate([scale] * (emission.shape[1] // 128), axis=1)
    weighted = (emission[...].astype(F32) * scale).astype(BF16)
    rows = dot(order[...], observations[...]).astype(BF16)
    information = dot(rows, weighted)
    half = rows.shape[0] // 2
    first = lax.axis_index("core") == 0
    yield 1, None, jnp.where(first, information[half:], information[:half])
    yield 0, None, jnp.where(first, information[:half], information[half:])


def chosen(number, values):
    out = values[0]
    for i in range(1, len(values)):
        out = jnp.where(number == i, values[i], out)
    return out


def channel_slices(order, observations, emission):
    y = lax.axis_index("y")
    rows = dot(order[...], observations[...])
    width = rows.shape[1] // N_Y
    parts = [rows[:, i * width : (i + 1) * width] for i in range(N_Y)]
    for by in (1, 2, 3, 0):
        yield by, None, chosen(y, [parts[(i + by) % N_Y] for i in range(N_Y)])
    emission = emission[...].astype(F32)
    emission = chosen(y, [emission[i * width : (i + 1) * width] for i in range(N_Y)])
    yield 4, None, emission.astype(BF16)


def up_sweep(lead, a_cut, b_cut, m_cut, information):
    lead_high, lead_low = lead
    drive = mul(information, lead_high[0], lead_low[0])
    shown = mul(information, lead_high[1], lead_low[1])
    end = drive
    start = mul(information, lead_high[2], lead_low[2])
    ends, follows = [], []
    for level in range(5):
        half = end.shape[0] // 2
        first, second = end[:half], end[half:]
        follow = start[half:] + mul(first, m_cut[0][level], m_cut[1][level])
        ends.append(first)
        follows.append(follow)
        start = start[:half] + mul(follow, b_cut[0][level], b_cut[1][level])
        end = second + mul(first, a_cut[0][level], a_cut[1][level])
    return shown, end, start, ends, follows


def sub_sweep(a_cut, b_cut, m_cut, end, start):
    ends, follows = [], []
    for level in range(5, 8):
        by = 2 ** (level - 5)
        follow = roll(start, -by) + mul(end, m_cut[0][level], m_cut[1][level])
        ends.append(end)
        follows.append(follow)
        start = start + mul(follow, b_cut[0][level], b_cut[1][level])
        end = mul(end, a_cut[0][level], a_cut[1][level]) + roll(end, -by)
    return end, start, ends, follows


def block_ends(total, theirs, lead_h, lead_l, m_h, m_l, b_h, b_l, a_h, a_l):
    first = lax.axis_index("core") == 0
    total, theirs = total[...], theirs[...]
    information = jnp.concatenate(
        [jnp.where(first, total, theirs), jnp.where(first, theirs, total)], axis=0
    )
    yield 0, None, information
    a_cut, b_cut, m_cut = (a_h, a_l), (b_h, b_l), (m_h, m_l)
    _, end, start, _, _ = up_sweep((lead_h, lead_l), a_cut, b_cut, m_cut, information)
    end, start, _, _ = sub_sweep(a_cut, b_cut, m_cut, end, start)
    pair = jnp.concatenate([end[None, :1], start[None, :1]], axis=1)
    yield 1, None, jnp.broadcast_to(pair, (BLOCKS, 2, end.shape[1]))


def spread_first(rows, by):
    rows = jnp.where(row_index(rows) % (2 * by) == 0, rows, 0.0)
    step = 1
    while step < 2 * by:
        rows = rows + roll(rows, step)
        step *= 2
    return rows


def joined(pieces):
    width = pieces[0].shape[1]
    return jnp.concatenate(
        [piece[...].reshape(-1, 1, SUB, width) for piece in pieces], axis=1
    ).reshape(-1, width)


def block_trees(
    i0, i1, i2, i3, lead_h, lead_l, m_h, m_l, b_h, b_l, a_h, a_l, o0, o1, o2, o3
):
    a_cut, b_cut, m_cut = (a_h, a_l), (b_h, b_l), (m_h, m_l)
    information = joined([i0, i1, i2, i3])
    shown, end, start, ends, follows = up_sweep(
        (lead_h, lead_l), a_cut, b_cut, m_cut, information
    )
    yield 0, None, shown
    at = 0
    for i in range(5):
        yield 1, (at, ends[i].shape[0]), ends[i]
        yield 2, (at, ends[i].shape[0]), follows[i]
        at += ends[i].shape[0]
    _, _, sub_ends, sub_follows = sub_sweep(a_cut, b_cut, m_cut, end, start)
    count = end.shape[0]
    for i in range(3):
        yield 3, (i * count, count), spread_first(sub_ends[i], 2**i)
        yield 4, (i * count, count), spread_first(sub_follows[i], 2**i)
    yield 5, None, joined([o0, o1, o2, o3]).astype(BF16)


def states_and_sums(
    gathered,
    a_big_h,
    a_big_l,
    lead_h,
    lead_l,
    m_h,
    m_l,
    b_big_h,
    b_big_l,
    sub_ends,
    sub_follows,
    a_h,
    a_l,
    n_h,
    n_l,
    b_h,
    b_l,
    ends,
    follows,
    shown,
    emission,
    observed,
    natural,
):
    block = lax.axis_index("y") * N_Z + lax.axis_index("z")
    width = shown.shape[1]
    gathered = gathered[...]
    after = gathered[:, 0]
    index = row_index(after)
    for level in range(5):
        by = 2**level
        before = jnp.where(index >= by, roll(after, by), 0.0)
        after = after + mul(before, a_big_h[level], a_big_l[level])
    enter = jnp.where(index >= 1, roll(after, 1), 0.0)
    follow = gathered[:, 1] + mul(enter, m_h[...], m_l[...])
    final = after - mul(after, lead_h[4], lead_l[4])
    follow = jnp.where(index < BLOCKS - 1, roll(follow, -1), final)
    for level in range(5):
        by = 2**level
        later = jnp.where(index < BLOCKS - by, roll(follow, -by), 0.0)
        follow = follow + mul(later, b_big_h[level], b_big_l[level])

    place = lax.broadcasted_iota(jnp.int32, (N_Y * SUB, BLOCKS), 0)
    source = lax.broadcasted_iota(jnp.int32, (N_Y * SUB, BLOCKS), 1)
    wanted = block - N_Z * (place // SUB)
    pick = (source == jnp.where(wanted < 0, wanted + BLOCKS, wanted)).astype(BF16)

    def picked(rows):
        high, low = cut(rows)
        return dot(pick, high) + dot(pick, low)

    enter, follow = picked(enter), picked(follow)
    count = N_Y * SUB
    index = row_index(enter)
    for level in (7, 6, 5):
        by = 2 ** (level - 5)
        part = (level - 5) * count
        second = sub_ends[part : part + count] + mul(enter, a_h[level], a_l[level])
        first = (
            sub_follows[part : part + count]
            + mul(enter, n_h[level], n_l[level])
            + mul(follow, b_h[level], b_l[level])
        )
        is_second = (index // by) % 2 == 1
        enter = jnp.where(is_second, second, enter)
        follow = jnp.where(is_second, follow, first)

    bottom = ends.shape[0]
    for level in (4, 3, 2, 1, 0):
        rows = enter.shape[0]
        top, bottom = bottom, bottom - rows
        second = ends[bottom:top] + mul(enter, a_h[level], a_l[level])
        first = (
            follows[bottom:top]
            + mul(enter, n_h[level], n_l[level])
            + mul(follow, b_h[level], b_l[level])
        )
        enter = jnp.concatenate([enter, second], axis=0)
        follow = jnp.concatenate([first, follow], axis=0)
    smoothed = shown[...] + mul(enter, lead_h[3], lead_l[3]) + follow
    observed, emission, natural = observed[...], emission[...], natural[...]

    high, low = cut(smoothed)
    cross = dot(observed, high, ((0,), (0,)))
    predicted = dot(high, emission, ((1,), (1,)))
    error = observed.astype(F32) - predicted
    error = jnp.broadcast_to(jnp.sum(error * error, axis=0, keepdims=True), (8, error.shape[1]))
    crossed = dot(high, jnp.concatenate([high, low], axis=1), ((0,), (0,)))
    moment = crossed[:, :width] + (crossed[:, width:] + crossed[:, width:].T)

    channels = cross.shape[0]
    share, line = width // N_Y, channels // N_Z
    y = block // N_Z
    mine = chosen(y, [moment[i * share : (i + 1) * share] for i in range(N_Y)])
    free = share * jnp.where(y == N_Y - 1, 0, y + 1)
    lane = lax.broadcasted_iota(jnp.int32, (8, width), 1)
    row = lax.broadcasted_iota(jnp.int32, (8, width), 0)
    is_free = (lane >= free) & (lane < free + share)
    is_error = (lane >= free) & (lane < free + line) & (row == 0)
    chunks = []
    for z in range(N_Z):
        turned = roll_lanes(error, free + (width - line * z))
        tile = jnp.where(is_free, 0.0, mine[8 * z : 8 * z + 8])
        chunks.append(jnp.where(is_error, turned, tile))
    yield 1, None, jnp.concatenate([cross.reshape(N_Z, line, width), jnp.stack(chunks)], axis=1)

    own = smoothed.reshape(-1, N_Y, SUB, width)[:, 0].reshape(-1, width)
    high, rest = own.astype(BF16), own
    out = dot(natural, high)
    for _ in range(2):
        rest = rest - high.astype(F32)
        high = rest.astype(BF16)
        out = out + dot(natural, high)
    yield 0, None, out


def add_pieces(pieces):
    total = pieces[0]
    for i in range(1, N_Z):
        total = total + pieces[i]
    yield 0, None, jnp.broadcast_to(total[None], (N_Z,) + total.shape)


def assemble(bins, *sums):
    place = lax.axis_index("y")
    sums = [part[...] for part in sums]
    width = sums[0].shape[2]
    share = width // N_Y
    line = sums[0].shape[1] - 8
    lane = lax.broadcasted_iota(jnp.int32, (8, width), 1)
    cross, moment, errors = [], [], []
    for y in range(N_Y):
        whole = chosen(place, [sums[(i - y) % N_Y] for i in range(N_Y)])
        cross.append(whole[:, :line].reshape(-1, width) * (1.0 / math.sqrt(bins)))
        moment.append(whole[:, line:].reshape(-1, width))
        error = jnp.zeros((8, width), F32)
        for z in range(N_Z):
            turned = roll_lanes(whole[z, line:], (line * z - share * ((y + 1) % N_Y)) % width)
            error = jnp.where((lane >= line * z) & (lane < line * z + line), turned, error)
        errors.append(error[:1] * (1.0 / bins))
    moment = jnp.concatenate(moment, axis=0)
    row = lax.broadcasted_iota(jnp.int32, moment.shape, 0) // share
    column = lax.broadcasted_iota(jnp.int32, moment.shape, 1) // share
    free = column == jnp.where(row == N_Y - 1, 0, row + 1)
    moment = jnp.where(free, moment.T, moment) * (1.0 / bins)
    yield 0, None, jnp.concatenate(cross, axis=0)
    yield 1, None, moment
    yield 2, None, jnp.concatenate(errors, axis=1)


def shift(value, axis, count, by):
    return lax.ppermute(value, axis, [(i, (i + by) % count) for i in range(count)])


def bit_reversed(count):
    bits = count.bit_length() - 1
    return [int(format(i, "0%db" % bits)[::-1], 2) for i in range(count)]


def row_order(bins):
    length = bins // SUB
    times = np.array([[j * length + t for j in range(SUB)] for t in bit_reversed(length)])
    return np.eye(bins, dtype=np.float32)[times.reshape(-1)]


def local(
    observations, emission, noise_precision, transition, info_gain, smoother_gain, smoother_input
):
    bins, channels = observations.shape
    width = transition.shape[0]
    order = jnp.asarray(row_order(bins), BF16)
    natural = jnp.asarray(row_order(bins).T, BF16)

    mine, other = call(
        information_part,
        [((bins // 2, width), F32)] * 2,
        order,
        noise_precision.reshape(1, channels),
        emission,
        observations,
        large=(0, 1, 2, 3),
    )
    mine = mine + shift(other, "core", N_CORE, 1)
    mine, later = lax.optimization_barrier((mine, observations))
    moved = [shift(mine, "x", N_X, by) for by in (2, 1, 3)]

    part = channels // N_Y
    *slices, emission_part = call(
        channel_slices,
        [((bins, part), F32)] * N_Y + [((part, width), BF16)],
        order,
        later,
        emission,
    )
    observed = slices[:1] + [shift(slices[by], "y", N_Y, by) for by in (1, 2, 3)]

    square = (width, width)
    stack = lambda n: [((n,) + square, BF16)] * 2
    small = call(
        small_powers,
        stack(5) + stack(8) * 4 + [(square, F32)] * 3,
        transition,
        info_gain,
        smoother_gain,
        smoother_input,
    )
    lead, a_cut, b_cut, m_cut, n_cut = (small[i : i + 2] for i in range(0, 10, 2))

    total = mine + moved[0] + moved[1] + moved[2]
    theirs = shift(total, "core", N_CORE, 1)
    information, ends = call(
        block_ends,
        [((bins, width), F32), ((BLOCKS, 2, width), F32)],
        total,
        theirs,
        *lead,
        *m_cut,
        *b_cut,
        *a_cut,
    )
    ends, observed = lax.optimization_barrier((ends, observed))
    gathered = lax.all_to_all(ends, ("y", "z"), 0, 0)
    gathered, information = lax.optimization_barrier((gathered, information))
    informations = [information] + [shift(information, "y", N_Y, by) for by in (1, 2, 3)]
    big = call(big_powers, stack(5) * 2 + [(square, BF16)] * 2, *small[10:])
    tree_rows = N_Y * SUB * 31
    shown, tree_ends, follows, sub_ends, sub_follows, seen = call(
        block_trees,
        [
            ((N_Y * bins, width), F32),
            ((tree_rows, width), F32),
            ((tree_rows, width), F32),
            ((3 * N_Y * SUB, width), F32),
            ((3 * N_Y * SUB, width), F32),
            ((N_Y * bins, part), BF16),
        ],
        *informations,
        *lead,
        *m_cut,
        *b_cut,
        *a_cut,
        *observed,
    )
    rows = channels // (N_Y * N_Z) + 8
    smoothed, payload = call(
        states_and_sums,
        [((bins, width), F32), ((N_Z, rows, width), F32)],
        gathered,
        *big[:2],
        *lead,
        *big[4:],
        *big[2:4],
        sub_ends,
        sub_follows,
        *a_cut,
        *n_cut,
        *b_cut,
        tree_ends,
        follows,
        shown,
        emission_part,
        seen,
        natural,
    )
    payload = lax.all_to_all(payload, "z", 0, 0)
    (spread,) = call(add_pieces, [((N_Z, rows, width), F32)], payload)
    whole = lax.all_to_all(spread, "z", 0, 0)
    far, near, back = (shift(whole, "y", N_Y, by) for by in (2, 1, 3))
    cross, moment, error = call(
        functools.wraps(assemble)(functools.partial(assemble, bins * BLOCKS)),
        [((channels, width), F32), (square, F32), ((1, channels), F32)],
        whole,
        near,
        far,
        back,
        sent=(0, 1, 2),
    )
    return smoothed, cross, error.reshape(channels), moment


def solution(mesh):
    tm, chan = ("y", "z"), ("x", "core")
    split = Mesh(mesh.devices.reshape(N_Y, N_Z, N_X, N_CORE), tm + chan)
    placed = (P(tm, chan), P(chan, None), P(chan), P(), P(), P(), P())
    return jax.shard_map(
        local,
        mesh=split,
        in_specs=placed,
        out_specs=(P(tm, None), P(chan, None), P(chan), P()),
        check_vma=False,
    )
```

profile of v0, /device:TPU:24, one launch (start us, length us, event | category | flops | bytes accessed | tf_op | source)
XLA Modules:
  0.0 128.2 jit_solution(974339598655369093)
XLA Ops:
  0.7 2.5 %information_part.1 = (f32[128,256]{1,0:T(8,128)S(1)}, f32[128,256]{1,0:T(8,128)S(1)}) custom-call(bf16[256,256]{1,0:T(8,128)(2,1)} %constant.4.clone.refs_0_, f32[1,1024]{1,0:T(1,128)} %bitcast.2, bf16[1024,256]{1,0:T(8,128)(2,1)} %refs_2_.5, bf16[256,1024]{1,0:T(8,128)(2,1)} %refs_1_.2), custom_call_target="tpu_custom_call" | custom-call | tf_op jit(solution)/shard_map/information_part/pallas_call | solution.py:90
  3.2 0.1 collective-permute-start
  3.3 1.3 %collective-permute-done = f32[128,256]{1,0:T(8,128)S(1)} collective-permute-done((f32[128,256]{1,0:T(8,128)S(1)}, f32[128,256]{1,0:T(8,128)S(1)}, u32[]{:S(2)}, u32[]{:S(2)}) %collective-permute-start) | collective-permute-done | bytes 131104 | tf_op jit(solution)/shard_map/ppermute | solution.py:440
  4.7 2.8 %collective-permute-start.3 = (f32[128,256]{1,0:T(8,128)S(1)}, f32[128,256]{1,0:T(8,128)S(1)}, u32[]{:S(2)}, u32[]{:S(2)}) collective-permute-start(f32[128,256]{1,0:T(8,128)S(1)} %add.12), channel_id=1, source_target_pairs={{0,6},{2,0},{4,2},{6,4},{1,7},{3,1},{5,3},{7,5},{8,14},{10,8},{12,... | collective-permute-start | bytes 393224 | tf_op jit(solution)/shard_map/ppermute | solution.py:440
  7.5 2.3 %collective-permute-start.1 = (f32[128,256]{1,0:T(8,128)S(1)}, f32[128,256]{1,0:T(8,128)S(1)}, u32[]{:S(2)}, u32[]{:S(2)}) collective-permute-start(f32[128,256]{1,0:T(8,128)S(1)} %add.12), channel_id=1, source_target_pairs={{0,4},{2,6},{4,0},{6,2},{1,5},{3,7},{5,1},{7,3},{8,12},{10,14},{12... | collective-permute-start | bytes 393224 | tf_op jit(solution)/shard_map/ppermute | solution.py:440
  9.8 1.0 channel_slices.1
  10.8 0.3 collective-permute-start.5
  11.1 2.6 %collective-permute-start.6 = (f32[256,256]{1,0:T(8,128)S(1)}, f32[256,256]{1,0:T(8,128)S(1)}, u32[]{:S(2)}, u32[]{:S(2)}) collective-permute-start(f32[256,256]{1,0:T(8,128)S(1)} %get-tuple-element.67), channel_id=1, source_target_pairs={{0,128},{64,192},{128,0},{192,64},{1,129},{65,193},{129,1},{193,65... | collective-permute-start | bytes 786440 | tf_op jit(solution)/shard_map/ppermute | solution.py:440
  13.8 3.0 %collective-permute-done.2 = f32[128,256]{1,0:T(8,128)S(1)} collective-permute-done((f32[128,256]{1,0:T(8,128)S(1)}, f32[128,256]{1,0:T(8,128)S(1)}, u32[]{:S(2)}, u32[]{:S(2)}) %collective-permute-start.2) | collective-permute-done | bytes 131104 | tf_op jit(solution)/shard_map/ppermute | solution.py:440
  16.8 0.3 collective-permute-start.4
  17.2 8.5 %small_powers.1 = (bf16[5,256,256]{2,1,0:T(8,128)(2,1)S(1)}, bf16[5,256,256]{2,1,0:T(8,128)(2,1)S(1)}, bf16[8,256,256]{2,1,0:T(8,128)(2,1)S(1)}, bf16[8,256,256]...) custom-call(f32[256,256]{1,0:T(8,128)S(1)} %copy-done.3, ...), custom_call_target="tpu_custom_call" | custom-call | tf_op jit(solution)/shard_map/small_powers/pallas_call | solution.py:90
  25.6 3.5 %block_ends.1 = (f32[256,256]{1,0:T(8,128)S(1)}, f32[32,2,256]{2,1,0:T(2,128)S(1)}) custom-call(f32[128,256]{1,0:T(8,128)S(1)} %add_add_fusion.refs_0_, f32[128,256]{1,0:T(8,128)S(1)} %collective-permute-done.4.refs_1_, bf16[5,256,256]{2,1,0:T(8,128)(2,1)S(1)} %get-tuple-element.55.refs_2_.refs_4_.refs_3_, ...), custom_call_target="tpu_custom_call" | custom-call | tf_op jit(solution)/shard_map/block_ends/pallas_call | solution.py:90
  29.2 19.4 %all_to_all.15.refs_0_ = f32[32,2,256]{2,1,0:T(2,128)S(1)} all-to-all(f32[32,2,256]{2,1,0:T(2,128)S(1)} %get-tuple-element.69), channel_id=1, replica_groups=mesh['y'=4,'z'=8,'x'=4,'core'=2] {'y','z'}, dimensions={0} | all-to-all | bytes 131072 | tf_op jit(solution)/shard_map/all_to_all | solution.py:510
  48.6 0.7 collective-permute-start.10
  49.4 2.8 %collective-permute-start.9 = (f32[256,256]{1,0:T(8,128)S(1)}, f32[256,256]{1,0:T(8,128)S(1)}, u32[]{:S(2)}, u32[]{:S(2)}) collective-permute-start(f32[256,256]{1,0:T(8,128)S(1)} %get-tuple-element.81.refs_0_), channel_id=1, source_target_pairs={{0,128},{64,192},{128,0},{192,64},{1,129},{65,193},{129,1},{193,65... | collective-permute-start | bytes 786440 | tf_op jit(solution)/shard_map/ppermute | solution.py:440
  52.2 1.2 collective-permute-start.8
  53.4 3.1 %big_powers.1 = (bf16[5,256,256]{2,1,0:T(8,128)(2,1)S(1)}, bf16[5,256,256]{2,1,0:T(8,128)(2,1)S(1)}, bf16[5,256,256]{2,1,0:T(8,128)(2,1)S(1)}, bf16[5,256,256]{2...) custom-call(f32[256,256]{1,0:T(8,128)S(1)} %get-tuple-element.72.refs_0_, ...), custom_call_target="tpu_custom_call" | custom-call | tf_op jit(solution)/shard_map/big_powers/pallas_call | solution.py:90
  56.5 2.3 %collective-permute-done.10.refs_3_ = f32[256,256]{1,0:T(8,128)S(1)} collective-permute-done((f32[256,256]{1,0:T(8,128)S(1)}, f32[256,256]{1,0:T(8,128)S(1)}, u32[]{:S(2)}, u32[]{:S(2)}) %collective-permute-start.10) | collective-permute-done | bytes 262176 | tf_op jit(solution)/shard_map/ppermute | solution.py:440
  58.8 4.2 %collective-permute-done.9.refs_2_ = f32[256,256]{1,0:T(8,128)S(1)} collective-permute-done((f32[256,256]{1,0:T(8,128)S(1)}, f32[256,256]{1,0:T(8,128)S(1)}, u32[]{:S(2)}, u32[]{:S(2)}) %collective-permute-start.9) | collective-permute-done | bytes 262176 | tf_op jit(solution)/shard_map/ppermute | solution.py:440
  63.0 0.3 collective-permute-done.8.refs_1_
  63.4 7.0 %block_trees.1 = (f32[1024,256]{1,0:T(8,128)S(1)}, f32[992,256]{1,0:T(8,128)S(1)}, f32[992,256]{1,0:T(8,128)S(1)}, f32[96,256]{1,0:T(8,128)S(1)}, f32[96,256]{1,0:T(8,128)S(1)}, /*index=5*/bf16[1024,256]{1,0:T(8,128)(2,1)S(1)}) custom-call(f32[256,256]{1,0:T(8,128)S(1)} %get-tuple-element.81.refs_0_, f32[256,256]{1,0:T(8,128)S(1)} %collective-permute-done.8.refs_1_, ...), custom_call_target="tpu_custom_call" | custom-call | tf_op jit(solution)/shard_map/block_trees/pallas_call | solution.py:90
  70.3 7.1 %states_and_sums.1 = (f32[256,256]{1,0:T(8,128)S(1)}, f32[8,40,256]{2,1,0:T(8,128)S(1)}) custom-call(f32[32,2,256]{2,1,0:T(2,128)S(1)} %all_to_all.15.refs_0_, bf16[5,256,256]{2,1,0:T(8,128)(2,1)S(1)} %get-tuple-element.75.refs_1_, bf16[5,256,256]{2,1,0:T(8,128)(2,1)S(1)} %get-tuple-element.76.refs_2_, ...), custom_call_target="tpu_custom_call" | custom-call | tf_op jit(solution)/shard_map/states_and_sums/pallas_call | solution.py:90
  77.5 15.1 %all_to_all.16.refs_0_ = f32[8,40,256]{2,1,0:T(8,128)S(1)} all-to-all(f32[8,40,256]{2,1,0:T(8,128)S(1)} %get-tuple-element.96), channel_id=1, replica_groups=mesh['y'=4,'z'=8,'x'=4,'core'=2] {'z'}, dimensions={0} | all-to-all | bytes 655360 | tf_op jit(solution)/shard_map/all_to_all | solution.py:553
  92.5 0.6 add_pieces.1
  93.1 14.3 %all_to_all.17.refs_0_ = f32[8,40,256]{2,1,0:T(8,128)S(1)} all-to-all(f32[8,40,256]{2,1,0:T(8,128)S(1)} %add_pieces.1), channel_id=1, replica_groups=mesh['y'=4,'z'=8,'x'=4,'core'=2] {'z'}, dimensions={0} | all-to-all | bytes 655360 | tf_op jit(solution)/shard_map/all_to_all | solution.py:555
  107.4 3.7 %collective-permute-start.13 = (f32[8,40,256]{2,1,0:T(8,128)S(1)}, f32[8,40,256]{2,1,0:T(8,128)S(1)}, u32[]{:S(2)}, u32[]{:S(2)}) collective-permute-start(f32[8,40,256]{2,1,0:T(8,128)S(1)} %all_to_all.17.refs_0_), channel_id=1, source_target_pairs={{0,192},{64,0},{128,64},{192,128},{1,193},{65,1},{129,65},{193,129... | collective-permute-start | bytes 983048 | tf_op jit(solution)/shard_map/ppermute | solution.py:440
  111.1 2.6 %collective-permute-start.12 = (f32[8,40,256]{2,1,0:T(8,128)S(1)}, f32[8,40,256]{2,1,0:T(8,128)S(1)}, u32[]{:S(2)}, u32[]{:S(2)}) collective-permute-start(f32[8,40,256]{2,1,0:T(8,128)S(1)} %all_to_all.17.refs_0_), channel_id=1, source_target_pairs={{0,128},{64,192},{128,0},{192,64},{1,129},{65,193},{129,1},{193,65... | collective-permute-start | bytes 983048 | tf_op jit(solution)/shard_map/ppermute | solution.py:440
  113.7 0.1 collective-permute-start.11
  113.8 0.7 copy.13
  114.5 5.5 %collective-permute-done.13.refs_3_ = f32[8,40,256]{2,1,0:T(8,128)S(1)} collective-permute-done((f32[8,40,256]{2,1,0:T(8,128)S(1)}, f32[8,40,256]{2,1,0:T(8,128)S(1)}, u32[]{:S(2)}, u32[]{:S(2)}) %collective-permute-start.13) | collective-permute-done | bytes 327712 | tf_op jit(solution)/shard_map/ppermute | solution.py:440
  120.0 5.9 %collective-permute-done.12.refs_2_ = f32[8,40,256]{2,1,0:T(8,128)S(1)} collective-permute-done((f32[8,40,256]{2,1,0:T(8,128)S(1)}, f32[8,40,256]{2,1,0:T(8,128)S(1)}, u32[]{:S(2)}, u32[]{:S(2)}) %collective-permute-start.12) | collective-permute-done | bytes 327712 | tf_op jit(solution)/shard_map/ppermute | solution.py:440
  125.9 2.1 %assemble.1 = (f32[1024,256]{1,0:T(8,128)}, f32[256,256]{1,0:T(8,128)}, f32[1,1024]{1,0:T(1,128)}) custom-call(f32[8,40,256]{2,1,0:T(8,128)S(1)} %all_to_all.17.refs_0_, f32[8,40,256]{2,1,0:T(8,128)S(1)} %collective-permute-done.11.refs_1_, f32[8,40,256]{2,1,0:T(8,128)S(1)} %collective-permute-done.12.refs_2_, f32[8,40,256]{2,1,0:T(8,128)S(1)} %collective-permute-done.13.refs_3_), custom_call_target="tpu_custom_call" | custom-call | tf_op jit(solution)/shard_map/assemble/pallas_call | solution.py:90
  (27 shorter events, 0.1 us)
Async XLA Ops:
  0.6 9.2 %copy-start = (bf16[1024,256]{1,0:T(8,128)(2,1)S(1)}, bf16[1024,256]{1,0:T(8,128)(2,1)}, u32[]{:S(2)}) copy-start(bf16[1024,256]{1,0:T(8,128)(2,1)} %refs_2_.5) | copy-start | bytes 1572868
  0.6 9.2 %copy-start.1 = (bf16[256,1024]{1,0:T(8,128)(2,1)S(1)}, bf16[256,1024]{1,0:T(8,128)(2,1)}, u32[]{:S(2)}) copy-start(bf16[256,1024]{1,0:T(8,128)(2,1)} %refs_1_.2) | copy-start | bytes 1572868
  3.2 1.4 %collective-permute-start = (f32[128,256]{1,0:T(8,128)S(1)}, f32[128,256]{1,0:T(8,128)S(1)}, u32[]{:S(2)}, u32[]{:S(2)}) collective-permute-start(f32[128,256]{1,0:T(8,128)S(1)} %get-tuple-element.53), channel_id=1, source_target_pairs={{0,1},{1,0},{2,3},{3,2},{4,5},{5,4},{6,7},{7,6},{8,9},{9,8},{10,11... | collective-permute-start | bytes 393224 | tf_op jit(solution)/shard_map/ppermute | solution.py:440
  4.6 5.2 %copy-start.2 = (bf16[256,256]{1,0:T(8,128)(2,1)S(1)}, bf16[256,256]{1,0:T(8,128)(2,1)}, u32[]{:S(2)}) copy-start(bf16[256,256]{1,0:T(8,128)(2,1)} %constant.4.clone.refs_0_) | copy-start | bytes 393220
  4.7 9.1 %collective-permute-start.3 = (f32[128,256]{1,0:T(8,128)S(1)}, f32[128,256]{1,0:T(8,128)S(1)}, u32[]{:S(2)}, u32[]{:S(2)}) collective-permute-start(f32[128,256]{1,0:T(8,128)S(1)} %add.12), channel_id=1, source_target_pairs={{0,6},{2,0},{4,2},{6,4},{1,7},{3,1},{5,3},{7,5},{8,14},{10,8},{12,... | collective-permute-start | bytes 393224 | tf_op jit(solution)/shard_map/ppermute | solution.py:440
  7.5 9.3 %collective-permute-start.2 = (f32[128,256]{1,0:T(8,128)S(1)}, f32[128,256]{1,0:T(8,128)S(1)}, u32[]{:S(2)}, u32[]{:S(2)}) collective-permute-start(f32[128,256]{1,0:T(8,128)S(1)} %add.12), channel_id=1, source_target_pairs={{0,2},{2,4},{4,6},{6,0},{1,3},{3,5},{5,7},{7,1},{8,10},{10,12},{12... | collective-permute-start | bytes 393224 | tf_op jit(solution)/shard_map/ppermute | solution.py:440
  7.5 9.3 %collective-permute-start.1 = (f32[128,256]{1,0:T(8,128)S(1)}, f32[128,256]{1,0:T(8,128)S(1)}, u32[]{:S(2)}, u32[]{:S(2)}) collective-permute-start(f32[128,256]{1,0:T(8,128)S(1)} %add.12), channel_id=1, source_target_pairs={{0,4},{2,6},{4,0},{6,2},{1,5},{3,7},{5,1},{7,3},{8,12},{10,14},{12... | collective-permute-start | bytes 393224 | tf_op jit(solution)/shard_map/ppermute | solution.py:440
  9.8 7.3 %copy-start.5 = (f32[256,256]{1,0:T(8,128)S(1)}, f32[256,256]{1,0:T(8,128)}, u32[]{:S(2)}) copy-start(f32[256,256]{1,0:T(8,128)} %refs_2_.4) | copy-start | bytes 786436
  9.8 7.3 %copy-start.6 = (f32[256,256]{1,0:T(8,128)S(1)}, f32[256,256]{1,0:T(8,128)}, u32[]{:S(2)}) copy-start(f32[256,256]{1,0:T(8,128)} %refs_3_.3) | copy-start | bytes 786436
  10.8 18.3 %collective-permute-start.5 = (f32[256,256]{1,0:T(8,128)S(1)}, f32[256,256]{1,0:T(8,128)S(1)}, u32[]{:S(2)}, u32[]{:S(2)}) collective-permute-start(f32[256,256]{1,0:T(8,128)S(1)} %get-tuple-element.66), channel_id=1, source_target_pairs={{0,64},{64,128},{128,192},{192,0},{1,65},{65,129},{129,193},{193,1... | collective-permute-start | bytes 786440 | tf_op jit(solution)/shard_map/ppermute | solution.py:440
  11.1 18.0 %collective-permute-start.6 = (f32[256,256]{1,0:T(8,128)S(1)}, f32[256,256]{1,0:T(8,128)S(1)}, u32[]{:S(2)}, u32[]{:S(2)}) collective-permute-start(f32[256,256]{1,0:T(8,128)S(1)} %get-tuple-element.67), channel_id=1, source_target_pairs={{0,128},{64,192},{128,0},{192,64},{1,129},{65,193},{129,1},{193,65... | collective-permute-start | bytes 786440 | tf_op jit(solution)/shard_map/ppermute | solution.py:440
  13.7 3.4 %copy-start.3 = (f32[256,256]{1,0:T(8,128)S(1)}, f32[256,256]{1,0:T(8,128)}, u32[]{:S(2)}) copy-start(f32[256,256]{1,0:T(8,128)} %refs_0_.3) | copy-start | bytes 786436
  13.7 3.4 %copy-start.4 = (f32[256,256]{1,0:T(8,128)S(1)}, f32[256,256]{1,0:T(8,128)}, u32[]{:S(2)}) copy-start(f32[256,256]{1,0:T(8,128)} %refs_1_.1) | copy-start | bytes 786436
  13.7 15.4 %collective-permute-start.7 = (f32[256,256]{1,0:T(8,128)S(1)}, f32[256,256]{1,0:T(8,128)S(1)}, u32[]{:S(2)}, u32[]{:S(2)}) collective-permute-start(f32[256,256]{1,0:T(8,128)S(1)} %get-tuple-element.68), channel_id=1, source_target_pairs={{0,192},{64,0},{128,64},{192,128},{1,193},{65,1},{129,65},{193,129... | collective-permute-start | bytes 786440 | tf_op jit(solution)/shard_map/ppermute | solution.py:440
  16.8 8.8 %collective-permute-start.4 = (f32[128,256]{1,0:T(8,128)S(1)}, f32[128,256]{1,0:T(8,128)S(1)}, u32[]{:S(2)}, u32[]{:S(2)}) collective-permute-start(f32[128,256]{1,0:T(8,128)S(1)} %add_add_fusion.refs_0_), channel_id=1, source_target_pairs={{0,1},{1,0},{2,3},{3,2},{4,5},{5,4},{6,7},{7,6},{8,9},{9,8},{10,11... | collective-permute-start | bytes 393224 | tf_op jit(solution)/shard_map/ppermute | solution.py:440
  48.6 10.2 %collective-permute-start.10 = (f32[256,256]{1,0:T(8,128)S(1)}, f32[256,256]{1,0:T(8,128)S(1)}, u32[]{:S(2)}, u32[]{:S(2)}) collective-permute-start(f32[256,256]{1,0:T(8,128)S(1)} %get-tuple-element.81.refs_0_), channel_id=1, source_target_pairs={{0,192},{64,0},{128,64},{192,128},{1,193},{65,1},{129,65},{193,129... | collective-permute-start | bytes 786440 | tf_op jit(solution)/shard_map/ppermute | solution.py:440
  49.4 13.7 %collective-permute-start.9 = (f32[256,256]{1,0:T(8,128)S(1)}, f32[256,256]{1,0:T(8,128)S(1)}, u32[]{:S(2)}, u32[]{:S(2)}) collective-permute-start(f32[256,256]{1,0:T(8,128)S(1)} %get-tuple-element.81.refs_0_), channel_id=1, source_target_pairs={{0,128},{64,192},{128,0},{192,64},{1,129},{65,193},{129,1},{193,65... | collective-permute-start | bytes 786440 | tf_op jit(solution)/shard_map/ppermute | solution.py:440
  52.2 11.2 %collective-permute-start.8 = (f32[256,256]{1,0:T(8,128)S(1)}, f32[256,256]{1,0:T(8,128)S(1)}, u32[]{:S(2)}, u32[]{:S(2)}) collective-permute-start(f32[256,256]{1,0:T(8,128)S(1)} %get-tuple-element.81.refs_0_), channel_id=1, source_target_pairs={{0,64},{64,128},{128,192},{192,0},{1,65},{65,129},{129,193},{193,1... | collective-permute-start | bytes 786440 | tf_op jit(solution)/shard_map/ppermute | solution.py:440
  56.5 13.9 %copy-start.7 = (bf16[256,256]{1,0:T(8,128)(2,1)S(1)}, bf16[256,256]{1,0:T(8,128)(2,1)}, u32[]{:S(2)}) copy-start(bf16[256,256]{1,0:T(8,128)(2,1)} %constant.5.clone.refs_22_) | copy-start | bytes 393220
  107.4 12.6 %collective-permute-start.13 = (f32[8,40,256]{2,1,0:T(8,128)S(1)}, f32[8,40,256]{2,1,0:T(8,128)S(1)}, u32[]{:S(2)}, u32[]{:S(2)}) collective-permute-start(f32[8,40,256]{2,1,0:T(8,128)S(1)} %all_to_all.17.refs_0_), channel_id=1, source_target_pairs={{0,192},{64,0},{128,64},{192,128},{1,193},{65,1},{129,65},{193,129... | collective-permute-start | bytes 983048 | tf_op jit(solution)/shard_map/ppermute | solution.py:440
  111.1 14.8 %collective-permute-start.12 = (f32[8,40,256]{2,1,0:T(8,128)S(1)}, f32[8,40,256]{2,1,0:T(8,128)S(1)}, u32[]{:S(2)}, u32[]{:S(2)}) collective-permute-start(f32[8,40,256]{2,1,0:T(8,128)S(1)} %all_to_all.17.refs_0_), channel_id=1, source_target_pairs={{0,128},{64,192},{128,0},{192,64},{1,129},{65,193},{129,1},{193,65... | collective-permute-start | bytes 983048 | tf_op jit(solution)/shard_map/ppermute | solution.py:440
  113.7 12.1 %collective-permute-start.11 = (f32[8,40,256]{2,1,0:T(8,128)S(1)}, f32[8,40,256]{2,1,0:T(8,128)S(1)}, u32[]{:S(2)}, u32[]{:S(2)}) collective-permute-start(f32[8,40,256]{2,1,0:T(8,128)S(1)} %all_to_all.17.refs_0_), channel_id=1, source_target_pairs={{0,64},{64,128},{128,192},{192,0},{1,65},{65,129},{129,193},{193,1... | collective-permute-start | bytes 983048 | tf_op jit(solution)/shard_map/ppermute | solution.py:440
where the time goes:
time: 131 us; the launch traced here: 128 us
  blocking collectives  48.8 us (37%)
  Pallas kernels  35.4 us (27%)
  waiting for transfers between devices  22.6 us (17%)
  starting transfers between devices  19.5 us (15%)
    pallas_call x9, Pallas kernels, call(): pl.pallas_call(kernel, out_shape=[(pltpu.HBM if i in sent else pltpu.VMEM...  35.4 us
    ppermute x14, waiting for transfers between devices, shift(): lax.ppermute(value, axis, [(i, (i + by) % count) for i in range(count)])  22.6 us
    ppermute x14, starting transfers between devices, shift(): lax.ppermute(value, axis, [(i, (i + by) % count) for i in range(count)])  19.5 us
    all_to_all x1, blocking collectives, local(): gathered = lax.all_to_all(ends, ('y', 'z'), 0, 0)  19.4 us
    all_to_all x1, blocking collectives, local(): payload = lax.all_to_all(payload, 'z', 0, 0)  15.1 us
    all_to_all x1, blocking collectives, local(): whole = lax.all_to_all(spread, 'z', 0, 0)  14.3 us
  transfers between devices with their start and end apart: 14, of which 7 were waited for; matrix products, arithmetic and copies ran while one was open for 1% of the time, Pallas kernels for 13%

commit v1 on v0

--- a/solution.py
+++ b/solution.py
@@ -120,56 +120,84 @@
     return lax.dot_general(left, right, (dims, ((), ())), preferred_element_type=F32)
 
 
+def cut(value):
+    count = value.shape[0]
+    if count < 16:
+        value = jnp.concatenate([value, value], axis=0)
+    high = value.astype(BF16)
+    return high, (value - high.astype(F32)).astype(BF16), count
+
+
+def cut_full(value):
+    high = value.astype(BF16)
+    rest = value - high.astype(F32)
+    middle = rest.astype(BF16)
+    return high, middle, (rest - middle.astype(F32)).astype(BF16)
+
+
+def dot_pairs(pairs):
+    left = jnp.concatenate([pair[0] for pair in pairs], axis=1)
+    right = jnp.concatenate([pair[1] for pair in pairs], axis=0)
+    return dot(left, right)
+
+
 def dot_full(left, right):
-    return jnp.dot(left, right, precision=lax.Precision.HIGHEST, preferred_element_type=F32)
-
-
-def cut(value):
-    high = value.astype(BF16)
-    return high, (value - high.astype(F32)).astype(BF16)
-
-
-def mul(rows, high, low):
-    rows_high, rows_low = cut(rows)
-    return dot(rows_high, high) + (dot(rows_low, high) + dot(rows_high, low))
+    a, b = left, right
+    return dot_pairs(
+        [(a[0], b[0]), (a[0], b[1]), (a[1], b[0]), (a[1], b[1]), (a[0], b[2]), (a[2], b[0])]
+    )
+
+
+def mul(rows, matrix):
+    return dot_pairs(pairs_of(rows, matrix))[: rows[2]]
+
+
+def pairs_of(rows, matrix):
+    return [(rows[0], matrix[0]), (rows[1], matrix[0]), (rows[0], matrix[1])]
+
+
+def at(matrices, level):
+    return matrices[0][level], matrices[1][level]
 
 
 def put(first, place, value):
-    high, low = cut(value)
-    yield first, place, high
-    yield first + 1, place, low
+    yield first, place, value[0]
+    yield first + 1, place, value[1]
 
 
 def small_powers(transition, info_gain, smoother_gain, smoother_input):
-    a, g = transition[...].T, smoother_input[...].T
-    b, k = smoother_gain[...].T, info_gain[...].T
+    a, g = cut_full(transition[...].T), cut_full(smoother_input[...].T)
+    b, k = cut_full(smoother_gain[...].T), cut_full(info_gain[...].T)
     ag = dot_full(a, g)
-    m = dot_full(ag, b)
+    kg = dot_full(k, g)
+    m = dot_full(cut_full(ag), b)
+    for i, value in enumerate([k, cut(kg), cut(dot_full(cut_full(kg), b)), cut(ag), g]):
+        yield from put(0, i, value)
     for level in range(8):
+        m_cut = cut(m)
         yield from put(2, level, a)
         yield from put(4, level, b)
-        yield from put(6, level, m)
-        n = mul(a, *cut(m))
-        m = m + mul(n, *cut(b))
+        yield from put(6, level, m_cut)
+        n_cut = cut(mul((a[0], a[1], a[0].shape[0]), m_cut))
+        m = m + mul(n_cut, b)
         a, b = dot_full(a, a), dot_full(b, b)
-        yield from put(8, level, n)
-        if level == 0:
-            kg = dot_full(k, g)
-            for i, value in enumerate([k, kg, dot_full(kg, smoother_gain[...].T), ag, g]):
-                yield from put(0, i, value)
+        if level < 7:
+            a, b = cut_full(a), cut_full(b)
+        yield from put(8, level, n_cut)
     yield 10, None, a
     yield 11, None, b
     yield 12, None, m
 
 
 def big_powers(a, b, m):
-    yield from put(4, None, m[...])
+    yield from put(4, None, cut(m[...]))
     a, b = a[...], b[...]
     for level in range(5):
-        if level:
-            a, b = dot_full(a, a), dot_full(b, b)
+        a, b = cut_full(a), cut_full(b)
         yield from put(0, level, a)
         yield from put(2, level, b)
+        if level < 4:
+            a, b = dot_full(a, a), dot_full(b, b)
 
 
 def information_part(order, noise_precision, emission, observations):
@@ -182,6 +210,7 @@
     first = lax.axis_index("core") == 0
     yield 1, None, jnp.where(first, information[half:], information[:half])
     yield 0, None, jnp.where(first, information[:half], information[half:])
+    yield 2, None, rows
 
 
 def chosen(number, values):
@@ -191,33 +220,19 @@
     return out
 
 
-def channel_slices(order, observations, emission):
-    y = lax.axis_index("y")
-    rows = dot(order[...], observations[...])
-    width = rows.shape[1] // N_Y
-    parts = [rows[:, i * width : (i + 1) * width] for i in range(N_Y)]
-    for by in (1, 2, 3, 0):
-        yield by, None, chosen(y, [parts[(i + by) % N_Y] for i in range(N_Y)])
-    emission = emission[...].astype(F32)
-    emission = chosen(y, [emission[i * width : (i + 1) * width] for i in range(N_Y)])
-    yield 4, None, emission.astype(BF16)
-
-
 def up_sweep(lead, a_cut, b_cut, m_cut, information):
-    lead_high, lead_low = lead
-    drive = mul(information, lead_high[0], lead_low[0])
-    shown = mul(information, lead_high[1], lead_low[1])
-    end = drive
-    start = mul(information, lead_high[2], lead_low[2])
+    information = cut(information)
+    end, shown, start = (mul(information, at(lead, i)) for i in range(3))
     ends, follows = [], []
     for level in range(5):
         half = end.shape[0] // 2
         first, second = end[:half], end[half:]
-        follow = start[half:] + mul(first, m_cut[0][level], m_cut[1][level])
+        first_cut = cut(first)
+        follow = start[half:] + mul(first_cut, at(m_cut, level))
         ends.append(first)
         follows.append(follow)
-        start = start[:half] + mul(follow, b_cut[0][level], b_cut[1][level])
-        end = second + mul(first, a_cut[0][level], a_cut[1][level])
+        start = start[:half] + mul(cut(follow), at(b_cut, level))
+        end = second + mul(first_cut, at(a_cut, level))
     return shown, end, start, ends, follows
 
 
@@ -225,26 +240,41 @@
     ends, follows = [], []
     for level in range(5, 8):
         by = 2 ** (level - 5)
-        follow = roll(start, -by) + mul(end, m_cut[0][level], m_cut[1][level])
+        end_cut = cut(end)
+        follow = roll(start, -by) + mul(end_cut, at(m_cut, level))
         ends.append(end)
         follows.append(follow)
-        start = start + mul(follow, b_cut[0][level], b_cut[1][level])
-        end = mul(end, a_cut[0][level], a_cut[1][level]) + roll(end, -by)
+        start = start + mul(cut(follow), at(b_cut, level))
+        end = mul(end_cut, at(a_cut, level)) + roll(end, -by)
     return end, start, ends, follows
 
 
-def block_ends(total, theirs, lead_h, lead_l, m_h, m_l, b_h, b_l, a_h, a_l):
+def both_halves(total, theirs):
     first = lax.axis_index("core") == 0
     total, theirs = total[...], theirs[...]
-    information = jnp.concatenate(
+    return jnp.concatenate(
         [jnp.where(first, total, theirs), jnp.where(first, theirs, total)], axis=0
     )
-    yield 0, None, information
+
+
+def block_tree(total, theirs, lead_h, lead_l, m_h, m_l, b_h, b_l, a_h, a_l):
+    information = both_halves(total, theirs)
     a_cut, b_cut, m_cut = (a_h, a_l), (b_h, b_l), (m_h, m_l)
-    _, end, start, _, _ = up_sweep((lead_h, lead_l), a_cut, b_cut, m_cut, information)
-    end, start, _, _ = sub_sweep(a_cut, b_cut, m_cut, end, start)
+    shown, end, start, ends, follows = up_sweep(
+        (lead_h, lead_l), a_cut, b_cut, m_cut, information
+    )
+    end, start, sub_ends, sub_follows = sub_sweep(a_cut, b_cut, m_cut, end, start)
     pair = jnp.concatenate([end[None, :1], start[None, :1]], axis=1)
-    yield 1, None, jnp.broadcast_to(pair, (BLOCKS, 2, end.shape[1]))
+    yield 0, None, jnp.broadcast_to(pair, (BLOCKS, 2, end.shape[1]))
+    yield 1, None, shown
+    place = 0
+    for i in range(5):
+        yield 2, (place, ends[i].shape[0]), ends[i]
+        yield 3, (place, ends[i].shape[0]), follows[i]
+        place += ends[i].shape[0]
+    for i in range(3):
+        yield 4, (i * SUB, SUB), spread_first(sub_ends[i], 2**i)
+        yield 5, (i * SUB, SUB), spread_first(sub_follows[i], 2**i)
 
 
 def spread_first(rows, by):
@@ -254,35 +284,6 @@
         rows = rows + roll(rows, step)
         step *= 2
     return rows
-
-
-def joined(pieces):
-    width = pieces[0].shape[1]
-    return jnp.concatenate(
-        [piece[...].reshape(-1, 1, SUB, width) for piece in pieces], axis=1
-    ).reshape(-1, width)
-
-
-def block_trees(
-    i0, i1, i2, i3, lead_h, lead_l, m_h, m_l, b_h, b_l, a_h, a_l, o0, o1, o2, o3
-):
-    a_cut, b_cut, m_cut = (a_h, a_l), (b_h, b_l), (m_h, m_l)
-    information = joined([i0, i1, i2, i3])
-    shown, end, start, ends, follows = up_sweep(
-        (lead_h, lead_l), a_cut, b_cut, m_cut, information
-    )
-    yield 0, None, shown
-    at = 0
-    for i in range(5):
-        yield 1, (at, ends[i].shape[0]), ends[i]
-        yield 2, (at, ends[i].shape[0]), follows[i]
-        at += ends[i].shape[0]
-    _, _, sub_ends, sub_follows = sub_sweep(a_cut, b_cut, m_cut, end, start)
-    count = end.shape[0]
-    for i in range(3):
-        yield 3, (i * count, count), spread_first(sub_ends[i], 2**i)
-        yield 4, (i * count, count), spread_first(sub_follows[i], 2**i)
-    yield 5, None, joined([o0, o1, o2, o3]).astype(BF16)
 
 
 def states_and_sums(
@@ -308,7 +309,6 @@
     shown,
     emission,
     observed,
-    natural,
 ):
     block = lax.axis_index("y") * N_Z + lax.axis_index("z")
     width = shown.shape[1]
@@ -318,37 +318,39 @@
     for level in range(5):
         by = 2**level
         before = jnp.where(index >= by, roll(after, by), 0.0)
-        after = after + mul(before, a_big_h[level], a_big_l[level])
+        after = after + mul(cut(before), at((a_big_h, a_big_l), level))
     enter = jnp.where(index >= 1, roll(after, 1), 0.0)
-    follow = gathered[:, 1] + mul(enter, m_h[...], m_l[...])
-    final = after - mul(after, lead_h[4], lead_l[4])
+    follow = gathered[:, 1] + mul(cut(enter), (m_h[...], m_l[...]))
+    final = after - mul(cut(after), at((lead_h, lead_l), 4))
     follow = jnp.where(index < BLOCKS - 1, roll(follow, -1), final)
     for level in range(5):
         by = 2**level
         later = jnp.where(index < BLOCKS - by, roll(follow, -by), 0.0)
-        follow = follow + mul(later, b_big_h[level], b_big_l[level])
-
-    place = lax.broadcasted_iota(jnp.int32, (N_Y * SUB, BLOCKS), 0)
-    source = lax.broadcasted_iota(jnp.int32, (N_Y * SUB, BLOCKS), 1)
-    wanted = block - N_Z * (place // SUB)
-    pick = (source == jnp.where(wanted < 0, wanted + BLOCKS, wanted)).astype(BF16)
+        follow = follow + mul(cut(later), at((b_big_h, b_big_l), level))
+
+    source = lax.broadcasted_iota(jnp.int32, (16, BLOCKS), 1)
+    pick = (source == block).astype(BF16)
 
     def picked(rows):
-        high, low = cut(rows)
-        return dot(pick, high) + dot(pick, low)
+        high, low, _ = cut(rows)
+        return (dot(pick, high) + dot(pick, low))[:SUB]
+
+    def children(enter, follow, level):
+        enter = cut(enter)
+        first = pairs_of(enter, at((n_h, n_l), level)) + pairs_of(
+            cut(follow), at((b_h, b_l), level)
+        )
+        return mul(enter, at((a_h, a_l), level)), dot_pairs(first)[: enter[2]]
 
     enter, follow = picked(enter), picked(follow)
-    count = N_Y * SUB
+    count = SUB
     index = row_index(enter)
     for level in (7, 6, 5):
         by = 2 ** (level - 5)
         part = (level - 5) * count
-        second = sub_ends[part : part + count] + mul(enter, a_h[level], a_l[level])
-        first = (
-            sub_follows[part : part + count]
-            + mul(enter, n_h[level], n_l[level])
-            + mul(follow, b_h[level], b_l[level])
-        )
+        second, first = children(enter, follow, level)
+        second = sub_ends[part : part + count] + second
+        first = sub_follows[part : part + count] + first
         is_second = (index // by) % 2 == 1
         enter = jnp.where(is_second, second, enter)
         follow = jnp.where(is_second, follow, first)
@@ -357,18 +359,15 @@
     for level in (4, 3, 2, 1, 0):
         rows = enter.shape[0]
         top, bottom = bottom, bottom - rows
-        second = ends[bottom:top] + mul(enter, a_h[level], a_l[level])
-        first = (
-            follows[bottom:top]
-            + mul(enter, n_h[level], n_l[level])
-            + mul(follow, b_h[level], b_l[level])
-        )
+        second, first = children(enter, follow, level)
+        second = ends[bottom:top] + second
+        first = follows[bottom:top] + first
         enter = jnp.concatenate([enter, second], axis=0)
         follow = jnp.concatenate([first, follow], axis=0)
-    smoothed = shown[...] + mul(enter, lead_h[3], lead_l[3]) + follow
-    observed, emission, natural = observed[...], emission[...], natural[...]
-
-    high, low = cut(smoothed)
+    smoothed = shown[...] + mul(cut(enter), at((lead_h, lead_l), 3)) + follow
+    observed, emission = observed[...], emission[...]
+
+    high, low, _ = cut(smoothed)
     cross = dot(observed, high, ((0,), (0,)))
     predicted = dot(high, emission, ((1,), (1,)))
     error = observed.astype(F32) - predicted
@@ -376,30 +375,44 @@
     crossed = dot(high, jnp.concatenate([high, low], axis=1), ((0,), (0,)))
     moment = crossed[:, :width] + (crossed[:, width:] + crossed[:, width:].T)
 
-    channels = cross.shape[0]
+    channels = cross.shape[0] // N_Y
     share, line = width // N_Y, channels // N_Z
-    y = block // N_Z
-    mine = chosen(y, [moment[i * share : (i + 1) * share] for i in range(N_Y)])
-    free = share * jnp.where(y == N_Y - 1, 0, y + 1)
     lane = lax.broadcasted_iota(jnp.int32, (8, width), 1)
     row = lax.broadcasted_iota(jnp.int32, (8, width), 0)
-    is_free = (lane >= free) & (lane < free + share)
-    is_error = (lane >= free) & (lane < free + line) & (row == 0)
-    chunks = []
-    for z in range(N_Z):
-        turned = roll_lanes(error, free + (width - line * z))
-        tile = jnp.where(is_free, 0.0, mine[8 * z : 8 * z + 8])
-        chunks.append(jnp.where(is_error, turned, tile))
-    yield 1, None, jnp.concatenate([cross.reshape(N_Z, line, width), jnp.stack(chunks)], axis=1)
-
-    own = smoothed.reshape(-1, N_Y, SUB, width)[:, 0].reshape(-1, width)
-    high, rest = own.astype(BF16), own
-    out = dot(natural, high)
-    for _ in range(2):
+    parts = []
+    for y in range(N_Y):
+        free = share * ((y + 1) % N_Y)
+        is_free = (lane >= free) & (lane < free + share)
+        is_error = (lane >= free) & (lane < free + line) & (row == 0)
+        tiles = []
+        for z in range(N_Z):
+            turned = roll_lanes(
+                error[:, y * channels : (y + 1) * channels], (free - line * z) % width
+            )
+            top = y * share + 8 * z
+            tile = jnp.where(is_free, 0.0, moment[top : top + 8])
+            tiles.append(jnp.where(is_error, turned, tile))
+        mine = cross[y * channels : (y + 1) * channels].reshape(N_Z, line, width)
+        parts.append(jnp.concatenate([mine, jnp.stack(tiles)], axis=1))
+    y = block // N_Z
+    for by in (2, 1, 3, 0):
+        yield 1 + by, None, chosen(y, [parts[(i + by) % N_Y] for i in range(N_Y)])
+
+    yield 0, None, smoothed
+
+
+def in_time_order(natural, smoothed):
+    rest, out = smoothed[...], None
+    for _ in range(3):
+        high = rest.astype(BF16)
         rest = rest - high.astype(F32)
-        high = rest.astype(BF16)
-        out = out + dot(natural, high)
+        moved = dot(natural[...], high)
+        out = moved if out is None else out + moved
     yield 0, None, out
+
+
+def add_chunks(c0, c1, c2, c3):
+    yield 0, None, (c0[...] + c1[...]) + (c2[...] + c3[...])
 
 
 def add_pieces(pieces):
@@ -459,9 +472,9 @@
     order = jnp.asarray(row_order(bins), BF16)
     natural = jnp.asarray(row_order(bins).T, BF16)
 
-    mine, other = call(
+    mine, other, seen = call(
         information_part,
-        [((bins // 2, width), F32)] * 2,
+        [((bins // 2, width), F32)] * 2 + [((bins, channels), BF16)],
         order,
         noise_precision.reshape(1, channels),
         emission,
@@ -469,18 +482,7 @@
         large=(0, 1, 2, 3),
     )
     mine = mine + shift(other, "core", N_CORE, 1)
-    mine, later = lax.optimization_barrier((mine, observations))
     moved = [shift(mine, "x", N_X, by) for by in (2, 1, 3)]
-
-    part = channels // N_Y
-    *slices, emission_part = call(
-        channel_slices,
-        [((bins, part), F32)] * N_Y + [((part, width), BF16)],
-        order,
-        later,
-        emission,
-    )
-    observed = slices[:1] + [shift(slices[by], "y", N_Y, by) for by in (1, 2, 3)]
 
     square = (width, width)
     stack = lambda n: [((n,) + square, BF16)] * 2
@@ -492,13 +494,22 @@
         smoother_gain,
         smoother_input,
     )
+    moved, small = lax.optimization_barrier((moved, small))
     lead, a_cut, b_cut, m_cut, n_cut = (small[i : i + 2] for i in range(0, 10, 2))
+    big = call(big_powers, stack(5) * 2 + [(square, BF16)] * 2, *small[10:])
 
     total = mine + moved[0] + moved[1] + moved[2]
     theirs = shift(total, "core", N_CORE, 1)
-    information, ends = call(
-        block_ends,
-        [((bins, width), F32), ((BLOCKS, 2, width), F32)],
+    ends, *tree = call(
+        block_tree,
+        [
+            ((BLOCKS, 2, width), F32),
+            ((bins, width), F32),
+            ((SUB * 31, width), F32),
+            ((SUB * 31, width), F32),
+            ((SUB * 3, width), F32),
+            ((SUB * 3, width), F32),
+        ],
         total,
         theirs,
         *lead,
@@ -506,33 +517,14 @@
         *b_cut,
         *a_cut,
     )
-    ends, observed = lax.optimization_barrier((ends, observed))
+    ends, big = lax.optimization_barrier((ends, big))
     gathered = lax.all_to_all(ends, ("y", "z"), 0, 0)
-    gathered, information = lax.optimization_barrier((gathered, information))
-    informations = [information] + [shift(information, "y", N_Y, by) for by in (1, 2, 3)]
-    big = call(big_powers, stack(5) * 2 + [(square, BF16)] * 2, *small[10:])
-    tree_rows = N_Y * SUB * 31
-    shown, tree_ends, follows, sub_ends, sub_follows, seen = call(
-        block_trees,
-        [
-            ((N_Y * bins, width), F32),
-            ((tree_rows, width), F32),
-            ((tree_rows, width), F32),
-            ((3 * N_Y * SUB, width), F32),
-            ((3 * N_Y * SUB, width), F32),
-            ((N_Y * bins, part), BF16),
-        ],
-        *informations,
-        *lead,
-        *m_cut,
-        *b_cut,
-        *a_cut,
-        *observed,
-    )
     rows = channels // (N_Y * N_Z) + 8
-    smoothed, payload = call(
+    chunk = ((N_Z, rows, width), F32)
+    shown, tree_ends, follows, sub_ends, sub_follows = tree
+    smoothed, *chunks = call(
         states_and_sums,
-        [((bins, width), F32), ((N_Z, rows, width), F32)],
+        [((bins, width), F32)] + [chunk] * N_Y,
         gathered,
         *big[:2],
         *lead,
@@ -546,12 +538,14 @@
         tree_ends,
         follows,
         shown,
-        emission_part,
+        emission,
         seen,
-        natural,
-    )
+    )
+    far, near, back = (shift(chunks[by], "y", N_Y, by) for by in (2, 1, 3))
+    (smoothed,) = call(in_time_order, [((bins, width), F32)], natural, smoothed)
+    (payload,) = call(add_chunks, [chunk], chunks[0], near, far, back)
     payload = lax.all_to_all(payload, "z", 0, 0)
-    (spread,) = call(add_pieces, [((N_Z, rows, width), F32)], payload)
+    (spread,) = call(add_pieces, [chunk], payload)
     whole = lax.all_to_all(spread, "z", 0, 0)
     far, near, back = (shift(whole, "y", N_Y, by) for by in (2, 1, 3))
     cross, moment, error = call(

time: 131 us -> 124 us (0.947)
  the two profiles are of different devices: /device:TPU:24 before, /device:TPU:1 now
where the time goes in v1:
time: 124 us
  blocking collectives  46.5 us (38%)
  waiting for transfers between devices  30.4 us (25%)
  Pallas kernels  27.7 us (22%)
  starting transfers between devices  17.4 us (14%)
    ppermute x11, waiting for transfers between devices, shift(): lax.ppermute(value, axis, [(i, (i + by) % count) for i in range(count)])  30.4 us
    pallas_call x9, Pallas kernels, call(): pl.pallas_call(kernel, out_shape=[(pltpu.HBM if i in sent else pltpu.VMEM...  27.7 us
    all_to_all x1, blocking collectives, local(): gathered = lax.all_to_all(ends, ('y', 'z'), 0, 0)  19.9 us
    ppermute x11, starting transfers between devices, shift(): lax.ppermute(value, axis, [(i, (i + by) % count) for i in range(count)])  17.4 us
    all_to_all x1, blocking collectives, local(): payload = lax.all_to_all(payload, 'z', 0, 0)  13.4 us
    all_to_all x1, blocking collectives, local(): whole = lax.all_to_all(spread, 'z', 0, 0)  13.3 us
  transfers between devices with their start and end apart: 11, of which 7 were waited for; matrix products, arithmetic and copies ran while one was open for 1% of the time, Pallas kernels for 9%

profile of v1, /device:TPU:1, one launch (start us, length us, event | category | flops | bytes accessed | tf_op | source)
XLA Modules:
  0.0 123.8 jit_solution(16391483900938005915)
XLA Ops:
  0.7 2.5 %information_part.1 = (f32[128,256]{1,0:T(8,128)S(1)}, f32[128,256]{1,0:T(8,128)S(1)}, bf16[256,1024]{1,0:T(8,128)(2,1)S(1)}) custom-call(bf16[256,256]{1,0:T(8,128)(2,1)} %constant.4.clone.refs_0_, f32[1,1024]{1,0:T(1,128)} %bitcast.2, bf16[1024,256]{1,0:T(8,128)(2,1)} %refs_20_.1, bf16[256,1024]{1,0:T(8,128)(2,1)} %refs_3_.2), custom_call_target="tpu_custom_call" | custom-call | tf_op jit(solution)/shard_map/information_part/pallas_call | solution.py:90
  3.2 3.3 %collective-permute-start = (f32[128,256]{1,0:T(8,128)S(1)}, f32[128,256]{1,0:T(8,128)S(1)}, u32[]{:S(2)}, u32[]{:S(2)}) collective-permute-start(f32[128,256]{1,0:T(8,128)S(1)} %get-tuple-element.64), channel_id=1, source_target_pairs={{0,1},{1,0},{2,3},{3,2},{4,5},{5,4},{6,7},{7,6},{8,9},{9,8},{10,11... | collective-permute-start | bytes 393224 | tf_op jit(solution)/shard_map/ppermute | solution.py:453
  6.5 1.0 collective-permute-done
  7.5 0.8 collective-permute-start.3
  8.4 0.7 collective-permute-start.2
  9.1 1.0 collective-permute-start.1
  10.1 8.0 %small_powers.1 = (bf16[5,256,256]{2,1,0:T(8,128)(2,1)S(1)}, bf16[5,256,256]{2,1,0:T(8,128)(2,1)S(1)}, bf16[8,256,256]{2,1,0:T(8,128)(2,1)S(1)}, bf16[8,256,256]...) custom-call(f32[256,256]{1,0:T(8,128)S(1)} %copy-done.1, ...), custom_call_target="tpu_custom_call" | custom-call | tf_op jit(solution)/shard_map/small_powers/pallas_call | solution.py:90
  18.2 1.5 %collective-permute-start.4 = (f32[128,256]{1,0:T(8,128)S(1)}, f32[128,256]{1,0:T(8,128)S(1)}, u32[]{:S(2)}, u32[]{:S(2)}) collective-permute-start(f32[128,256]{1,0:T(8,128)S(1)} %add_add_fusion.refs_0_), channel_id=1, source_target_pairs={{0,1},{1,0},{2,3},{3,2},{4,5},{5,4},{6,7},{7,6},{8,9},{9,8},{10,11... | collective-permute-start | bytes 393224 | tf_op jit(solution)/shard_map/ppermute | solution.py:453
  19.6 2.9 %big_powers.1 = (bf16[5,256,256]{2,1,0:T(8,128)(2,1)S(1)}, bf16[5,256,256]{2,1,0:T(8,128)(2,1)S(1)}, bf16[5,256,256]{2,1,0:T(8,128)(2,1)S(1)}, bf16[5,256,256]{2...) custom-call(f32[256,256]{1,0:T(8,128)S(1)} %get-tuple-element.90.refs_0_, ...), custom_call_target="tpu_custom_call" | custom-call | tf_op jit(solution)/shard_map/big_powers/pallas_call | solution.py:90
  22.6 4.8 %block_tree.1 = (f32[32,2,256]{2,1,0:T(2,128)S(1)}, f32[256,256]{1,0:T(8,128)S(1)}, f32[248,256]{1,0:T(8,128)S(1)}, f32[248,256]{1,0:T(8,128)S(1)}, f32[24,256]{1,0:T(8,128)S(1)}, /*index=5*/f32[24,256]{1,0:T(8,128)S(1)}) custom-call(f32[128,256]{1,0:T(8,128)S(1)} %add_add_fusion.refs_0_, f32[128,256]{1,0:T(8,128)S(1)} %collective-permute-done.4.refs_1_, ...), custom_call_target="tpu_custom_call" | custom-call | tf_op jit(solution)/shard_map/block_tree/pallas_call | solution.py:90
  27.4 19.9 %all_to_all.15.refs_0_ = f32[32,2,256]{2,1,0:T(2,128)S(1)} all-to-all(f32[32,2,256]{2,1,0:T(2,128)S(1)} %get-tuple-element.99), channel_id=1, replica_groups=mesh['y'=4,'z'=8,'x'=4,'core'=2] {'y','z'}, dimensions={0} | all-to-all | bytes 131072 | tf_op jit(solution)/shard_map/all_to_all | solution.py:521
  47.2 5.3 %states_and_sums.1 = (f32[256,256]{1,0:T(8,128)S(1)}, f32[8,40,256]{2,1,0:T(8,128)S(1)}, f32[8,40,256]{2,1,0:T(8,128)S(1)}, f32[8,40,256]{2,1,0:T(8,128)S(1)}, f32[8,40,256]{2,1,0:T(8,128)S(1)}) custom-call(f32[32,2,256]{2,1,0:T(2,128)S(1)} %all_to_all.15.refs_0_, bf16[5,256,256]{2,1,0:T(8,128)(2,1)S(1)} %get-tuple-element.100.refs_1_, ...), custom_call_target="tpu_custom_call" | custom-call | tf_op jit(solution)/shard_map/states_and_sums/pallas_call | solution.py:90
  52.6 0.4 collective-permute-start.5
  53.0 1.7 %collective-permute-start.6 = (f32[8,40,256]{2,1,0:T(8,128)S(1)}, f32[8,40,256]{2,1,0:T(8,128)S(1)}, u32[]{:S(2)}, u32[]{:S(2)}) collective-permute-start(f32[8,40,256]{2,1,0:T(8,128)S(1)} %get-tuple-element.117), channel_id=1, source_target_pairs={{0,128},{64,192},{128,0},{192,64},{1,129},{65,193},{129,1},{193,65... | collective-permute-start | bytes 983048 | tf_op jit(solution)/shard_map/ppermute | solution.py:453
  54.7 1.3 %collective-permute-start.7 = (f32[8,40,256]{2,1,0:T(8,128)S(1)}, f32[8,40,256]{2,1,0:T(8,128)S(1)}, u32[]{:S(2)}, u32[]{:S(2)}) collective-permute-start(f32[8,40,256]{2,1,0:T(8,128)S(1)} %get-tuple-element.118), channel_id=1, source_target_pairs={{0,192},{64,0},{128,64},{192,128},{1,193},{65,1},{129,65},{193,129... | collective-permute-start | bytes 983048 | tf_op jit(solution)/shard_map/ppermute | solution.py:453
  56.1 6.2 %collective-permute-done.5.refs_1_ = f32[8,40,256]{2,1,0:T(8,128)S(1)} collective-permute-done((f32[8,40,256]{2,1,0:T(8,128)S(1)}, f32[8,40,256]{2,1,0:T(8,128)S(1)}, u32[]{:S(2)}, u32[]{:S(2)}) %collective-permute-start.5) | collective-permute-done | bytes 327712 | tf_op jit(solution)/shard_map/ppermute | solution.py:453
  62.2 5.9 %collective-permute-done.6.refs_2_ = f32[8,40,256]{2,1,0:T(8,128)S(1)} collective-permute-done((f32[8,40,256]{2,1,0:T(8,128)S(1)}, f32[8,40,256]{2,1,0:T(8,128)S(1)}, u32[]{:S(2)}, u32[]{:S(2)}) %collective-permute-start.6) | collective-permute-done | bytes 327712 | tf_op jit(solution)/shard_map/ppermute | solution.py:453
  68.1 2.0 %collective-permute-done.7.refs_3_ = f32[8,40,256]{2,1,0:T(8,128)S(1)} collective-permute-done((f32[8,40,256]{2,1,0:T(8,128)S(1)}, f32[8,40,256]{2,1,0:T(8,128)S(1)}, u32[]{:S(2)}, u32[]{:S(2)}) %collective-permute-start.7) | collective-permute-done | bytes 327712 | tf_op jit(solution)/shard_map/ppermute | solution.py:453
  70.1 0.6 add_chunks.1
  70.7 13.4 %all_to_all.16.refs_0_ = f32[8,40,256]{2,1,0:T(8,128)S(1)} all-to-all(f32[8,40,256]{2,1,0:T(8,128)S(1)} %add_chunks.1), channel_id=1, replica_groups=mesh['y'=4,'z'=8,'x'=4,'core'=2] {'z'}, dimensions={0} | all-to-all | bytes 655360 | tf_op jit(solution)/shard_map/all_to_all | solution.py:547
  84.1 0.6 add_pieces.1
  84.7 0.0 copy-start.5
  84.7 13.3 %all_to_all.17.refs_0_ = f32[8,40,256]{2,1,0:T(8,128)S(1)} all-to-all(f32[8,40,256]{2,1,0:T(8,128)S(1)} %add_pieces.1), channel_id=1, replica_groups=mesh['y'=4,'z'=8,'x'=4,'core'=2] {'z'}, dimensions={0} | all-to-all | bytes 655360 | tf_op jit(solution)/shard_map/all_to_all | solution.py:549
  98.0 6.0 %collective-permute-start.10 = (f32[8,40,256]{2,1,0:T(8,128)S(1)}, f32[8,40,256]{2,1,0:T(8,128)S(1)}, u32[]{:S(2)}, u32[]{:S(2)}) collective-permute-start(f32[8,40,256]{2,1,0:T(8,128)S(1)} %all_to_all.17.refs_0_), channel_id=1, source_target_pairs={{0,192},{64,0},{128,64},{192,128},{1,193},{65,1},{129,65},{193,129... | collective-permute-start | bytes 983048 | tf_op jit(solution)/shard_map/ppermute | solution.py:453
  104.0 0.1 collective-permute-start.9
  104.1 0.5 collective-permute-start.8
  104.6 0.8 in_time_order.1
  105.4 0.7 copy.13
  106.1 4.6 %collective-permute-done.10.refs_3_ = f32[8,40,256]{2,1,0:T(8,128)S(1)} collective-permute-done((f32[8,40,256]{2,1,0:T(8,128)S(1)}, f32[8,40,256]{2,1,0:T(8,128)S(1)}, u32[]{:S(2)}, u32[]{:S(2)}) %collective-permute-start.10) | collective-permute-done | bytes 327712 | tf_op jit(solution)/shard_map/ppermute | solution.py:453
  110.7 0.8 collective-permute-done.9.refs_2_
  111.5 10.0 %collective-permute-done.8.refs_1_ = f32[8,40,256]{2,1,0:T(8,128)S(1)} collective-permute-done((f32[8,40,256]{2,1,0:T(8,128)S(1)}, f32[8,40,256]{2,1,0:T(8,128)S(1)}, u32[]{:S(2)}, u32[]{:S(2)}) %collective-permute-start.8) | collective-permute-done | bytes 327712 | tf_op jit(solution)/shard_map/ppermute | solution.py:453
  121.5 2.1 %assemble.1 = (f32[1024,256]{1,0:T(8,128)}, f32[256,256]{1,0:T(8,128)}, f32[1,1024]{1,0:T(1,128)}) custom-call(f32[8,40,256]{2,1,0:T(8,128)S(1)} %all_to_all.17.refs_0_, f32[8,40,256]{2,1,0:T(8,128)S(1)} %collective-permute-done.8.refs_1_, f32[8,40,256]{2,1,0:T(8,128)S(1)} %collective-permute-done.9.refs_2_, f32[8,40,256]{2,1,0:T(8,128)S(1)} %collective-permute-done.10.refs_3_), custom_call_target="tpu_custom_call" | custom-call | tf_op jit(solution)/shard_map/assemble/pallas_call | solution.py:90
  (17 shorter events, 0.1 us)
Async XLA Ops:
  0.6 9.5 %copy-start.2 = (f32[256,256]{1,0:T(8,128)S(1)}, f32[256,256]{1,0:T(8,128)}, u32[]{:S(2)}) copy-start(f32[256,256]{1,0:T(8,128)} %refs_1_.1) | copy-start | bytes 786436
  0.6 9.5 %copy-start.3 = (f32[256,256]{1,0:T(8,128)S(1)}, f32[256,256]{1,0:T(8,128)}, u32[]{:S(2)}) copy-start(f32[256,256]{1,0:T(8,128)} %refs_2_.3) | copy-start | bytes 786436
  0.7 9.5 %copy-start.4 = (f32[256,256]{1,0:T(8,128)S(1)}, f32[256,256]{1,0:T(8,128)}, u32[]{:S(2)}) copy-start(f32[256,256]{1,0:T(8,128)} %refs_3_.3) | copy-start | bytes 786436
  3.2 6.9 %copy-start.1 = (f32[256,256]{1,0:T(8,128)S(1)}, f32[256,256]{1,0:T(8,128)}, u32[]{:S(2)}) copy-start(f32[256,256]{1,0:T(8,128)} %refs_0_.3) | copy-start | bytes 786436
  3.2 4.3 %collective-permute-start = (f32[128,256]{1,0:T(8,128)S(1)}, f32[128,256]{1,0:T(8,128)S(1)}, u32[]{:S(2)}, u32[]{:S(2)}) collective-permute-start(f32[128,256]{1,0:T(8,128)S(1)} %get-tuple-element.64), channel_id=1, source_target_pairs={{0,1},{1,0},{2,3},{3,2},{4,5},{5,4},{6,7},{7,6},{8,9},{9,8},{10,11... | collective-permute-start | bytes 393224 | tf_op jit(solution)/shard_map/ppermute | solution.py:453
  7.5 10.6 %collective-permute-start.3 = (f32[128,256]{1,0:T(8,128)S(1)}, f32[128,256]{1,0:T(8,128)S(1)}, u32[]{:S(2)}, u32[]{:S(2)}) collective-permute-start(f32[128,256]{1,0:T(8,128)S(1)} %add.12), channel_id=1, source_target_pairs={{0,6},{2,0},{4,2},{6,4},{1,7},{3,1},{5,3},{7,5},{8,14},{10,8},{12,... | collective-permute-start | bytes 393224 | tf_op jit(solution)/shard_map/ppermute | solution.py:453
  8.4 9.7 %collective-permute-start.2 = (f32[128,256]{1,0:T(8,128)S(1)}, f32[128,256]{1,0:T(8,128)S(1)}, u32[]{:S(2)}, u32[]{:S(2)}) collective-permute-start(f32[128,256]{1,0:T(8,128)S(1)} %add.12), channel_id=1, source_target_pairs={{0,2},{2,4},{4,6},{6,0},{1,3},{3,5},{5,7},{7,1},{8,10},{10,12},{12... | collective-permute-start | bytes 393224 | tf_op jit(solution)/shard_map/ppermute | solution.py:453
  9.1 9.0 %collective-permute-start.1 = (f32[128,256]{1,0:T(8,128)S(1)}, f32[128,256]{1,0:T(8,128)S(1)}, u32[]{:S(2)}, u32[]{:S(2)}) collective-permute-start(f32[128,256]{1,0:T(8,128)S(1)} %add.12), channel_id=1, source_target_pairs={{0,4},{2,6},{4,0},{6,2},{1,5},{3,7},{5,1},{7,3},{8,12},{10,14},{12... | collective-permute-start | bytes 393224 | tf_op jit(solution)/shard_map/ppermute | solution.py:453
  18.2 4.4 %collective-permute-start.4 = (f32[128,256]{1,0:T(8,128)S(1)}, f32[128,256]{1,0:T(8,128)S(1)}, u32[]{:S(2)}, u32[]{:S(2)}) collective-permute-start(f32[128,256]{1,0:T(8,128)S(1)} %add_add_fusion.refs_0_), channel_id=1, source_target_pairs={{0,1},{1,0},{2,3},{3,2},{4,5},{5,4},{6,7},{7,6},{8,9},{9,8},{10,11... | collective-permute-start | bytes 393224 | tf_op jit(solution)/shard_map/ppermute | solution.py:453
  22.6 24.7 %copy-start = (bf16[1024,256]{1,0:T(8,128)(2,1)S(1)}, bf16[1024,256]{1,0:T(8,128)(2,1)}, u32[]{:S(2)}) copy-start(bf16[1024,256]{1,0:T(8,128)(2,1)} %refs_20_.1) | copy-start | bytes 1572868
  52.6 9.7 %collective-permute-start.5 = (f32[8,40,256]{2,1,0:T(8,128)S(1)}, f32[8,40,256]{2,1,0:T(8,128)S(1)}, u32[]{:S(2)}, u32[]{:S(2)}) collective-permute-start(f32[8,40,256]{2,1,0:T(8,128)S(1)} %get-tuple-element.116), channel_id=1, source_target_pairs={{0,64},{64,128},{128,192},{192,0},{1,65},{65,129},{129,193},{193,1... | collective-permute-start | bytes 983048 | tf_op jit(solution)/shard_map/ppermute | solution.py:453
  53.0 15.1 %collective-permute-start.6 = (f32[8,40,256]{2,1,0:T(8,128)S(1)}, f32[8,40,256]{2,1,0:T(8,128)S(1)}, u32[]{:S(2)}, u32[]{:S(2)}) collective-permute-start(f32[8,40,256]{2,1,0:T(8,128)S(1)} %get-tuple-element.117), channel_id=1, source_target_pairs={{0,128},{64,192},{128,0},{192,64},{1,129},{65,193},{129,1},{193,65... | collective-permute-start | bytes 983048 | tf_op jit(solution)/shard_map/ppermute | solution.py:453
  54.7 15.4 %collective-permute-start.7 = (f32[8,40,256]{2,1,0:T(8,128)S(1)}, f32[8,40,256]{2,1,0:T(8,128)S(1)}, u32[]{:S(2)}, u32[]{:S(2)}) collective-permute-start(f32[8,40,256]{2,1,0:T(8,128)S(1)} %get-tuple-element.118), channel_id=1, source_target_pairs={{0,192},{64,0},{128,64},{192,128},{1,193},{65,1},{129,65},{193,129... | collective-permute-start | bytes 983048 | tf_op jit(solution)/shard_map/ppermute | solution.py:453
  84.7 19.9 %copy-start.5 = (bf16[256,256]{1,0:T(8,128)(2,1)S(1)}, bf16[256,256]{1,0:T(8,128)(2,1)}, u32[]{:S(2)}) copy-start(bf16[256,256]{1,0:T(8,128)(2,1)} %constant.5.clone.refs_0_) | copy-start | bytes 393220
  98.0 12.7 %collective-permute-start.10 = (f32[8,40,256]{2,1,0:T(8,128)S(1)}, f32[8,40,256]{2,1,0:T(8,128)S(1)}, u32[]{:S(2)}, u32[]{:S(2)}) collective-permute-start(f32[8,40,256]{2,1,0:T(8,128)S(1)} %all_to_all.17.refs_0_), channel_id=1, source_target_pairs={{0,192},{64,0},{128,64},{192,128},{1,193},{65,1},{129,65},{193,129... | collective-permute-start | bytes 983048 | tf_op jit(solution)/shard_map/ppermute | solution.py:453
  104.0 7.5 %collective-permute-start.9 = (f32[8,40,256]{2,1,0:T(8,128)S(1)}, f32[8,40,256]{2,1,0:T(8,128)S(1)}, u32[]{:S(2)}, u32[]{:S(2)}) collective-permute-start(f32[8,40,256]{2,1,0:T(8,128)S(1)} %all_to_all.17.refs_0_), channel_id=1, source_target_pairs={{0,128},{64,192},{128,0},{192,64},{1,129},{65,193},{129,1},{193,65... | collective-permute-start | bytes 983048 | tf_op jit(solution)/shard_map/ppermute | solution.py:453
  104.1 17.4 %collective-permute-start.8 = (f32[8,40,256]{2,1,0:T(8,128)S(1)}, f32[8,40,256]{2,1,0:T(8,128)S(1)}, u32[]{:S(2)}, u32[]{:S(2)}) collective-permute-start(f32[8,40,256]{2,1,0:T(8,128)S(1)} %all_to_all.17.refs_0_), channel_id=1, source_target_pairs={{0,64},{64,128},{128,192},{192,0},{1,65},{65,129},{129,193},{193,1... | collective-permute-start | bytes 983048 | tf_op jit(solution)/shard_map/ppermute | solution.py:453

commit v2 on v1

--- a/solution.py
+++ b/solution.py
@@ -31,26 +31,29 @@
     return [(i * (shape[0] // count), shape[0] // count) for i in range(count)]
 
 
-def call(body, outs, *args, large=(), sent=(), limit=16):
+def call(body, outs, *args, large=(), sent=(), aliases={}, limit=16):
     if not KERNELS:
         results = [jnp.zeros(shape, dtype) for shape, dtype in outs]
+        for i in aliases:
+            results[aliases[i]] = args[i]
         for i, place, value in body(*args):
             if place is None:
                 results[i] = value
             elif isinstance(place, int):
                 results[i] = results[i].at[place].set(value)
             else:
-                results[i] = results[i].at[place[0] : place[0] + place[1]].set(value)
+                results[i] = lax.dynamic_update_slice_in_dim(results[i], value, place[0], 0)
         return results
 
     n_in, n_out = len(args), len(outs)
+    loaded = [i for i in large if i not in aliases]
 
     def kernel(*refs):
         values, out_refs, rest = list(refs[:n_in]), refs[n_in : n_in + n_out], refs[n_in + n_out :]
-        targets = dict(zip(sent, rest[len(large) : -2]))
+        targets = dict(zip(sent, rest[len(loaded) : -2]))
         in_sems, out_sems = rest[-2:]
         number = 0
-        for i, buffer in zip(large, rest[: len(large)]):
+        for i, buffer in zip(loaded, rest[: len(loaded)]):
             copies = []
             for start, size in pieces_of(buffer.shape):
                 rows = pl.ds(start, size)
@@ -70,9 +73,9 @@
                 continue
             buffer = targets[i]
             buffer[index] = value
-            spans = pieces_of(value.shape) if place is None else [place]
-            for start, size in spans:
-                rows = pl.ds(start, size)
+            first = 0 if place is None else place[0]
+            for start, size in pieces_of(value.shape):
+                rows = pl.ds(first + start, size)
                 leaving.append(
                     pltpu.make_async_copy(
                         buffer.at[rows], out_refs[i].at[rows], out_sems.at[len(leaving)]
@@ -92,9 +95,10 @@
         out_shape=[(pltpu.HBM if i in sent else pltpu.VMEM)(*kind) for i, kind in enumerate(outs)],
         in_specs=[far if i in large else vmem for i in range(n_in)],
         out_specs=[far if i in sent else vmem for i in range(n_out)],
-        scratch_shapes=[pltpu.VMEM(args[i].shape, args[i].dtype) for i in large]
+        scratch_shapes=[pltpu.VMEM(args[i].shape, args[i].dtype) for i in loaded]
         + [pltpu.VMEM(*outs[i]) for i in sent]
         + [pltpu.SemaphoreType.DMA((32,)), pltpu.SemaphoreType.DMA((32,))],
+        input_output_aliases=dict(aliases),
         compiler_params=pltpu.CompilerParams(vmem_limit_bytes=limit * 2**20),
         name=body.__name__,
     )(*args)
@@ -149,11 +153,12 @@
 
 
 def mul(rows, matrix):
-    return dot_pairs(pairs_of(rows, matrix))[: rows[2]]
-
-
-def pairs_of(rows, matrix):
-    return [(rows[0], matrix[0]), (rows[1], matrix[0]), (rows[0], matrix[1])]
+    count = rows[0].shape[0]
+    if count > 128:
+        return dot_pairs([(rows[0], matrix[0]), (rows[1], matrix[0]), (rows[0], matrix[1])])
+    found = dot(jnp.concatenate(rows[:2], axis=0), matrix[0])
+    found = found[:count] + (found[count:] + dot(rows[0], matrix[1]))
+    return found[: rows[2]]
 
 
 def at(matrices, level):
@@ -165,24 +170,31 @@
     yield first + 1, place, value[1]
 
 
+def squares(a, b, level):
+    if level < 3:
+        a, b = cut_full(a), cut_full(b)
+        return dot_full(a, a), dot_full(b, b)
+    a, b = cut(a), cut(b)
+    return mul(a, a), mul(b, b)
+
+
 def small_powers(transition, info_gain, smoother_gain, smoother_input):
-    a, g = cut_full(transition[...].T), cut_full(smoother_input[...].T)
-    b, k = cut_full(smoother_gain[...].T), cut_full(info_gain[...].T)
-    ag = dot_full(a, g)
-    kg = dot_full(k, g)
-    m = dot_full(cut_full(ag), b)
-    for i, value in enumerate([k, cut(kg), cut(dot_full(cut_full(kg), b)), cut(ag), g]):
+    a, g = transition[...].T, cut(smoother_input[...].T)
+    b, k = smoother_gain[...].T, cut(info_gain[...].T)
+    a_cut, b_cut = cut(a), cut(b)
+    ag = cut(mul(a_cut, g))
+    kg = cut(mul(k, g))
+    m = mul(ag, b_cut)
+    for i, value in enumerate([k, kg, cut(mul(kg, b_cut)), ag, g]):
         yield from put(0, i, value)
     for level in range(8):
-        m_cut = cut(m)
-        yield from put(2, level, a)
-        yield from put(4, level, b)
+        a_cut, b_cut, m_cut = cut(a), cut(b), cut(m)
+        yield from put(2, level, a_cut)
+        yield from put(4, level, b_cut)
         yield from put(6, level, m_cut)
-        n_cut = cut(mul((a[0], a[1], a[0].shape[0]), m_cut))
-        m = m + mul(n_cut, b)
-        a, b = dot_full(a, a), dot_full(b, b)
-        if level < 7:
-            a, b = cut_full(a), cut_full(b)
+        n_cut = cut(mul(a_cut, m_cut))
+        m = m + mul(n_cut, b_cut)
+        a, b = squares(a, b, level)
         yield from put(8, level, n_cut)
     yield 10, None, a
     yield 11, None, b
@@ -193,11 +205,10 @@
     yield from put(4, None, cut(m[...]))
     a, b = a[...], b[...]
     for level in range(5):
-        a, b = cut_full(a), cut_full(b)
-        yield from put(0, level, a)
-        yield from put(2, level, b)
+        yield from put(0, level, cut(a))
+        yield from put(2, level, cut(b))
         if level < 4:
-            a, b = dot_full(a, a), dot_full(b, b)
+            a, b = squares(a, b, 8 + level)
 
 
 def information_part(order, noise_precision, emission, observations):
@@ -337,10 +348,8 @@
 
     def children(enter, follow, level):
         enter = cut(enter)
-        first = pairs_of(enter, at((n_h, n_l), level)) + pairs_of(
-            cut(follow), at((b_h, b_l), level)
-        )
-        return mul(enter, at((a_h, a_l), level)), dot_pairs(first)[: enter[2]]
+        first = mul(enter, at((n_h, n_l), level)) + mul(cut(follow), at((b_h, b_l), level))
+        return mul(enter, at((a_h, a_l), level)), first
 
     enter, follow = picked(enter), picked(follow)
     count = SUB
@@ -422,31 +431,54 @@
     yield 0, None, jnp.broadcast_to(total[None], (N_Z,) + total.shape)
 
 
-def assemble(bins, *sums):
-    place = lax.axis_index("y")
-    sums = [part[...] for part in sums]
-    width = sums[0].shape[2]
-    share = width // N_Y
-    line = sums[0].shape[1] - 8
-    lane = lax.broadcasted_iota(jnp.int32, (8, width), 1)
-    cross, moment, errors = [], [], []
-    for y in range(N_Y):
-        whole = chosen(place, [sums[(i - y) % N_Y] for i in range(N_Y)])
-        cross.append(whole[:, :line].reshape(-1, width) * (1.0 / math.sqrt(bins)))
-        moment.append(whole[:, line:].reshape(-1, width))
+def blocks_of(bins, by_pieces):
+    y = lax.axis_index("y")
+    for by, piece in by_pieces:
+        place = y - by
+        place = jnp.where(place < 0, place + N_Y, place)
+        width = piece.shape[2]
+        share, line = width // N_Y, piece.shape[1] - 8
+        cross = piece[:, :line].reshape(-1, width) * (1.0 / math.sqrt(bins))
+        moment = piece[:, line:].reshape(-1, width)
+        lane = lax.broadcasted_iota(jnp.int32, (8, width), 1)
+        free = share * jnp.where(place == N_Y - 1, 0, place + 1)
         error = jnp.zeros((8, width), F32)
         for z in range(N_Z):
-            turned = roll_lanes(whole[z, line:], (line * z - share * ((y + 1) % N_Y)) % width)
+            turned = roll_lanes(moment[8 * z : 8 * z + 8], width + line * z - free)
             error = jnp.where((lane >= line * z) & (lane < line * z + line), turned, error)
-        errors.append(error[:1] * (1.0 / bins))
-    moment = jnp.concatenate(moment, axis=0)
+        yield 0, (tiled(place * cross.shape[0]), cross.shape[0]), cross
+        yield 1, (tiled(place * share), share), moment
+        yield 2, (tiled(place * 8), 8), error
+
+
+def tiled(start):
+    return pl.multiple_of(start, 8) if KERNELS else start
+
+
+def first_blocks(bins, own, far):
+    yield from blocks_of(bins, [(0, own[...]), (2, far[...])])
+
+
+def last_blocks(bins, near, back, cross, moments, errors):
+    moment, error = moments[...], errors[...]
+    for i, (start, size), value in blocks_of(bins, [(1, near[...]), (3, back[...])]):
+        if i == 0:
+            yield 0, (start, size), value
+            continue
+        rows = moment if i == 1 else error
+        mine = (row_index(rows) >= start) & (row_index(rows) < start + size)
+        rows = jnp.where(mine, jnp.concatenate([value] * N_Y, axis=0), rows)
+        if i == 1:
+            moment = rows
+        else:
+            error = rows
+    share = moment.shape[0] // N_Y
     row = lax.broadcasted_iota(jnp.int32, moment.shape, 0) // share
     column = lax.broadcasted_iota(jnp.int32, moment.shape, 1) // share
     free = column == jnp.where(row == N_Y - 1, 0, row + 1)
-    moment = jnp.where(free, moment.T, moment) * (1.0 / bins)
-    yield 0, None, jnp.concatenate(cross, axis=0)
-    yield 1, None, moment
-    yield 2, None, jnp.concatenate(errors, axis=1)
+    yield 1, None, jnp.where(free, moment.T, moment) * (1.0 / bins)
+    error = jnp.concatenate([error[8 * i : 8 * i + 1] for i in range(N_Y)], axis=1)
+    yield 2, None, error * (1.0 / bins)
 
 
 def shift(value, axis, count, by):
@@ -548,14 +580,22 @@
     (spread,) = call(add_pieces, [chunk], payload)
     whole = lax.all_to_all(spread, "z", 0, 0)
     far, near, back = (shift(whole, "y", N_Y, by) for by in (2, 1, 3))
+    named = lambda body: functools.wraps(body)(functools.partial(body, bins * BLOCKS))
+    kinds = [((channels, width), F32), (square, F32)]
     cross, moment, error = call(
-        functools.wraps(assemble)(functools.partial(assemble, bins * BLOCKS)),
-        [((channels, width), F32), (square, F32), ((1, channels), F32)],
-        whole,
+        named(first_blocks), kinds + [((8 * N_Y, width), F32)], whole, far, sent=(0,)
+    )
+    cross, moment, error = call(
+        named(last_blocks),
+        kinds + [((1, channels), F32)],
         near,
-        far,
         back,
+        cross,
+        moment,
+        error,
+        large=(2,),
         sent=(0, 1, 2),
+        aliases={2: 0},
     )
     return smoothed, cross, error.reshape(channels), moment
 

time: 124 us -> 118 us (0.952)
  the two profiles are of different devices: /device:TPU:1 before, /device:TPU:24 now
where the time goes in v2:
time: 118 us; the launch traced here: 117 us
  blocking collectives  51.3 us (43%)
  waiting for transfers between devices  25.6 us (22%)
  Pallas kernels  25.3 us (21%)
  starting transfers between devices  13.2 us (11%)
    ppermute x11, waiting for transfers between devices, shift(): lax.ppermute(value, axis, [(i, (i + by) % count) for i in range(count)])  25.6 us
    pallas_call x10, Pallas kernels, call(): pl.pallas_call(kernel, out_shape=[(pltpu.HBM if i in sent else pltpu.VMEM...  25.3 us
    all_to_all x1, blocking collectives, local(): gathered = lax.all_to_all(ends, ('y', 'z'), 0, 0)  19.6 us
    all_to_all x1, blocking collectives, local(): payload = lax.all_to_all(payload, 'z', 0, 0)  16.1 us
    all_to_all x1, blocking collectives, local(): whole = lax.all_to_all(spread, 'z', 0, 0)  15.6 us
    ppermute x11, starting transfers between devices, shift(): lax.ppermute(value, axis, [(i, (i + by) % count) for i in range(count)])  13.2 us
  transfers between devices with their start and end apart: 11, of which 6 were waited for; matrix products, arithmetic and copies ran while one was open for 1% of the time, Pallas kernels for 9%

profile of v2, /device:TPU:24, one launch (start us, length us, event | category | flops | bytes accessed | tf_op | source)
XLA Modules:
  0.0 117.1 jit_solution(2533894030946104232)
XLA Ops:
  0.7 2.5 %information_part.1 = (f32[128,256]{1,0:T(8,128)S(1)}, f32[128,256]{1,0:T(8,128)S(1)}, bf16[256,1024]{1,0:T(8,128)(2,1)S(1)}) custom-call(bf16[256,256]{1,0:T(8,128)(2,1)} %constant.4.clone.refs_0_, f32[1,1024]{1,0:T(1,128)} %bitcast.2, bf16[1024,256]{1,0:T(8,128)(2,1)} %refs_20_.1, bf16[256,1024]{1,0:T(8,128)(2,1)} %refs_3_.2), custom_call_target="tpu_custom_call" | custom-call | tf_op jit(solution)/shard_map/information_part/pallas_call | solution.py:93
  3.2 0.0 copy-start.1
  3.2 0.1 collective-permute-start
  3.3 1.3 %collective-permute-done = f32[128,256]{1,0:T(8,128)S(1)} collective-permute-done((f32[128,256]{1,0:T(8,128)S(1)}, f32[128,256]{1,0:T(8,128)S(1)}, u32[]{:S(2)}, u32[]{:S(2)}) %collective-permute-start) | collective-permute-done | bytes 131104 | tf_op jit(solution)/shard_map/ppermute | solution.py:485
  4.7 2.8 %collective-permute-start.3 = (f32[128,256]{1,0:T(8,128)S(1)}, f32[128,256]{1,0:T(8,128)S(1)}, u32[]{:S(2)}, u32[]{:S(2)}) collective-permute-start(f32[128,256]{1,0:T(8,128)S(1)} %add.12), channel_id=1, source_target_pairs={{0,6},{2,0},{4,2},{6,4},{1,7},{3,1},{5,3},{7,5},{8,14},{10,8},{12,... | collective-permute-start | bytes 393224 | tf_op jit(solution)/shard_map/ppermute | solution.py:485
  7.5 2.3 %collective-permute-start.1 = (f32[128,256]{1,0:T(8,128)S(1)}, f32[128,256]{1,0:T(8,128)S(1)}, u32[]{:S(2)}, u32[]{:S(2)}) collective-permute-start(f32[128,256]{1,0:T(8,128)S(1)} %add.12), channel_id=1, source_target_pairs={{0,4},{2,6},{4,0},{6,2},{1,5},{3,7},{5,1},{7,3},{8,12},{10,14},{12... | collective-permute-start | bytes 393224 | tf_op jit(solution)/shard_map/ppermute | solution.py:485
  9.8 6.6 %small_powers.1 = (bf16[5,256,256]{2,1,0:T(8,128)(2,1)S(1)}, bf16[5,256,256]{2,1,0:T(8,128)(2,1)S(1)}, bf16[8,256,256]{2,1,0:T(8,128)(2,1)S(1)}, bf16[8,256,256]...) custom-call(f32[256,256]{1,0:T(8,128)S(1)} %copy-done.1, ...), custom_call_target="tpu_custom_call" | custom-call | tf_op jit(solution)/shard_map/small_powers/pallas_call | solution.py:93
  16.4 0.4 collective-permute-done.2
  16.8 0.1 collective-permute-start.4
  16.9 2.1 %big_powers.1 = (bf16[5,256,256]{2,1,0:T(8,128)(2,1)S(1)}, bf16[5,256,256]{2,1,0:T(8,128)(2,1)S(1)}, bf16[5,256,256]{2,1,0:T(8,128)(2,1)S(1)}, bf16[5,256,256]{2...) custom-call(f32[256,256]{1,0:T(8,128)S(1)} %get-tuple-element.93.refs_0_, ...), custom_call_target="tpu_custom_call" | custom-call | tf_op jit(solution)/shard_map/big_powers/pallas_call | solution.py:93
  19.0 0.0 copy-start
  19.0 4.0 %block_tree.1 = (f32[32,2,256]{2,1,0:T(2,128)S(1)}, f32[256,256]{1,0:T(8,128)S(1)}, f32[248,256]{1,0:T(8,128)S(1)}, f32[248,256]{1,0:T(8,128)S(1)}, f32[24,256]{1,0:T(8,128)S(1)}, /*index=5*/f32[24,256]{1,0:T(8,128)S(1)}) custom-call(f32[128,256]{1,0:T(8,128)S(1)} %add_add_fusion.refs_0_, f32[128,256]{1,0:T(8,128)S(1)} %collective-permute-done.4.refs_1_, ...), custom_call_target="tpu_custom_call" | custom-call | tf_op jit(solution)/shard_map/block_tree/pallas_call | solution.py:93
  23.1 19.6 %all_to_all.15.refs_0_ = f32[32,2,256]{2,1,0:T(2,128)S(1)} all-to-all(f32[32,2,256]{2,1,0:T(2,128)S(1)} %get-tuple-element.102), channel_id=1, replica_groups=mesh['y'=4,'z'=8,'x'=4,'core'=2] {'y','z'}, dimensions={0} | all-to-all | bytes 131072 | tf_op jit(solution)/shard_map/all_to_all | solution.py:553
  42.7 4.9 %states_and_sums.1 = (f32[256,256]{1,0:T(8,128)S(1)}, f32[8,40,256]{2,1,0:T(8,128)S(1)}, f32[8,40,256]{2,1,0:T(8,128)S(1)}, f32[8,40,256]{2,1,0:T(8,128)S(1)}, f32[8,40,256]{2,1,0:T(8,128)S(1)}) custom-call(f32[32,2,256]{2,1,0:T(2,128)S(1)} %all_to_all.15.refs_0_, bf16[5,256,256]{2,1,0:T(8,128)(2,1)S(1)} %get-tuple-element.103.refs_1_, ...), custom_call_target="tpu_custom_call" | custom-call | tf_op jit(solution)/shard_map/states_and_sums/pallas_call | solution.py:93
  47.6 2.1 %collective-permute-start.5 = (f32[8,40,256]{2,1,0:T(8,128)S(1)}, f32[8,40,256]{2,1,0:T(8,128)S(1)}, u32[]{:S(2)}, u32[]{:S(2)}) collective-permute-start(f32[8,40,256]{2,1,0:T(8,128)S(1)} %get-tuple-element.119), channel_id=1, source_target_pairs={{0,64},{64,128},{128,192},{192,0},{1,65},{65,129},{129,193},{193,1... | collective-permute-start | bytes 983048 | tf_op jit(solution)/shard_map/ppermute | solution.py:485
  49.8 0.7 collective-permute-start.6
  50.5 0.7 collective-permute-start.7
  51.3 11.8 %collective-permute-done.5.refs_1_ = f32[8,40,256]{2,1,0:T(8,128)S(1)} collective-permute-done((f32[8,40,256]{2,1,0:T(8,128)S(1)}, f32[8,40,256]{2,1,0:T(8,128)S(1)}, u32[]{:S(2)}, u32[]{:S(2)}) %collective-permute-start.5) | collective-permute-done | bytes 327712 | tf_op jit(solution)/shard_map/ppermute | solution.py:485
  63.1 3.7 %collective-permute-done.7.refs_3_ = f32[8,40,256]{2,1,0:T(8,128)S(1)} collective-permute-done((f32[8,40,256]{2,1,0:T(8,128)S(1)}, f32[8,40,256]{2,1,0:T(8,128)S(1)}, u32[]{:S(2)}, u32[]{:S(2)}) %collective-permute-start.7) | collective-permute-done | bytes 327712 | tf_op jit(solution)/shard_map/ppermute | solution.py:485
  66.7 0.6 add_chunks.1
  67.4 16.1 %all_to_all.16.refs_0_ = f32[8,40,256]{2,1,0:T(8,128)S(1)} all-to-all(f32[8,40,256]{2,1,0:T(8,128)S(1)} %add_chunks.1), channel_id=1, replica_groups=mesh['y'=4,'z'=8,'x'=4,'core'=2] {'z'}, dimensions={0} | all-to-all | bytes 655360 | tf_op jit(solution)/shard_map/all_to_all | solution.py:579
  83.5 0.6 add_pieces.1
  84.1 0.0 copy-start.5
  84.1 15.6 %all_to_all.17.refs_0_ = f32[8,40,256]{2,1,0:T(8,128)S(1)} all-to-all(f32[8,40,256]{2,1,0:T(8,128)S(1)} %add_pieces.1), channel_id=1, replica_groups=mesh['y'=4,'z'=8,'x'=4,'core'=2] {'z'}, dimensions={0} | all-to-all | bytes 655360 | tf_op jit(solution)/shard_map/all_to_all | solution.py:581
  99.7 1.0 collective-permute-start.10
  100.7 3.2 %collective-permute-start.8 = (f32[8,40,256]{2,1,0:T(8,128)S(1)}, f32[8,40,256]{2,1,0:T(8,128)S(1)}, u32[]{:S(2)}, u32[]{:S(2)}) collective-permute-start(f32[8,40,256]{2,1,0:T(8,128)S(1)} %all_to_all.17.refs_0_), channel_id=1, source_target_pairs={{0,64},{64,128},{128,192},{192,0},{1,65},{65,129},{129,193},{193,1... | collective-permute-start | bytes 983048 | tf_op jit(solution)/shard_map/ppermute | solution.py:485
  103.9 0.8 in_time_order.1
  104.8 0.7 copy.15
  105.5 6.3 %collective-permute-done.10.refs_1_ = f32[8,40,256]{2,1,0:T(8,128)S(1)} collective-permute-done((f32[8,40,256]{2,1,0:T(8,128)S(1)}, f32[8,40,256]{2,1,0:T(8,128)S(1)}, u32[]{:S(2)}, u32[]{:S(2)}) %collective-permute-start.10) | collective-permute-done | bytes 327712 | tf_op jit(solution)/shard_map/ppermute | solution.py:485
  111.8 1.4 %first_blocks.1 = (f32[1024,256]{1,0:T(8,128)}, f32[256,256]{1,0:T(8,128)S(1)}, f32[32,256]{1,0:T(8,128)S(1)}) custom-call(f32[8,40,256]{2,1,0:T(8,128)S(1)} %all_to_all.17.refs_0_, f32[8,40,256]{2,1,0:T(8,128)S(1)} %collective-permute-done.10.refs_1_), custom_call_target="tpu_custom_call" | custom-call | tf_op jit(solution)/shard_map/first_blocks/pallas_call | solution.py:93
  113.2 2.1 %collective-permute-done.9.refs_1_ = f32[8,40,256]{2,1,0:T(8,128)S(1)} collective-permute-done((f32[8,40,256]{2,1,0:T(8,128)S(1)}, f32[8,40,256]{2,1,0:T(8,128)S(1)}, u32[]{:S(2)}, u32[]{:S(2)}) %collective-permute-start.9) | collective-permute-done | bytes 327712 | tf_op jit(solution)/shard_map/ppermute | solution.py:485
  115.4 1.6 %last_blocks.1 = (f32[1024,256]{1,0:T(8,128)}, f32[256,256]{1,0:T(8,128)}, f32[1,1024]{1,0:T(1,128)}) custom-call(f32[8,40,256]{2,1,0:T(8,128)S(1)} %collective-permute-done.8.refs_0_, f32[8,40,256]{2,1,0:T(8,128)S(1)} %collective-permute-done.9.refs_1_, f32[1024,256]{1,0:T(8,128)} %get-tuple-element.122.refs_2_, ...), custom_call_target="tpu_custom_call", output_to_operand_aliasing={{0}: (2, {})} | custom-call | tf_op jit(solution)/shard_map/last_blocks/pallas_call | solution.py:93
  (18 shorter events, 0.1 us)
Async XLA Ops:
  0.6 9.2 %copy-start.2 = (f32[256,256]{1,0:T(8,128)S(1)}, f32[256,256]{1,0:T(8,128)}, u32[]{:S(2)}) copy-start(f32[256,256]{1,0:T(8,128)} %refs_1_.1) | copy-start | bytes 786436
  0.6 9.2 %copy-start.3 = (f32[256,256]{1,0:T(8,128)S(1)}, f32[256,256]{1,0:T(8,128)}, u32[]{:S(2)}) copy-start(f32[256,256]{1,0:T(8,128)} %refs_2_.3) | copy-start | bytes 786436
  0.7 9.2 %copy-start.4 = (f32[256,256]{1,0:T(8,128)S(1)}, f32[256,256]{1,0:T(8,128)}, u32[]{:S(2)}) copy-start(f32[256,256]{1,0:T(8,128)} %refs_3_.3) | copy-start | bytes 786436
  3.2 6.6 %copy-start.1 = (f32[256,256]{1,0:T(8,128)S(1)}, f32[256,256]{1,0:T(8,128)}, u32[]{:S(2)}) copy-start(f32[256,256]{1,0:T(8,128)} %refs_0_.3) | copy-start | bytes 786436
  3.2 1.4 %collective-permute-start = (f32[128,256]{1,0:T(8,128)S(1)}, f32[128,256]{1,0:T(8,128)S(1)}, u32[]{:S(2)}, u32[]{:S(2)}) collective-permute-start(f32[128,256]{1,0:T(8,128)S(1)} %get-tuple-element.67), channel_id=1, source_target_pairs={{0,1},{1,0},{2,3},{3,2},{4,5},{5,4},{6,7},{7,6},{8,9},{9,8},{10,11... | collective-permute-start | bytes 393224 | tf_op jit(solution)/shard_map/ppermute | solution.py:485
  4.7 11.8 %collective-permute-start.3 = (f32[128,256]{1,0:T(8,128)S(1)}, f32[128,256]{1,0:T(8,128)S(1)}, u32[]{:S(2)}, u32[]{:S(2)}) collective-permute-start(f32[128,256]{1,0:T(8,128)S(1)} %add.12), channel_id=1, source_target_pairs={{0,6},{2,0},{4,2},{6,4},{1,7},{3,1},{5,3},{7,5},{8,14},{10,8},{12,... | collective-permute-start | bytes 393224 | tf_op jit(solution)/shard_map/ppermute | solution.py:485
  7.5 9.3 %collective-permute-start.2 = (f32[128,256]{1,0:T(8,128)S(1)}, f32[128,256]{1,0:T(8,128)S(1)}, u32[]{:S(2)}, u32[]{:S(2)}) collective-permute-start(f32[128,256]{1,0:T(8,128)S(1)} %add.12), channel_id=1, source_target_pairs={{0,2},{2,4},{4,6},{6,0},{1,3},{3,5},{5,7},{7,1},{8,10},{10,12},{12... | collective-permute-start | bytes 393224 | tf_op jit(solution)/shard_map/ppermute | solution.py:485
  7.5 9.3 %collective-permute-start.1 = (f32[128,256]{1,0:T(8,128)S(1)}, f32[128,256]{1,0:T(8,128)S(1)}, u32[]{:S(2)}, u32[]{:S(2)}) collective-permute-start(f32[128,256]{1,0:T(8,128)S(1)} %add.12), channel_id=1, source_target_pairs={{0,4},{2,6},{4,0},{6,2},{1,5},{3,7},{5,1},{7,3},{8,12},{10,14},{12... | collective-permute-start | bytes 393224 | tf_op jit(solution)/shard_map/ppermute | solution.py:485
  16.8 2.2 %collective-permute-start.4 = (f32[128,256]{1,0:T(8,128)S(1)}, f32[128,256]{1,0:T(8,128)S(1)}, u32[]{:S(2)}, u32[]{:S(2)}) collective-permute-start(f32[128,256]{1,0:T(8,128)S(1)} %add_add_fusion.refs_0_), channel_id=1, source_target_pairs={{0,1},{1,0},{2,3},{3,2},{4,5},{5,4},{6,7},{7,6},{8,9},{9,8},{10,11... | collective-permute-start | bytes 393224 | tf_op jit(solution)/shard_map/ppermute | solution.py:485
  19.0 23.7 %copy-start = (bf16[1024,256]{1,0:T(8,128)(2,1)S(1)}, bf16[1024,256]{1,0:T(8,128)(2,1)}, u32[]{:S(2)}) copy-start(bf16[1024,256]{1,0:T(8,128)(2,1)} %refs_20_.1) | copy-start | bytes 1572868
  47.6 15.4 %collective-permute-start.5 = (f32[8,40,256]{2,1,0:T(8,128)S(1)}, f32[8,40,256]{2,1,0:T(8,128)S(1)}, u32[]{:S(2)}, u32[]{:S(2)}) collective-permute-start(f32[8,40,256]{2,1,0:T(8,128)S(1)} %get-tuple-element.119), channel_id=1, source_target_pairs={{0,64},{64,128},{128,192},{192,0},{1,65},{65,129},{129,193},{193,1... | collective-permute-start | bytes 983048 | tf_op jit(solution)/shard_map/ppermute | solution.py:485
  49.8 13.3 %collective-permute-start.6 = (f32[8,40,256]{2,1,0:T(8,128)S(1)}, f32[8,40,256]{2,1,0:T(8,128)S(1)}, u32[]{:S(2)}, u32[]{:S(2)}) collective-permute-start(f32[8,40,256]{2,1,0:T(8,128)S(1)} %get-tuple-element.120), channel_id=1, source_target_pairs={{0,128},{64,192},{128,0},{192,64},{1,129},{65,193},{129,1},{193,65... | collective-permute-start | bytes 983048 | tf_op jit(solution)/shard_map/ppermute | solution.py:485
  50.5 16.2 %collective-permute-start.7 = (f32[8,40,256]{2,1,0:T(8,128)S(1)}, f32[8,40,256]{2,1,0:T(8,128)S(1)}, u32[]{:S(2)}, u32[]{:S(2)}) collective-permute-start(f32[8,40,256]{2,1,0:T(8,128)S(1)} %get-tuple-element.121), channel_id=1, source_target_pairs={{0,192},{64,0},{128,64},{192,128},{1,193},{65,1},{129,65},{193,129... | collective-permute-start | bytes 983048 | tf_op jit(solution)/shard_map/ppermute | solution.py:485
  84.1 19.8 %copy-start.5 = (bf16[256,256]{1,0:T(8,128)(2,1)S(1)}, bf16[256,256]{1,0:T(8,128)(2,1)}, u32[]{:S(2)}) copy-start(bf16[256,256]{1,0:T(8,128)(2,1)} %constant.5.clone.refs_0_) | copy-start | bytes 393220
  99.7 12.2 %collective-permute-start.10 = (f32[8,40,256]{2,1,0:T(8,128)S(1)}, f32[8,40,256]{2,1,0:T(8,128)S(1)}, u32[]{:S(2)}, u32[]{:S(2)}) collective-permute-start(f32[8,40,256]{2,1,0:T(8,128)S(1)} %all_to_all.17.refs_0_), channel_id=1, source_target_pairs={{0,128},{64,192},{128,0},{192,64},{1,129},{65,193},{129,1},{193,65... | collective-permute-start | bytes 983048 | tf_op jit(solution)/shard_map/ppermute | solution.py:485
  100.7 14.7 %collective-permute-start.9 = (f32[8,40,256]{2,1,0:T(8,128)S(1)}, f32[8,40,256]{2,1,0:T(8,128)S(1)}, u32[]{:S(2)}, u32[]{:S(2)}) collective-permute-start(f32[8,40,256]{2,1,0:T(8,128)S(1)} %all_to_all.17.refs_0_), channel_id=1, source_target_pairs={{0,192},{64,0},{128,64},{192,128},{1,193},{65,1},{129,65},{193,129... | collective-permute-start | bytes 983048 | tf_op jit(solution)/shard_map/ppermute | solution.py:485
  100.7 14.7 %collective-permute-start.8 = (f32[8,40,256]{2,1,0:T(8,128)S(1)}, f32[8,40,256]{2,1,0:T(8,128)S(1)}, u32[]{:S(2)}, u32[]{:S(2)}) collective-permute-start(f32[8,40,256]{2,1,0:T(8,128)S(1)} %all_to_all.17.refs_0_), channel_id=1, source_target_pairs={{0,64},{64,128},{128,192},{192,0},{1,65},{65,129},{129,193},{193,1... | collective-permute-start | bytes 983048 | tf_op jit(solution)/shard_map/ppermute | solution.py:485

commit v3 on v2

--- a/solution.py
+++ b/solution.py
@@ -161,8 +161,11 @@
     return found[: rows[2]]
 
 
-def at(matrices, level):
-    return matrices[0][level], matrices[1][level]
+def at(stacks, level):
+    for high, low in stacks:
+        if level < high.shape[0]:
+            return high[level], low[level]
+        level -= high.shape[0]
 
 
 def put(first, place, value):
@@ -178,37 +181,48 @@
     return mul(a, a), mul(b, b)
 
 
-def small_powers(transition, info_gain, smoother_gain, smoother_input):
+FIRST = 6
+
+
+def powers(transition, info_gain, smoother_gain, smoother_input):
     a, g = transition[...].T, cut(smoother_input[...].T)
     b, k = smoother_gain[...].T, cut(info_gain[...].T)
     a_cut, b_cut = cut(a), cut(b)
     ag = cut(mul(a_cut, g))
     kg = cut(mul(k, g))
-    m = mul(ag, b_cut)
-    for i, value in enumerate([k, kg, cut(mul(kg, b_cut)), ag, g]):
-        yield from put(0, i, value)
-    for level in range(8):
-        a_cut, b_cut, m_cut = cut(a), cut(b), cut(m)
-        yield from put(2, level, a_cut)
-        yield from put(4, level, b_cut)
-        yield from put(6, level, m_cut)
+    m_cut = None
+    for level in range(13):
+        a_cut, b_cut = cut(a), cut(b)
+        place = level if level < 8 else level - 8
+        yield from put(2 if level < 8 else 10, place, a_cut)
+        yield from put(4 if level < 8 else 12, place, b_cut)
+        if level < 12:
+            a, b = squares(a, b, level)
+        if level == 0:
+            m = mul(ag, b_cut)
+            for i, value in enumerate([k, kg, cut(mul(kg, b_cut)), ag, g]):
+                yield from put(0, i, value)
+        if level <= FIRST:
+            m_cut = cut(m)
+            yield from put(6, level, m_cut)
+        if level < FIRST:
+            n_cut = cut(mul(a_cut, m_cut))
+            m = m + mul(n_cut, b_cut)
+            yield from put(8, level, n_cut)
+    yield 14, None, m
+
+
+def last_effects(a_h, a_l, b_h, b_l, m):
+    m = m[...]
+    for level in range(FIRST, 8):
+        m_cut = cut(m)
+        if level > FIRST:
+            yield from put(0, level - FIRST - 1, m_cut)
+        a_cut = (a_h[level], a_l[level], m.shape[0])
         n_cut = cut(mul(a_cut, m_cut))
-        m = m + mul(n_cut, b_cut)
-        a, b = squares(a, b, level)
-        yield from put(8, level, n_cut)
-    yield 10, None, a
-    yield 11, None, b
-    yield 12, None, m
-
-
-def big_powers(a, b, m):
-    yield from put(4, None, cut(m[...]))
-    a, b = a[...], b[...]
-    for level in range(5):
-        yield from put(0, level, cut(a))
-        yield from put(2, level, cut(b))
-        if level < 4:
-            a, b = squares(a, b, 8 + level)
+        yield from put(2, level - FIRST, n_cut)
+        m = m + mul(n_cut, (b_h[level], b_l[level]))
+    yield from put(4, None, cut(m))
 
 
 def information_part(order, noise_precision, emission, observations):
@@ -268,11 +282,14 @@
     )
 
 
-def block_tree(total, theirs, lead_h, lead_l, m_h, m_l, b_h, b_l, a_h, a_l):
+def block_tree(
+    total, theirs, lead_h, lead_l, m_h, m_l, m_last_h, m_last_l, b_h, b_l, a_h, a_l
+):
     information = both_halves(total, theirs)
-    a_cut, b_cut, m_cut = (a_h, a_l), (b_h, b_l), (m_h, m_l)
+    a_cut, b_cut = [(a_h, a_l)], [(b_h, b_l)]
+    m_cut = [(m_h, m_l), (m_last_h, m_last_l)]
     shown, end, start, ends, follows = up_sweep(
-        (lead_h, lead_l), a_cut, b_cut, m_cut, information
+        [(lead_h, lead_l)], a_cut, b_cut, m_cut, information
     )
     end, start, sub_ends, sub_follows = sub_sweep(a_cut, b_cut, m_cut, end, start)
     pair = jnp.concatenate([end[None, :1], start[None, :1]], axis=1)
@@ -313,6 +330,8 @@
     a_l,
     n_h,
     n_l,
+    n_last_h,
+    n_last_l,
     b_h,
     b_l,
     ends,
@@ -329,15 +348,15 @@
     for level in range(5):
         by = 2**level
         before = jnp.where(index >= by, roll(after, by), 0.0)
-        after = after + mul(cut(before), at((a_big_h, a_big_l), level))
+        after = after + mul(cut(before), at([(a_big_h, a_big_l)], level))
     enter = jnp.where(index >= 1, roll(after, 1), 0.0)
     follow = gathered[:, 1] + mul(cut(enter), (m_h[...], m_l[...]))
-    final = after - mul(cut(after), at((lead_h, lead_l), 4))
+    final = after - mul(cut(after), at([(lead_h, lead_l)], 4))
     follow = jnp.where(index < BLOCKS - 1, roll(follow, -1), final)
     for level in range(5):
         by = 2**level
         later = jnp.where(index < BLOCKS - by, roll(follow, -by), 0.0)
-        follow = follow + mul(cut(later), at((b_big_h, b_big_l), level))
+        follow = follow + mul(cut(later), at([(b_big_h, b_big_l)], level))
 
     source = lax.broadcasted_iota(jnp.int32, (16, BLOCKS), 1)
     pick = (source == block).astype(BF16)
@@ -348,8 +367,8 @@
 
     def children(enter, follow, level):
         enter = cut(enter)
-        first = mul(enter, at((n_h, n_l), level)) + mul(cut(follow), at((b_h, b_l), level))
-        return mul(enter, at((a_h, a_l), level)), first
+        first = mul(enter, at([(n_h, n_l), (n_last_h, n_last_l)], level)) + mul(cut(follow), at([(b_h, b_l)], level))
+        return mul(enter, at([(a_h, a_l)], level)), first
 
     enter, follow = picked(enter), picked(follow)
     count = SUB
@@ -373,7 +392,7 @@
         first = follows[bottom:top] + first
         enter = jnp.concatenate([enter, second], axis=0)
         follow = jnp.concatenate([first, follow], axis=0)
-    smoothed = shown[...] + mul(cut(enter), at((lead_h, lead_l), 3)) + follow
+    smoothed = shown[...] + mul(cut(enter), at([(lead_h, lead_l)], 3)) + follow
     observed, emission = observed[...], emission[...]
 
     high, low, _ = cut(smoothed)
@@ -455,13 +474,13 @@
     return pl.multiple_of(start, 8) if KERNELS else start
 
 
-def first_blocks(bins, own, far):
-    yield from blocks_of(bins, [(0, own[...]), (2, far[...])])
-
-
-def last_blocks(bins, near, back, cross, moments, errors):
+def first_blocks(bins, own, near):
+    yield from blocks_of(bins, [(0, own[...]), (1, near[...])])
+
+
+def last_blocks(bins, back, far, cross, moments, errors):
     moment, error = moments[...], errors[...]
-    for i, (start, size), value in blocks_of(bins, [(1, near[...]), (3, back[...])]):
+    for i, (start, size), value in blocks_of(bins, [(3, back[...]), (2, far[...])]):
         if i == 0:
             yield 0, (start, size), value
             continue
@@ -485,6 +504,10 @@
     return lax.ppermute(value, axis, [(i, (i + by) % count) for i in range(count)])
 
 
+def shift_flat(value, axis, count, by):
+    return shift(value.reshape(-1, value.shape[-1]), axis, count, by).reshape(value.shape)
+
+
 def bit_reversed(count):
     bits = count.bit_length() - 1
     return [int(format(i, "0%db" % bits)[::-1], 2) for i in range(count)]
@@ -518,17 +541,23 @@
 
     square = (width, width)
     stack = lambda n: [((n,) + square, BF16)] * 2
-    small = call(
-        small_powers,
-        stack(5) + stack(8) * 4 + [(square, F32)] * 3,
+    known = call(
+        powers,
+        stack(5) + stack(8) * 2 + stack(FIRST + 1) + stack(FIRST) + stack(5) * 2 + [(square, F32)],
         transition,
         info_gain,
         smoother_gain,
         smoother_input,
     )
-    moved, small = lax.optimization_barrier((moved, small))
-    lead, a_cut, b_cut, m_cut, n_cut = (small[i : i + 2] for i in range(0, 10, 2))
-    big = call(big_powers, stack(5) * 2 + [(square, BF16)] * 2, *small[10:])
+    moved, known = lax.optimization_barrier((moved, known))
+    lead, a_cut, b_cut, m_cut, n_cut, a_big, b_big = (known[i : i + 2] for i in range(0, 14, 2))
+    late = call(
+        last_effects,
+        stack(7 - FIRST) + stack(8 - FIRST) + [(square, BF16)] * 2,
+        *a_cut,
+        *b_cut,
+        known[14],
+    )
 
     total = mine + moved[0] + moved[1] + moved[2]
     theirs = shift(total, "core", N_CORE, 1)
@@ -546,10 +575,11 @@
         theirs,
         *lead,
         *m_cut,
+        *late[:2],
         *b_cut,
         *a_cut,
     )
-    ends, big = lax.optimization_barrier((ends, big))
+    ends, late = lax.optimization_barrier((ends, late))
     gathered = lax.all_to_all(ends, ("y", "z"), 0, 0)
     rows = channels // (N_Y * N_Z) + 8
     chunk = ((N_Z, rows, width), F32)
@@ -558,14 +588,15 @@
         states_and_sums,
         [((bins, width), F32)] + [chunk] * N_Y,
         gathered,
-        *big[:2],
+        *a_big,
         *lead,
-        *big[4:],
-        *big[2:4],
+        *late[4:],
+        *b_big,
         sub_ends,
         sub_follows,
         *a_cut,
         *n_cut,
+        *late[2:4],
         *b_cut,
         tree_ends,
         follows,
@@ -573,23 +604,23 @@
         emission,
         seen,
     )
-    far, near, back = (shift(chunks[by], "y", N_Y, by) for by in (2, 1, 3))
+    back, near, far = (shift_flat(chunks[by], "y", N_Y, by) for by in (3, 1, 2))
     (smoothed,) = call(in_time_order, [((bins, width), F32)], natural, smoothed)
-    (payload,) = call(add_chunks, [chunk], chunks[0], near, far, back)
+    (payload,) = call(add_chunks, [chunk], chunks[0], near, back, far)
     payload = lax.all_to_all(payload, "z", 0, 0)
     (spread,) = call(add_pieces, [chunk], payload)
     whole = lax.all_to_all(spread, "z", 0, 0)
-    far, near, back = (shift(whole, "y", N_Y, by) for by in (2, 1, 3))
+    far, near, back = (shift_flat(whole, "y", N_Y, by) for by in (2, 1, 3))
     named = lambda body: functools.wraps(body)(functools.partial(body, bins * BLOCKS))
     kinds = [((channels, width), F32), (square, F32)]
     cross, moment, error = call(
-        named(first_blocks), kinds + [((8 * N_Y, width), F32)], whole, far, sent=(0,)
+        named(first_blocks), kinds + [((8 * N_Y, width), F32)], whole, near, sent=(0,)
     )
     cross, moment, error = call(
         named(last_blocks),
         kinds + [((1, channels), F32)],
-        near,
         back,
+        far,
         cross,
         moment,
         error,

time: 118 us -> 111 us (0.941)
  blocking collectives: 51.3 us -> 46.7 us
  waiting for transfers between devices: 25.6 us -> 24.2 us
    all_to_all x1, blocking collectives: 16.1 us -> 13.6 us  [local(): payload = lax.all_to_all(payload, 'z', 0, 0)]
    all_to_all x1, blocking collectives: 15.6 us -> 13.7 us  [local(): whole = lax.all_to_all(spread, 'z', 0, 0)]
    ppermute x11, waiting for transfers between devices: 25.6 us -> 24.2 us  [shift(): lax.ppermute(value, axis, [(i, (i + by) % count) for i in range(count)])]
  transfers between devices with their start and end apart: 11 -> 11, of which waited for: 6 -> 6; matrix products, arithmetic and copies ran while one was open for 1% -> 1% of each run, Pallas kernels for 9% -> 10%
where the time goes in v3:
time: 111 us
  blocking collectives  46.7 us (42%)
  Pallas kernels  25.4 us (23%)
  waiting for transfers between devices  24.2 us (22%)
  starting transfers between devices  12.5 us (11%)
    pallas_call x10, Pallas kernels, call(): pl.pallas_call(kernel, out_shape=[(pltpu.HBM if i in sent else pltpu.VMEM...  25.4 us
    ppermute x11, waiting for transfers between devices, shift(): lax.ppermute(value, axis, [(i, (i + by) % count) for i in range(count)])  24.2 us
    all_to_all x1, blocking collectives, local(): gathered = lax.all_to_all(ends, ('y', 'z'), 0, 0)  19.4 us
    all_to_all x1, blocking collectives, local(): whole = lax.all_to_all(spread, 'z', 0, 0)  13.7 us
    all_to_all x1, blocking collectives, local(): payload = lax.all_to_all(payload, 'z', 0, 0)  13.6 us
    ppermute x11, starting transfers between devices, shift(): lax.ppermute(value, axis, [(i, (i + by) % count) for i in range(count)])  12.5 us
  transfers between devices with their start and end apart: 11, of which 6 were waited for; matrix products, arithmetic and copies ran while one was open for 1% of the time, Pallas kernels for 10%

profile of v3, /device:TPU:24, one launch (start us, length us, event | category | flops | bytes accessed | tf_op | source)
XLA Modules:
  0.0 110.6 jit_solution(10955150928455614612)
XLA Ops:
  0.7 2.5 %information_part.1 = (f32[128,256]{1,0:T(8,128)S(1)}, f32[128,256]{1,0:T(8,128)S(1)}, bf16[256,1024]{1,0:T(8,128)(2,1)S(1)}) custom-call(bf16[256,256]{1,0:T(8,128)(2,1)} %constant.4.clone.refs_0_, f32[1,1024]{1,0:T(1,128)} %bitcast.24, bf16[1024,256]{1,0:T(8,128)(2,1)} %refs_22_.1, bf16[256,1024]{1,0:T(8,128)(2,1)} %refs_3_.2), custom_call_target="tpu_custom_call" | custom-call | tf_op jit(solution)/shard_map/information_part/pallas_call | solution.py:93
  3.2 0.0 copy-start.1
  3.2 0.1 collective-permute-start
  3.3 1.3 %collective-permute-done = f32[128,256]{1,0:T(8,128)S(1)} collective-permute-done((f32[128,256]{1,0:T(8,128)S(1)}, f32[128,256]{1,0:T(8,128)S(1)}, u32[]{:S(2)}, u32[]{:S(2)}) %collective-permute-start) | collective-permute-done | bytes 131104 | tf_op jit(solution)/shard_map/ppermute | solution.py:504
  4.7 2.8 %collective-permute-start.3 = (f32[128,256]{1,0:T(8,128)S(1)}, f32[128,256]{1,0:T(8,128)S(1)}, u32[]{:S(2)}, u32[]{:S(2)}) collective-permute-start(f32[128,256]{1,0:T(8,128)S(1)} %add.12), channel_id=1, source_target_pairs={{0,6},{2,0},{4,2},{6,4},{1,7},{3,1},{5,3},{7,5},{8,14},{10,8},{12,... | collective-permute-start | bytes 393224 | tf_op jit(solution)/shard_map/ppermute | solution.py:504
  7.5 2.3 %collective-permute-start.1 = (f32[128,256]{1,0:T(8,128)S(1)}, f32[128,256]{1,0:T(8,128)S(1)}, u32[]{:S(2)}, u32[]{:S(2)}) collective-permute-start(f32[128,256]{1,0:T(8,128)S(1)} %add.12), channel_id=1, source_target_pairs={{0,4},{2,6},{4,0},{6,2},{1,5},{3,7},{5,1},{7,3},{8,12},{10,14},{12... | collective-permute-start | bytes 393224 | tf_op jit(solution)/shard_map/ppermute | solution.py:504
  9.8 7.0 %powers.1 = (bf16[5,256,256]{2,1,0:T(8,128)(2,1)S(1)}, bf16[5,256,256]{2,1,0:T(8,128)(2,1)S(1)}, bf16[8,256,256]{2,1,0:T(8,128)(2,1)S(1)}, bf16[8,256,256]{2,1,0...) custom-call(f32[256,256]{1,0:T(8,128)S(1)} %copy-done.1, ...), custom_call_target="tpu_custom_call" | custom-call | tf_op jit(solution)/shard_map/powers/pallas_call | solution.py:93
  16.9 0.3 collective-permute-start.4
  17.2 1.8 %last_effects.1 = (bf16[1,256,256]{2,1,0:T(8,128)(2,1)S(1)}, bf16[1,256,256]{2,1,0:T(8,128)(2,1)S(1)}, bf16[2,256,256]{2,1,0:T(8,128)(2,1)S(1)}, bf16[2,256,256]...) custom-call(bf16[8,256,256]{2,1,0:T(8,128)(2,1)S(1)} %get-tuple-element.92.refs_0_.refs_10_.refs_11_, ...), custom_call_target="tpu_custom_call" | custom-call | tf_op jit(solution)/shard_map/last_effects/pallas_call | solution.py:93
  19.0 0.0 copy-start
  19.0 4.0 %block_tree.1 = (f32[32,2,256]{2,1,0:T(2,128)S(1)}, f32[256,256]{1,0:T(8,128)S(1)}, f32[248,256]{1,0:T(8,128)S(1)}, f32[248,256]{1,0:T(8,128)S(1)}, f32[24,256]{1,0:T(8,128)S(1)}, /*index=5*/f32[24,256]{1,0:T(8,128)S(1)}) custom-call(f32[128,256]{1,0:T(8,128)S(1)} %add_add_fusion.refs_0_, f32[128,256]{1,0:T(8,128)S(1)} %collective-permute-done.4.refs_1_, ...), custom_call_target="tpu_custom_call" | custom-call | tf_op jit(solution)/shard_map/block_tree/pallas_call | solution.py:93
  23.0 19.4 %all_to_all.15.refs_0_ = f32[32,2,256]{2,1,0:T(2,128)S(1)} all-to-all(f32[32,2,256]{2,1,0:T(2,128)S(1)} %get-tuple-element.104), channel_id=1, replica_groups=mesh['y'=4,'z'=8,'x'=4,'core'=2] {'y','z'}, dimensions={0} | all-to-all | bytes 131072 | tf_op jit(solution)/shard_map/all_to_all | solution.py:583
  42.5 4.9 %states_and_sums.1 = (f32[256,256]{1,0:T(8,128)S(1)}, f32[8,40,256]{2,1,0:T(8,128)S(1)}, f32[8,40,256]{2,1,0:T(8,128)S(1)}, f32[8,40,256]{2,1,0:T(8,128)S(1)}, f32[8,40,256]{2,1,0:T(8,128)S(1)}) custom-call(f32[32,2,256]{2,1,0:T(2,128)S(1)} %all_to_all.15.refs_0_, bf16[5,256,256]{2,1,0:T(8,128)(2,1)S(1)} %get-tuple-element.105.refs_1_, ...), custom_call_target="tpu_custom_call" | custom-call | tf_op jit(solution)/shard_map/states_and_sums/pallas_call | solution.py:93
  47.4 2.2 %collective-permute-start.5 = (f32[320,256]{1,0:T(8,128)S(1)}, f32[320,256]{1,0:T(8,128)S(1)}, u32[]{:S(2)}, u32[]{:S(2)}) collective-permute-start(f32[320,256]{1,0:T(8,128)S(1)} %bitcast.23), channel_id=1, source_target_pairs={{0,64},{64,128},{128,192},{192,0},{1,65},{65,129},{129,193},{193,1... | collective-permute-start | bytes 983048 | tf_op jit(solution)/shard_map/ppermute | solution.py:504
  49.6 2.1 %collective-permute-start.7 = (f32[320,256]{1,0:T(8,128)S(1)}, f32[320,256]{1,0:T(8,128)S(1)}, u32[]{:S(2)}, u32[]{:S(2)}) collective-permute-start(f32[320,256]{1,0:T(8,128)S(1)} %bitcast.21), channel_id=1, source_target_pairs={{0,128},{64,192},{128,0},{192,64},{1,129},{65,193},{129,1},{193,65... | collective-permute-start | bytes 983048 | tf_op jit(solution)/shard_map/ppermute | solution.py:504
  51.7 11.2 %collective-permute-done.5 = f32[320,256]{1,0:T(8,128)S(1)} collective-permute-done((f32[320,256]{1,0:T(8,128)S(1)}, f32[320,256]{1,0:T(8,128)S(1)}, u32[]{:S(2)}, u32[]{:S(2)}) %collective-permute-start.5) | collective-permute-done | bytes 327712 | tf_op jit(solution)/shard_map/ppermute | solution.py:504
  62.8 3.4 %collective-permute-done.6 = f32[320,256]{1,0:T(8,128)S(1)} collective-permute-done((f32[320,256]{1,0:T(8,128)S(1)}, f32[320,256]{1,0:T(8,128)S(1)}, u32[]{:S(2)}, u32[]{:S(2)}) %collective-permute-start.6) | collective-permute-done | bytes 327712 | tf_op jit(solution)/shard_map/ppermute | solution.py:504
  66.2 0.6 add_chunks.1
  66.9 13.6 %all_to_all.16.refs_0_ = f32[8,40,256]{2,1,0:T(8,128)S(1)} all-to-all(f32[8,40,256]{2,1,0:T(8,128)S(1)} %add_chunks.1), channel_id=1, replica_groups=mesh['y'=4,'z'=8,'x'=4,'core'=2] {'z'}, dimensions={0} | all-to-all | bytes 655360 | tf_op jit(solution)/shard_map/all_to_all | solution.py:610
  80.4 0.6 add_pieces.1
  81.0 0.0 copy-start.5
  81.0 13.7 %all_to_all.17.refs_0_ = f32[8,40,256]{2,1,0:T(8,128)S(1)} all-to-all(f32[8,40,256]{2,1,0:T(8,128)S(1)} %add_pieces.1), channel_id=1, replica_groups=mesh['y'=4,'z'=8,'x'=4,'core'=2] {'z'}, dimensions={0} | all-to-all | bytes 655360 | tf_op jit(solution)/shard_map/all_to_all | solution.py:612
  94.7 0.5 collective-permute-start.10
  95.3 0.8 collective-permute-start.9
  96.1 1.4 %collective-permute-start.8 = (f32[320,256]{1,0:T(8,128)S(1)}, f32[320,256]{1,0:T(8,128)S(1)}, u32[]{:S(2)}, u32[]{:S(2)}) collective-permute-start(f32[320,256]{1,0:T(8,128)S(1)} %bitcast.14), channel_id=1, source_target_pairs={{0,192},{64,0},{128,64},{192,128},{1,193},{65,1},{129,65},{193,129... | collective-permute-start | bytes 983048 | tf_op jit(solution)/shard_map/ppermute | solution.py:504
  97.5 0.8 in_time_order.1
  98.4 0.7 copy.15
  99.1 3.6 %collective-permute-done.10 = f32[320,256]{1,0:T(8,128)S(1)} collective-permute-done((f32[320,256]{1,0:T(8,128)S(1)}, f32[320,256]{1,0:T(8,128)S(1)}, u32[]{:S(2)}, u32[]{:S(2)}) %collective-permute-start.10) | collective-permute-done | bytes 327712 | tf_op jit(solution)/shard_map/ppermute | solution.py:504
  102.7 1.4 %first_blocks.1 = (f32[1024,256]{1,0:T(8,128)}, f32[256,256]{1,0:T(8,128)S(1)}, f32[32,256]{1,0:T(8,128)S(1)}) custom-call(f32[8,40,256]{2,1,0:T(8,128)S(1)} %all_to_all.17.refs_0_, f32[8,40,256]{2,1,0:T(8,128)S(1)} %bitcast.15), custom_call_target="tpu_custom_call" | custom-call | tf_op jit(solution)/shard_map/first_blocks/pallas_call | solution.py:93
  104.1 1.3 %collective-permute-done.9 = f32[320,256]{1,0:T(8,128)S(1)} collective-permute-done((f32[320,256]{1,0:T(8,128)S(1)}, f32[320,256]{1,0:T(8,128)S(1)}, u32[]{:S(2)}, u32[]{:S(2)}) %collective-permute-start.9) | collective-permute-done | bytes 327712 | tf_op jit(solution)/shard_map/ppermute | solution.py:504
  105.4 3.4 %collective-permute-done.8 = f32[320,256]{1,0:T(8,128)S(1)} collective-permute-done((f32[320,256]{1,0:T(8,128)S(1)}, f32[320,256]{1,0:T(8,128)S(1)}, u32[]{:S(2)}, u32[]{:S(2)}) %collective-permute-start.8) | collective-permute-done | bytes 327712 | tf_op jit(solution)/shard_map/ppermute | solution.py:504
  108.8 1.6 %last_blocks.1 = (f32[1024,256]{1,0:T(8,128)}, f32[256,256]{1,0:T(8,128)}, f32[1,1024]{1,0:T(1,128)}) custom-call(f32[8,40,256]{2,1,0:T(8,128)S(1)} %bitcast.20, f32[8,40,256]{2,1,0:T(8,128)S(1)} %bitcast.19, f32[1024,256]{1,0:T(8,128)} %get-tuple-element.126.refs_2_, f32[256,256]{1,0:T(8,128)S(1)} %get-tuple-element.127.refs_3_, ...), custom_call_target="tpu_custom_call", output_to_operand_aliasing={{0}: (2, {})} | custom-call | tf_op jit(solution)/shard_map/last_blocks/pallas_call | solution.py:93
  (18 shorter events, 0.1 us)
Async XLA Ops:
  0.6 9.2 %copy-start.2 = (f32[256,256]{1,0:T(8,128)S(1)}, f32[256,256]{1,0:T(8,128)}, u32[]{:S(2)}) copy-start(f32[256,256]{1,0:T(8,128)} %refs_1_.1) | copy-start | bytes 786436
  0.6 9.2 %copy-start.3 = (f32[256,256]{1,0:T(8,128)S(1)}, f32[256,256]{1,0:T(8,128)}, u32[]{:S(2)}) copy-start(f32[256,256]{1,0:T(8,128)} %refs_2_.3) | copy-start | bytes 786436
  0.7 9.2 %copy-start.4 = (f32[256,256]{1,0:T(8,128)S(1)}, f32[256,256]{1,0:T(8,128)}, u32[]{:S(2)}) copy-start(f32[256,256]{1,0:T(8,128)} %refs_3_.3) | copy-start | bytes 786436
  3.2 6.6 %copy-start.1 = (f32[256,256]{1,0:T(8,128)S(1)}, f32[256,256]{1,0:T(8,128)}, u32[]{:S(2)}) copy-start(f32[256,256]{1,0:T(8,128)} %refs_0_.3) | copy-start | bytes 786436
  3.2 1.4 %collective-permute-start = (f32[128,256]{1,0:T(8,128)S(1)}, f32[128,256]{1,0:T(8,128)S(1)}, u32[]{:S(2)}, u32[]{:S(2)}) collective-permute-start(f32[128,256]{1,0:T(8,128)S(1)} %get-tuple-element.69), channel_id=1, source_target_pairs={{0,1},{1,0},{2,3},{3,2},{4,5},{5,4},{6,7},{7,6},{8,9},{9,8},{10,11... | collective-permute-start | bytes 393224 | tf_op jit(solution)/shard_map/ppermute | solution.py:504
  4.7 12.2 %collective-permute-start.3 = (f32[128,256]{1,0:T(8,128)S(1)}, f32[128,256]{1,0:T(8,128)S(1)}, u32[]{:S(2)}, u32[]{:S(2)}) collective-permute-start(f32[128,256]{1,0:T(8,128)S(1)} %add.12), channel_id=1, source_target_pairs={{0,6},{2,0},{4,2},{6,4},{1,7},{3,1},{5,3},{7,5},{8,14},{10,8},{12,... | collective-permute-start | bytes 393224 | tf_op jit(solution)/shard_map/ppermute | solution.py:504
  7.5 9.4 %collective-permute-start.2 = (f32[128,256]{1,0:T(8,128)S(1)}, f32[128,256]{1,0:T(8,128)S(1)}, u32[]{:S(2)}, u32[]{:S(2)}) collective-permute-start(f32[128,256]{1,0:T(8,128)S(1)} %add.12), channel_id=1, source_target_pairs={{0,2},{2,4},{4,6},{6,0},{1,3},{3,5},{5,7},{7,1},{8,10},{10,12},{12... | collective-permute-start | bytes 393224 | tf_op jit(solution)/shard_map/ppermute | solution.py:504
  7.5 9.4 %collective-permute-start.1 = (f32[128,256]{1,0:T(8,128)S(1)}, f32[128,256]{1,0:T(8,128)S(1)}, u32[]{:S(2)}, u32[]{:S(2)}) collective-permute-start(f32[128,256]{1,0:T(8,128)S(1)} %add.12), channel_id=1, source_target_pairs={{0,4},{2,6},{4,0},{6,2},{1,5},{3,7},{5,1},{7,3},{8,12},{10,14},{12... | collective-permute-start | bytes 393224 | tf_op jit(solution)/shard_map/ppermute | solution.py:504
  16.9 2.1 %collective-permute-start.4 = (f32[128,256]{1,0:T(8,128)S(1)}, f32[128,256]{1,0:T(8,128)S(1)}, u32[]{:S(2)}, u32[]{:S(2)}) collective-permute-start(f32[128,256]{1,0:T(8,128)S(1)} %add_add_fusion.refs_0_), channel_id=1, source_target_pairs={{0,1},{1,0},{2,3},{3,2},{4,5},{5,4},{6,7},{7,6},{8,9},{9,8},{10,11... | collective-permute-start | bytes 393224 | tf_op jit(solution)/shard_map/ppermute | solution.py:504
  19.0 23.5 %copy-start = (bf16[1024,256]{1,0:T(8,128)(2,1)S(1)}, bf16[1024,256]{1,0:T(8,128)(2,1)}, u32[]{:S(2)}) copy-start(bf16[1024,256]{1,0:T(8,128)(2,1)} %refs_22_.1) | copy-start | bytes 1572868
  47.4 15.4 %collective-permute-start.5 = (f32[320,256]{1,0:T(8,128)S(1)}, f32[320,256]{1,0:T(8,128)S(1)}, u32[]{:S(2)}, u32[]{:S(2)}) collective-permute-start(f32[320,256]{1,0:T(8,128)S(1)} %bitcast.23), channel_id=1, source_target_pairs={{0,64},{64,128},{128,192},{192,0},{1,65},{65,129},{129,193},{193,1... | collective-permute-start | bytes 983048 | tf_op jit(solution)/shard_map/ppermute | solution.py:504
  49.6 16.6 %collective-permute-start.6 = (f32[320,256]{1,0:T(8,128)S(1)}, f32[320,256]{1,0:T(8,128)S(1)}, u32[]{:S(2)}, u32[]{:S(2)}) collective-permute-start(f32[320,256]{1,0:T(8,128)S(1)} %bitcast.22), channel_id=1, source_target_pairs={{0,192},{64,0},{128,64},{192,128},{1,193},{65,1},{129,65},{193,129... | collective-permute-start | bytes 983048 | tf_op jit(solution)/shard_map/ppermute | solution.py:504
  49.6 16.6 %collective-permute-start.7 = (f32[320,256]{1,0:T(8,128)S(1)}, f32[320,256]{1,0:T(8,128)S(1)}, u32[]{:S(2)}, u32[]{:S(2)}) collective-permute-start(f32[320,256]{1,0:T(8,128)S(1)} %bitcast.21), channel_id=1, source_target_pairs={{0,128},{64,192},{128,0},{192,64},{1,129},{65,193},{129,1},{193,65... | collective-permute-start | bytes 983048 | tf_op jit(solution)/shard_map/ppermute | solution.py:504
  81.0 16.5 %copy-start.5 = (bf16[256,256]{1,0:T(8,128)(2,1)S(1)}, bf16[256,256]{1,0:T(8,128)(2,1)}, u32[]{:S(2)}) copy-start(bf16[256,256]{1,0:T(8,128)(2,1)} %constant.5.clone.refs_0_) | copy-start | bytes 393220
  94.7 7.9 %collective-permute-start.10 = (f32[320,256]{1,0:T(8,128)S(1)}, f32[320,256]{1,0:T(8,128)S(1)}, u32[]{:S(2)}, u32[]{:S(2)}) collective-permute-start(f32[320,256]{1,0:T(8,128)S(1)} %bitcast.12), channel_id=1, source_target_pairs={{0,64},{64,128},{128,192},{192,0},{1,65},{65,129},{129,193},{193,1... | collective-permute-start | bytes 983048 | tf_op jit(solution)/shard_map/ppermute | solution.py:504
  95.3 10.1 %collective-permute-start.9 = (f32[320,256]{1,0:T(8,128)S(1)}, f32[320,256]{1,0:T(8,128)S(1)}, u32[]{:S(2)}, u32[]{:S(2)}) collective-permute-start(f32[320,256]{1,0:T(8,128)S(1)} %bitcast.13), channel_id=1, source_target_pairs={{0,128},{64,192},{128,0},{192,64},{1,129},{65,193},{129,1},{193,65... | collective-permute-start | bytes 983048 | tf_op jit(solution)/shard_map/ppermute | solution.py:504
  96.1 12.7 %collective-permute-start.8 = (f32[320,256]{1,0:T(8,128)S(1)}, f32[320,256]{1,0:T(8,128)S(1)}, u32[]{:S(2)}, u32[]{:S(2)}) collective-permute-start(f32[320,256]{1,0:T(8,128)S(1)} %bitcast.14), channel_id=1, source_target_pairs={{0,192},{64,0},{128,64},{192,128},{1,193},{65,1},{129,65},{193,129... | collective-permute-start | bytes 983048 | tf_op jit(solution)/shard_map/ppermute | solution.py:504

commit v4 on v3

--- a/solution.py
+++ b/solution.py
@@ -478,7 +478,7 @@
     yield from blocks_of(bins, [(0, own[...]), (1, near[...])])
 
 
-def last_blocks(bins, back, far, cross, moments, errors):
+def last_blocks(bins, far, back, cross, moments, errors):
     moment, error = moments[...], errors[...]
     for i, (start, size), value in blocks_of(bins, [(3, back[...]), (2, far[...])]):
         if i == 0:
@@ -619,8 +619,8 @@
     cross, moment, error = call(
         named(last_blocks),
         kinds + [((1, channels), F32)],
+        far,
         back,
-        far,
         cross,
         moment,
         error,

time: 111 us -> 111 us (level)
  transfers between devices with their start and end apart: 11 -> 11, of which waited for: 6 -> 5; matrix products, arithmetic and copies ran while one was open for 1% -> 1% of each run, Pallas kernels for 10% -> 10%
where the time goes in v4:
time: 111 us; the launch traced here: 110 us
  blocking collectives  46.7 us (42%)
  Pallas kernels  25.4 us (23%)
  waiting for transfers between devices  23.4 us (21%)
  starting transfers between devices  13.1 us (12%)
    pallas_call x10, Pallas kernels, call(): pl.pallas_call(kernel, out_shape=[(pltpu.HBM if i in sent else pltpu.VMEM...  25.4 us
    ppermute x11, waiting for transfers between devices, shift(): lax.ppermute(value, axis, [(i, (i + by) % count) for i in range(count)])  23.4 us
    all_to_all x1, blocking collectives, local(): gathered = lax.all_to_all(ends, ('y', 'z'), 0, 0)  19.4 us
    all_to_all x1, blocking collectives, local(): whole = lax.all_to_all(spread, 'z', 0, 0)  13.7 us
    all_to_all x1, blocking collectives, local(): payload = lax.all_to_all(payload, 'z', 0, 0)  13.6 us
    ppermute x11, starting transfers between devices, shift(): lax.ppermute(value, axis, [(i, (i + by) % count) for i in range(count)])  13.1 us
  transfers between devices with their start and end apart: 11, of which 5 were waited for; matrix products, arithmetic and copies ran while one was open for 1% of the time, Pallas kernels for 10%

profile of v4, /device:TPU:24, one launch (start us, length us, event | category | flops | bytes accessed | tf_op | source)
XLA Modules:
  0.0 110.4 jit_solution(441009801025194058)
XLA Ops:
  0.7 2.5 %information_part.1 = (f32[128,256]{1,0:T(8,128)S(1)}, f32[128,256]{1,0:T(8,128)S(1)}, bf16[256,1024]{1,0:T(8,128)(2,1)S(1)}) custom-call(bf16[256,256]{1,0:T(8,128)(2,1)} %constant.4.clone.refs_0_, f32[1,1024]{1,0:T(1,128)} %bitcast.24, bf16[1024,256]{1,0:T(8,128)(2,1)} %refs_22_.1, bf16[256,1024]{1,0:T(8,128)(2,1)} %refs_3_.2), custom_call_target="tpu_custom_call" | custom-call | tf_op jit(solution)/shard_map/information_part/pallas_call | solution.py:93
  3.2 0.0 copy-start.1
  3.2 0.1 collective-permute-start
  3.3 1.3 %collective-permute-done = f32[128,256]{1,0:T(8,128)S(1)} collective-permute-done((f32[128,256]{1,0:T(8,128)S(1)}, f32[128,256]{1,0:T(8,128)S(1)}, u32[]{:S(2)}, u32[]{:S(2)}) %collective-permute-start) | collective-permute-done | bytes 131104 | tf_op jit(solution)/shard_map/ppermute | solution.py:504
  4.7 2.8 %collective-permute-start.3 = (f32[128,256]{1,0:T(8,128)S(1)}, f32[128,256]{1,0:T(8,128)S(1)}, u32[]{:S(2)}, u32[]{:S(2)}) collective-permute-start(f32[128,256]{1,0:T(8,128)S(1)} %add.12), channel_id=1, source_target_pairs={{0,6},{2,0},{4,2},{6,4},{1,7},{3,1},{5,3},{7,5},{8,14},{10,8},{12,... | collective-permute-start | bytes 393224 | tf_op jit(solution)/shard_map/ppermute | solution.py:504
  7.5 0.0 collective-permute-start.2
  7.5 2.3 %collective-permute-start.1 = (f32[128,256]{1,0:T(8,128)S(1)}, f32[128,256]{1,0:T(8,128)S(1)}, u32[]{:S(2)}, u32[]{:S(2)}) collective-permute-start(f32[128,256]{1,0:T(8,128)S(1)} %add.12), channel_id=1, source_target_pairs={{0,4},{2,6},{4,0},{6,2},{1,5},{3,7},{5,1},{7,3},{8,12},{10,14},{12... | collective-permute-start | bytes 393224 | tf_op jit(solution)/shard_map/ppermute | solution.py:504
  9.8 7.0 %powers.1 = (bf16[5,256,256]{2,1,0:T(8,128)(2,1)S(1)}, bf16[5,256,256]{2,1,0:T(8,128)(2,1)S(1)}, bf16[8,256,256]{2,1,0:T(8,128)(2,1)S(1)}, bf16[8,256,256]{2,1,0...) custom-call(f32[256,256]{1,0:T(8,128)S(1)} %copy-done.1, ...), custom_call_target="tpu_custom_call" | custom-call | tf_op jit(solution)/shard_map/powers/pallas_call | solution.py:93
  16.9 0.3 collective-permute-start.4
  17.2 1.8 %last_effects.1 = (bf16[1,256,256]{2,1,0:T(8,128)(2,1)S(1)}, bf16[1,256,256]{2,1,0:T(8,128)(2,1)S(1)}, bf16[2,256,256]{2,1,0:T(8,128)(2,1)S(1)}, bf16[2,256,256]...) custom-call(bf16[8,256,256]{2,1,0:T(8,128)(2,1)S(1)} %get-tuple-element.92.refs_0_.refs_10_.refs_11_, ...), custom_call_target="tpu_custom_call" | custom-call | tf_op jit(solution)/shard_map/last_effects/pallas_call | solution.py:93
  19.0 0.0 copy-start
  19.0 4.0 %block_tree.1 = (f32[32,2,256]{2,1,0:T(2,128)S(1)}, f32[256,256]{1,0:T(8,128)S(1)}, f32[248,256]{1,0:T(8,128)S(1)}, f32[248,256]{1,0:T(8,128)S(1)}, f32[24,256]{1,0:T(8,128)S(1)}, /*index=5*/f32[24,256]{1,0:T(8,128)S(1)}) custom-call(f32[128,256]{1,0:T(8,128)S(1)} %add_add_fusion.refs_0_, f32[128,256]{1,0:T(8,128)S(1)} %collective-permute-done.4.refs_1_, ...), custom_call_target="tpu_custom_call" | custom-call | tf_op jit(solution)/shard_map/block_tree/pallas_call | solution.py:93
  23.0 19.4 %all_to_all.15.refs_0_ = f32[32,2,256]{2,1,0:T(2,128)S(1)} all-to-all(f32[32,2,256]{2,1,0:T(2,128)S(1)} %get-tuple-element.104), channel_id=1, replica_groups=mesh['y'=4,'z'=8,'x'=4,'core'=2] {'y','z'}, dimensions={0} | all-to-all | bytes 131072 | tf_op jit(solution)/shard_map/all_to_all | solution.py:583
  42.5 4.9 %states_and_sums.1 = (f32[256,256]{1,0:T(8,128)S(1)}, f32[8,40,256]{2,1,0:T(8,128)S(1)}, f32[8,40,256]{2,1,0:T(8,128)S(1)}, f32[8,40,256]{2,1,0:T(8,128)S(1)}, f32[8,40,256]{2,1,0:T(8,128)S(1)}) custom-call(f32[32,2,256]{2,1,0:T(2,128)S(1)} %all_to_all.15.refs_0_, bf16[5,256,256]{2,1,0:T(8,128)(2,1)S(1)} %get-tuple-element.105.refs_1_, ...), custom_call_target="tpu_custom_call" | custom-call | tf_op jit(solution)/shard_map/states_and_sums/pallas_call | solution.py:93
  47.4 2.2 %collective-permute-start.5 = (f32[320,256]{1,0:T(8,128)S(1)}, f32[320,256]{1,0:T(8,128)S(1)}, u32[]{:S(2)}, u32[]{:S(2)}) collective-permute-start(f32[320,256]{1,0:T(8,128)S(1)} %bitcast.23), channel_id=1, source_target_pairs={{0,64},{64,128},{128,192},{192,0},{1,65},{65,129},{129,193},{193,1... | collective-permute-start | bytes 983048 | tf_op jit(solution)/shard_map/ppermute | solution.py:504
  49.6 2.1 %collective-permute-start.7 = (f32[320,256]{1,0:T(8,128)S(1)}, f32[320,256]{1,0:T(8,128)S(1)}, u32[]{:S(2)}, u32[]{:S(2)}) collective-permute-start(f32[320,256]{1,0:T(8,128)S(1)} %bitcast.21), channel_id=1, source_target_pairs={{0,128},{64,192},{128,0},{192,64},{1,129},{65,193},{129,1},{193,65... | collective-permute-start | bytes 983048 | tf_op jit(solution)/shard_map/ppermute | solution.py:504
  51.7 11.2 %collective-permute-done.5 = f32[320,256]{1,0:T(8,128)S(1)} collective-permute-done((f32[320,256]{1,0:T(8,128)S(1)}, f32[320,256]{1,0:T(8,128)S(1)}, u32[]{:S(2)}, u32[]{:S(2)}) %collective-permute-start.5) | collective-permute-done | bytes 327712 | tf_op jit(solution)/shard_map/ppermute | solution.py:504
  62.8 3.4 %collective-permute-done.6 = f32[320,256]{1,0:T(8,128)S(1)} collective-permute-done((f32[320,256]{1,0:T(8,128)S(1)}, f32[320,256]{1,0:T(8,128)S(1)}, u32[]{:S(2)}, u32[]{:S(2)}) %collective-permute-start.6) | collective-permute-done | bytes 327712 | tf_op jit(solution)/shard_map/ppermute | solution.py:504
  66.2 0.6 add_chunks.1
  66.9 13.6 %all_to_all.16.refs_0_ = f32[8,40,256]{2,1,0:T(8,128)S(1)} all-to-all(f32[8,40,256]{2,1,0:T(8,128)S(1)} %add_chunks.1), channel_id=1, replica_groups=mesh['y'=4,'z'=8,'x'=4,'core'=2] {'z'}, dimensions={0} | all-to-all | bytes 655360 | tf_op jit(solution)/shard_map/all_to_all | solution.py:610
  80.4 0.6 add_pieces.1
  81.0 0.0 copy-start.5
  81.0 13.7 %all_to_all.17.refs_0_ = f32[8,40,256]{2,1,0:T(8,128)S(1)} all-to-all(f32[8,40,256]{2,1,0:T(8,128)S(1)} %add_pieces.1), channel_id=1, replica_groups=mesh['y'=4,'z'=8,'x'=4,'core'=2] {'z'}, dimensions={0} | all-to-all | bytes 655360 | tf_op jit(solution)/shard_map/all_to_all | solution.py:612
  94.7 0.5 collective-permute-start.10
  95.3 1.5 %collective-permute-start.9 = (f32[320,256]{1,0:T(8,128)S(1)}, f32[320,256]{1,0:T(8,128)S(1)}, u32[]{:S(2)}, u32[]{:S(2)}) collective-permute-start(f32[320,256]{1,0:T(8,128)S(1)} %bitcast.13), channel_id=1, source_target_pairs={{0,192},{64,0},{128,64},{192,128},{1,193},{65,1},{129,65},{193,129... | collective-permute-start | bytes 983048 | tf_op jit(solution)/shard_map/ppermute | solution.py:504
  96.8 1.4 %collective-permute-start.8 = (f32[320,256]{1,0:T(8,128)S(1)}, f32[320,256]{1,0:T(8,128)S(1)}, u32[]{:S(2)}, u32[]{:S(2)}) collective-permute-start(f32[320,256]{1,0:T(8,128)S(1)} %bitcast.14), channel_id=1, source_target_pairs={{0,128},{64,192},{128,0},{192,64},{1,129},{65,193},{129,1},{193,65... | collective-permute-start | bytes 983048 | tf_op jit(solution)/shard_map/ppermute | solution.py:504
  98.1 0.8 in_time_order.1
  99.0 0.7 copy.15
  99.7 3.0 %collective-permute-done.10 = f32[320,256]{1,0:T(8,128)S(1)} collective-permute-done((f32[320,256]{1,0:T(8,128)S(1)}, f32[320,256]{1,0:T(8,128)S(1)}, u32[]{:S(2)}, u32[]{:S(2)}) %collective-permute-start.10) | collective-permute-done | bytes 327712 | tf_op jit(solution)/shard_map/ppermute | solution.py:504
  102.7 1.4 %first_blocks.1 = (f32[1024,256]{1,0:T(8,128)}, f32[256,256]{1,0:T(8,128)S(1)}, f32[32,256]{1,0:T(8,128)S(1)}) custom-call(f32[8,40,256]{2,1,0:T(8,128)S(1)} %all_to_all.17.refs_0_, f32[8,40,256]{2,1,0:T(8,128)S(1)} %bitcast.15), custom_call_target="tpu_custom_call" | custom-call | tf_op jit(solution)/shard_map/first_blocks/pallas_call | solution.py:93
  104.1 4.5 %collective-permute-done.9 = f32[320,256]{1,0:T(8,128)S(1)} collective-permute-done((f32[320,256]{1,0:T(8,128)S(1)}, f32[320,256]{1,0:T(8,128)S(1)}, u32[]{:S(2)}, u32[]{:S(2)}) %collective-permute-start.9) | collective-permute-done | bytes 327712 | tf_op jit(solution)/shard_map/ppermute | solution.py:504
  108.6 1.6 %last_blocks.1 = (f32[1024,256]{1,0:T(8,128)}, f32[256,256]{1,0:T(8,128)}, f32[1,1024]{1,0:T(1,128)}) custom-call(f32[8,40,256]{2,1,0:T(8,128)S(1)} %bitcast.20, f32[8,40,256]{2,1,0:T(8,128)S(1)} %bitcast.19, f32[1024,256]{1,0:T(8,128)} %get-tuple-element.126.refs_2_, f32[256,256]{1,0:T(8,128)S(1)} %get-tuple-element.127.refs_3_, ...), custom_call_target="tpu_custom_call", output_to_operand_aliasing={{0}: (2, {})} | custom-call | tf_op jit(solution)/shard_map/last_blocks/pallas_call | solution.py:93
  (18 shorter events, 0.1 us)
Async XLA Ops:
  0.6 9.2 %copy-start.2 = (f32[256,256]{1,0:T(8,128)S(1)}, f32[256,256]{1,0:T(8,128)}, u32[]{:S(2)}) copy-start(f32[256,256]{1,0:T(8,128)} %refs_1_.1) | copy-start | bytes 786436
  0.6 9.2 %copy-start.3 = (f32[256,256]{1,0:T(8,128)S(1)}, f32[256,256]{1,0:T(8,128)}, u32[]{:S(2)}) copy-start(f32[256,256]{1,0:T(8,128)} %refs_2_.3) | copy-start | bytes 786436
  0.7 9.2 %copy-start.4 = (f32[256,256]{1,0:T(8,128)S(1)}, f32[256,256]{1,0:T(8,128)}, u32[]{:S(2)}) copy-start(f32[256,256]{1,0:T(8,128)} %refs_3_.3) | copy-start | bytes 786436
  3.2 6.6 %copy-start.1 = (f32[256,256]{1,0:T(8,128)S(1)}, f32[256,256]{1,0:T(8,128)}, u32[]{:S(2)}) copy-start(f32[256,256]{1,0:T(8,128)} %refs_0_.3) | copy-start | bytes 786436
  3.2 1.4 %collective-permute-start = (f32[128,256]{1,0:T(8,128)S(1)}, f32[128,256]{1,0:T(8,128)S(1)}, u32[]{:S(2)}, u32[]{:S(2)}) collective-permute-start(f32[128,256]{1,0:T(8,128)S(1)} %get-tuple-element.69), channel_id=1, source_target_pairs={{0,1},{1,0},{2,3},{3,2},{4,5},{5,4},{6,7},{7,6},{8,9},{9,8},{10,11... | collective-permute-start | bytes 393224 | tf_op jit(solution)/shard_map/ppermute | solution.py:504
  4.7 12.2 %collective-permute-start.3 = (f32[128,256]{1,0:T(8,128)S(1)}, f32[128,256]{1,0:T(8,128)S(1)}, u32[]{:S(2)}, u32[]{:S(2)}) collective-permute-start(f32[128,256]{1,0:T(8,128)S(1)} %add.12), channel_id=1, source_target_pairs={{0,6},{2,0},{4,2},{6,4},{1,7},{3,1},{5,3},{7,5},{8,14},{10,8},{12,... | collective-permute-start | bytes 393224 | tf_op jit(solution)/shard_map/ppermute | solution.py:504
  7.5 9.4 %collective-permute-start.2 = (f32[128,256]{1,0:T(8,128)S(1)}, f32[128,256]{1,0:T(8,128)S(1)}, u32[]{:S(2)}, u32[]{:S(2)}) collective-permute-start(f32[128,256]{1,0:T(8,128)S(1)} %add.12), channel_id=1, source_target_pairs={{0,2},{2,4},{4,6},{6,0},{1,3},{3,5},{5,7},{7,1},{8,10},{10,12},{12... | collective-permute-start | bytes 393224 | tf_op jit(solution)/shard_map/ppermute | solution.py:504
  7.5 9.4 %collective-permute-start.1 = (f32[128,256]{1,0:T(8,128)S(1)}, f32[128,256]{1,0:T(8,128)S(1)}, u32[]{:S(2)}, u32[]{:S(2)}) collective-permute-start(f32[128,256]{1,0:T(8,128)S(1)} %add.12), channel_id=1, source_target_pairs={{0,4},{2,6},{4,0},{6,2},{1,5},{3,7},{5,1},{7,3},{8,12},{10,14},{12... | collective-permute-start | bytes 393224 | tf_op jit(solution)/shard_map/ppermute | solution.py:504
  16.9 2.1 %collective-permute-start.4 = (f32[128,256]{1,0:T(8,128)S(1)}, f32[128,256]{1,0:T(8,128)S(1)}, u32[]{:S(2)}, u32[]{:S(2)}) collective-permute-start(f32[128,256]{1,0:T(8,128)S(1)} %add_add_fusion.refs_0_), channel_id=1, source_target_pairs={{0,1},{1,0},{2,3},{3,2},{4,5},{5,4},{6,7},{7,6},{8,9},{9,8},{10,11... | collective-permute-start | bytes 393224 | tf_op jit(solution)/shard_map/ppermute | solution.py:504
  19.0 23.5 %copy-start = (bf16[1024,256]{1,0:T(8,128)(2,1)S(1)}, bf16[1024,256]{1,0:T(8,128)(2,1)}, u32[]{:S(2)}) copy-start(bf16[1024,256]{1,0:T(8,128)(2,1)} %refs_22_.1) | copy-start | bytes 1572868
  47.4 15.4 %collective-permute-start.5 = (f32[320,256]{1,0:T(8,128)S(1)}, f32[320,256]{1,0:T(8,128)S(1)}, u32[]{:S(2)}, u32[]{:S(2)}) collective-permute-start(f32[320,256]{1,0:T(8,128)S(1)} %bitcast.23), channel_id=1, source_target_pairs={{0,64},{64,128},{128,192},{192,0},{1,65},{65,129},{129,193},{193,1... | collective-permute-start | bytes 983048 | tf_op jit(solution)/shard_map/ppermute | solution.py:504
  49.6 16.6 %collective-permute-start.6 = (f32[320,256]{1,0:T(8,128)S(1)}, f32[320,256]{1,0:T(8,128)S(1)}, u32[]{:S(2)}, u32[]{:S(2)}) collective-permute-start(f32[320,256]{1,0:T(8,128)S(1)} %bitcast.22), channel_id=1, source_target_pairs={{0,192},{64,0},{128,64},{192,128},{1,193},{65,1},{129,65},{193,129... | collective-permute-start | bytes 983048 | tf_op jit(solution)/shard_map/ppermute | solution.py:504
  49.6 16.6 %collective-permute-start.7 = (f32[320,256]{1,0:T(8,128)S(1)}, f32[320,256]{1,0:T(8,128)S(1)}, u32[]{:S(2)}, u32[]{:S(2)}) collective-permute-start(f32[320,256]{1,0:T(8,128)S(1)} %bitcast.21), channel_id=1, source_target_pairs={{0,128},{64,192},{128,0},{192,64},{1,129},{65,193},{129,1},{193,65... | collective-permute-start | bytes 983048 | tf_op jit(solution)/shard_map/ppermute | solution.py:504
  81.0 17.1 %copy-start.5 = (bf16[256,256]{1,0:T(8,128)(2,1)S(1)}, bf16[256,256]{1,0:T(8,128)(2,1)}, u32[]{:S(2)}) copy-start(bf16[256,256]{1,0:T(8,128)(2,1)} %constant.5.clone.refs_0_) | copy-start | bytes 393220
  94.7 7.9 %collective-permute-start.10 = (f32[320,256]{1,0:T(8,128)S(1)}, f32[320,256]{1,0:T(8,128)S(1)}, u32[]{:S(2)}, u32[]{:S(2)}) collective-permute-start(f32[320,256]{1,0:T(8,128)S(1)} %bitcast.12), channel_id=1, source_target_pairs={{0,64},{64,128},{128,192},{192,0},{1,65},{65,129},{129,193},{193,1... | collective-permute-start | bytes 983048 | tf_op jit(solution)/shard_map/ppermute | solution.py:504
  95.3 13.3 %collective-permute-start.9 = (f32[320,256]{1,0:T(8,128)S(1)}, f32[320,256]{1,0:T(8,128)S(1)}, u32[]{:S(2)}, u32[]{:S(2)}) collective-permute-start(f32[320,256]{1,0:T(8,128)S(1)} %bitcast.13), channel_id=1, source_target_pairs={{0,192},{64,0},{128,64},{192,128},{1,193},{65,1},{129,65},{193,129... | collective-permute-start | bytes 983048 | tf_op jit(solution)/shard_map/ppermute | solution.py:504
  96.8 11.8 %collective-permute-start.8 = (f32[320,256]{1,0:T(8,128)S(1)}, f32[320,256]{1,0:T(8,128)S(1)}, u32[]{:S(2)}, u32[]{:S(2)}) collective-permute-start(f32[320,256]{1,0:T(8,128)S(1)} %bitcast.14), channel_id=1, source_target_pairs={{0,128},{64,192},{128,0},{192,64},{1,129},{65,193},{129,1},{193,65... | collective-permute-start | bytes 983048 | tf_op jit(solution)/shard_map/ppermute | solution.py:504

commit v5 on v4

--- a/solution.py
+++ b/solution.py
@@ -463,7 +463,9 @@
         free = share * jnp.where(place == N_Y - 1, 0, place + 1)
         error = jnp.zeros((8, width), F32)
         for z in range(N_Z):
-            turned = roll_lanes(moment[8 * z : 8 * z + 8], width + line * z - free)
+            by = line * z - free
+            by = jnp.where(by < 0, by + width, by)
+            turned = roll_lanes(moment[8 * z : 8 * z + 8], by)
             error = jnp.where((lane >= line * z) & (lane < line * z + line), turned, error)
         yield 0, (tiled(place * cross.shape[0]), cross.shape[0]), cross
         yield 1, (tiled(place * share), share), moment

time: 111 us -> 111 us (level)
  no operation moved by 1% of the time
where the time goes in v5:
time: 111 us; the launch traced here: 110 us
  blocking collectives  46.7 us (42%)
  Pallas kernels  25.4 us (23%)
  waiting for transfers between devices  23.4 us (21%)
  starting transfers between devices  13.1 us (12%)
    pallas_call x10, Pallas kernels, call(): pl.pallas_call(kernel, out_shape=[(pltpu.HBM if i in sent else pltpu.VMEM...  25.4 us
    ppermute x11, waiting for transfers between devices, shift(): lax.ppermute(value, axis, [(i, (i + by) % count) for i in range(count)])  23.4 us
    all_to_all x1, blocking collectives, local(): gathered = lax.all_to_all(ends, ('y', 'z'), 0, 0)  19.4 us
    all_to_all x1, blocking collectives, local(): whole = lax.all_to_all(spread, 'z', 0, 0)  13.7 us
    all_to_all x1, blocking collectives, local(): payload = lax.all_to_all(payload, 'z', 0, 0)  13.6 us
    ppermute x11, starting transfers between devices, shift(): lax.ppermute(value, axis, [(i, (i + by) % count) for i in range(count)])  13.1 us
  transfers between devices with their start and end apart: 11, of which 5 were waited for; matrix products, arithmetic and copies ran while one was open for 1% of the time, Pallas kernels for 10%

profile of v5, /device:TPU:24, one launch (start us, length us, event | category | flops | bytes accessed | tf_op | source)
XLA Modules:
  0.0 110.4 jit_solution(14391835329220358219)
XLA Ops:
  0.7 2.5 %information_part.1 = (f32[128,256]{1,0:T(8,128)S(1)}, f32[128,256]{1,0:T(8,128)S(1)}, bf16[256,1024]{1,0:T(8,128)(2,1)S(1)}) custom-call(bf16[256,256]{1,0:T(8,128)(2,1)} %constant.4.clone.refs_0_, f32[1,1024]{1,0:T(1,128)} %bitcast.24, bf16[1024,256]{1,0:T(8,128)(2,1)} %refs_22_.1, bf16[256,1024]{1,0:T(8,128)(2,1)} %refs_3_.2), custom_call_target="tpu_custom_call" | custom-call | tf_op jit(solution)/shard_map/information_part/pallas_call | solution.py:93
  3.2 0.0 copy-start.1
  3.2 0.1 collective-permute-start
  3.3 1.3 %collective-permute-done = f32[128,256]{1,0:T(8,128)S(1)} collective-permute-done((f32[128,256]{1,0:T(8,128)S(1)}, f32[128,256]{1,0:T(8,128)S(1)}, u32[]{:S(2)}, u32[]{:S(2)}) %collective-permute-start) | collective-permute-done | bytes 131104 | tf_op jit(solution)/shard_map/ppermute | solution.py:506
  4.7 2.8 %collective-permute-start.3 = (f32[128,256]{1,0:T(8,128)S(1)}, f32[128,256]{1,0:T(8,128)S(1)}, u32[]{:S(2)}, u32[]{:S(2)}) collective-permute-start(f32[128,256]{1,0:T(8,128)S(1)} %add.12), channel_id=1, source_target_pairs={{0,6},{2,0},{4,2},{6,4},{1,7},{3,1},{5,3},{7,5},{8,14},{10,8},{12,... | collective-permute-start | bytes 393224 | tf_op jit(solution)/shard_map/ppermute | solution.py:506
  7.5 0.0 collective-permute-start.2
  7.5 2.3 %collective-permute-start.1 = (f32[128,256]{1,0:T(8,128)S(1)}, f32[128,256]{1,0:T(8,128)S(1)}, u32[]{:S(2)}, u32[]{:S(2)}) collective-permute-start(f32[128,256]{1,0:T(8,128)S(1)} %add.12), channel_id=1, source_target_pairs={{0,4},{2,6},{4,0},{6,2},{1,5},{3,7},{5,1},{7,3},{8,12},{10,14},{12... | collective-permute-start | bytes 393224 | tf_op jit(solution)/shard_map/ppermute | solution.py:506
  9.8 7.0 %powers.1 = (bf16[5,256,256]{2,1,0:T(8,128)(2,1)S(1)}, bf16[5,256,256]{2,1,0:T(8,128)(2,1)S(1)}, bf16[8,256,256]{2,1,0:T(8,128)(2,1)S(1)}, bf16[8,256,256]{2,1,0...) custom-call(f32[256,256]{1,0:T(8,128)S(1)} %copy-done.1, ...), custom_call_target="tpu_custom_call" | custom-call | tf_op jit(solution)/shard_map/powers/pallas_call | solution.py:93
  16.9 0.3 collective-permute-start.4
  17.2 1.8 %last_effects.1 = (bf16[1,256,256]{2,1,0:T(8,128)(2,1)S(1)}, bf16[1,256,256]{2,1,0:T(8,128)(2,1)S(1)}, bf16[2,256,256]{2,1,0:T(8,128)(2,1)S(1)}, bf16[2,256,256]...) custom-call(bf16[8,256,256]{2,1,0:T(8,128)(2,1)S(1)} %get-tuple-element.92.refs_0_.refs_10_.refs_11_, ...), custom_call_target="tpu_custom_call" | custom-call | tf_op jit(solution)/shard_map/last_effects/pallas_call | solution.py:93
  19.0 0.0 copy-start
  19.0 4.0 %block_tree.1 = (f32[32,2,256]{2,1,0:T(2,128)S(1)}, f32[256,256]{1,0:T(8,128)S(1)}, f32[248,256]{1,0:T(8,128)S(1)}, f32[248,256]{1,0:T(8,128)S(1)}, f32[24,256]{1,0:T(8,128)S(1)}, /*index=5*/f32[24,256]{1,0:T(8,128)S(1)}) custom-call(f32[128,256]{1,0:T(8,128)S(1)} %add_add_fusion.refs_0_, f32[128,256]{1,0:T(8,128)S(1)} %collective-permute-done.4.refs_1_, ...), custom_call_target="tpu_custom_call" | custom-call | tf_op jit(solution)/shard_map/block_tree/pallas_call | solution.py:93
  23.0 19.4 %all_to_all.15.refs_0_ = f32[32,2,256]{2,1,0:T(2,128)S(1)} all-to-all(f32[32,2,256]{2,1,0:T(2,128)S(1)} %get-tuple-element.104), channel_id=1, replica_groups=mesh['y'=4,'z'=8,'x'=4,'core'=2] {'y','z'}, dimensions={0} | all-to-all | bytes 131072 | tf_op jit(solution)/shard_map/all_to_all | solution.py:585
  42.5 4.9 %states_and_sums.1 = (f32[256,256]{1,0:T(8,128)S(1)}, f32[8,40,256]{2,1,0:T(8,128)S(1)}, f32[8,40,256]{2,1,0:T(8,128)S(1)}, f32[8,40,256]{2,1,0:T(8,128)S(1)}, f32[8,40,256]{2,1,0:T(8,128)S(1)}) custom-call(f32[32,2,256]{2,1,0:T(2,128)S(1)} %all_to_all.15.refs_0_, bf16[5,256,256]{2,1,0:T(8,128)(2,1)S(1)} %get-tuple-element.105.refs_1_, ...), custom_call_target="tpu_custom_call" | custom-call | tf_op jit(solution)/shard_map/states_and_sums/pallas_call | solution.py:93
  47.4 2.2 %collective-permute-start.5 = (f32[320,256]{1,0:T(8,128)S(1)}, f32[320,256]{1,0:T(8,128)S(1)}, u32[]{:S(2)}, u32[]{:S(2)}) collective-permute-start(f32[320,256]{1,0:T(8,128)S(1)} %bitcast.23), channel_id=1, source_target_pairs={{0,64},{64,128},{128,192},{192,0},{1,65},{65,129},{129,193},{193,1... | collective-permute-start | bytes 983048 | tf_op jit(solution)/shard_map/ppermute | solution.py:506
  49.6 2.1 %collective-permute-start.7 = (f32[320,256]{1,0:T(8,128)S(1)}, f32[320,256]{1,0:T(8,128)S(1)}, u32[]{:S(2)}, u32[]{:S(2)}) collective-permute-start(f32[320,256]{1,0:T(8,128)S(1)} %bitcast.21), channel_id=1, source_target_pairs={{0,128},{64,192},{128,0},{192,64},{1,129},{65,193},{129,1},{193,65... | collective-permute-start | bytes 983048 | tf_op jit(solution)/shard_map/ppermute | solution.py:506
  51.7 11.2 %collective-permute-done.5 = f32[320,256]{1,0:T(8,128)S(1)} collective-permute-done((f32[320,256]{1,0:T(8,128)S(1)}, f32[320,256]{1,0:T(8,128)S(1)}, u32[]{:S(2)}, u32[]{:S(2)}) %collective-permute-start.5) | collective-permute-done | bytes 327712 | tf_op jit(solution)/shard_map/ppermute | solution.py:506
  62.8 3.4 %collective-permute-done.6 = f32[320,256]{1,0:T(8,128)S(1)} collective-permute-done((f32[320,256]{1,0:T(8,128)S(1)}, f32[320,256]{1,0:T(8,128)S(1)}, u32[]{:S(2)}, u32[]{:S(2)}) %collective-permute-start.6) | collective-permute-done | bytes 327712 | tf_op jit(solution)/shard_map/ppermute | solution.py:506
  66.2 0.6 add_chunks.1
  66.9 13.6 %all_to_all.16.refs_0_ = f32[8,40,256]{2,1,0:T(8,128)S(1)} all-to-all(f32[8,40,256]{2,1,0:T(8,128)S(1)} %add_chunks.1), channel_id=1, replica_groups=mesh['y'=4,'z'=8,'x'=4,'core'=2] {'z'}, dimensions={0} | all-to-all | bytes 655360 | tf_op jit(solution)/shard_map/all_to_all | solution.py:612
  80.4 0.6 add_pieces.1
  81.0 0.0 copy-start.5
  81.0 13.7 %all_to_all.17.refs_0_ = f32[8,40,256]{2,1,0:T(8,128)S(1)} all-to-all(f32[8,40,256]{2,1,0:T(8,128)S(1)} %add_pieces.1), channel_id=1, replica_groups=mesh['y'=4,'z'=8,'x'=4,'core'=2] {'z'}, dimensions={0} | all-to-all | bytes 655360 | tf_op jit(solution)/shard_map/all_to_all | solution.py:614
  94.7 0.5 collective-permute-start.10
  95.3 1.5 %collective-permute-start.9 = (f32[320,256]{1,0:T(8,128)S(1)}, f32[320,256]{1,0:T(8,128)S(1)}, u32[]{:S(2)}, u32[]{:S(2)}) collective-permute-start(f32[320,256]{1,0:T(8,128)S(1)} %bitcast.13), channel_id=1, source_target_pairs={{0,192},{64,0},{128,64},{192,128},{1,193},{65,1},{129,65},{193,129... | collective-permute-start | bytes 983048 | tf_op jit(solution)/shard_map/ppermute | solution.py:506
  96.8 1.4 %collective-permute-start.8 = (f32[320,256]{1,0:T(8,128)S(1)}, f32[320,256]{1,0:T(8,128)S(1)}, u32[]{:S(2)}, u32[]{:S(2)}) collective-permute-start(f32[320,256]{1,0:T(8,128)S(1)} %bitcast.14), channel_id=1, source_target_pairs={{0,128},{64,192},{128,0},{192,64},{1,129},{65,193},{129,1},{193,65... | collective-permute-start | bytes 983048 | tf_op jit(solution)/shard_map/ppermute | solution.py:506
  98.1 0.8 in_time_order.1
  99.0 0.7 copy.15
  99.7 3.0 %collective-permute-done.10 = f32[320,256]{1,0:T(8,128)S(1)} collective-permute-done((f32[320,256]{1,0:T(8,128)S(1)}, f32[320,256]{1,0:T(8,128)S(1)}, u32[]{:S(2)}, u32[]{:S(2)}) %collective-permute-start.10) | collective-permute-done | bytes 327712 | tf_op jit(solution)/shard_map/ppermute | solution.py:506
  102.7 1.4 %first_blocks.1 = (f32[1024,256]{1,0:T(8,128)}, f32[256,256]{1,0:T(8,128)S(1)}, f32[32,256]{1,0:T(8,128)S(1)}) custom-call(f32[8,40,256]{2,1,0:T(8,128)S(1)} %all_to_all.17.refs_0_, f32[8,40,256]{2,1,0:T(8,128)S(1)} %bitcast.15), custom_call_target="tpu_custom_call" | custom-call | tf_op jit(solution)/shard_map/first_blocks/pallas_call | solution.py:93
  104.1 4.5 %collective-permute-done.9 = f32[320,256]{1,0:T(8,128)S(1)} collective-permute-done((f32[320,256]{1,0:T(8,128)S(1)}, f32[320,256]{1,0:T(8,128)S(1)}, u32[]{:S(2)}, u32[]{:S(2)}) %collective-permute-start.9) | collective-permute-done | bytes 327712 | tf_op jit(solution)/shard_map/ppermute | solution.py:506
  108.6 1.6 %last_blocks.1 = (f32[1024,256]{1,0:T(8,128)}, f32[256,256]{1,0:T(8,128)}, f32[1,1024]{1,0:T(1,128)}) custom-call(f32[8,40,256]{2,1,0:T(8,128)S(1)} %bitcast.20, f32[8,40,256]{2,1,0:T(8,128)S(1)} %bitcast.19, f32[1024,256]{1,0:T(8,128)} %get-tuple-element.126.refs_2_, f32[256,256]{1,0:T(8,128)S(1)} %get-tuple-element.127.refs_3_, ...), custom_call_target="tpu_custom_call", output_to_operand_aliasing={{0}: (2, {})} | custom-call | tf_op jit(solution)/shard_map/last_blocks/pallas_call | solution.py:93
  (18 shorter events, 0.1 us)
Async XLA Ops:
  0.6 9.2 %copy-start.2 = (f32[256,256]{1,0:T(8,128)S(1)}, f32[256,256]{1,0:T(8,128)}, u32[]{:S(2)}) copy-start(f32[256,256]{1,0:T(8,128)} %refs_1_.1) | copy-start | bytes 786436
  0.6 9.2 %copy-start.3 = (f32[256,256]{1,0:T(8,128)S(1)}, f32[256,256]{1,0:T(8,128)}, u32[]{:S(2)}) copy-start(f32[256,256]{1,0:T(8,128)} %refs_2_.3) | copy-start | bytes 786436
  0.7 9.2 %copy-start.4 = (f32[256,256]{1,0:T(8,128)S(1)}, f32[256,256]{1,0:T(8,128)}, u32[]{:S(2)}) copy-start(f32[256,256]{1,0:T(8,128)} %refs_3_.3) | copy-start | bytes 786436
  3.2 6.6 %copy-start.1 = (f32[256,256]{1,0:T(8,128)S(1)}, f32[256,256]{1,0:T(8,128)}, u32[]{:S(2)}) copy-start(f32[256,256]{1,0:T(8,128)} %refs_0_.3) | copy-start | bytes 786436
  3.2 1.4 %collective-permute-start = (f32[128,256]{1,0:T(8,128)S(1)}, f32[128,256]{1,0:T(8,128)S(1)}, u32[]{:S(2)}, u32[]{:S(2)}) collective-permute-start(f32[128,256]{1,0:T(8,128)S(1)} %get-tuple-element.69), channel_id=1, source_target_pairs={{0,1},{1,0},{2,3},{3,2},{4,5},{5,4},{6,7},{7,6},{8,9},{9,8},{10,11... | collective-permute-start | bytes 393224 | tf_op jit(solution)/shard_map/ppermute | solution.py:506
  4.7 12.2 %collective-permute-start.3 = (f32[128,256]{1,0:T(8,128)S(1)}, f32[128,256]{1,0:T(8,128)S(1)}, u32[]{:S(2)}, u32[]{:S(2)}) collective-permute-start(f32[128,256]{1,0:T(8,128)S(1)} %add.12), channel_id=1, source_target_pairs={{0,6},{2,0},{4,2},{6,4},{1,7},{3,1},{5,3},{7,5},{8,14},{10,8},{12,... | collective-permute-start | bytes 393224 | tf_op jit(solution)/shard_map/ppermute | solution.py:506
  7.5 9.4 %collective-permute-start.2 = (f32[128,256]{1,0:T(8,128)S(1)}, f32[128,256]{1,0:T(8,128)S(1)}, u32[]{:S(2)}, u32[]{:S(2)}) collective-permute-start(f32[128,256]{1,0:T(8,128)S(1)} %add.12), channel_id=1, source_target_pairs={{0,2},{2,4},{4,6},{6,0},{1,3},{3,5},{5,7},{7,1},{8,10},{10,12},{12... | collective-permute-start | bytes 393224 | tf_op jit(solution)/shard_map/ppermute | solution.py:506
  7.5 9.4 %collective-permute-start.1 = (f32[128,256]{1,0:T(8,128)S(1)}, f32[128,256]{1,0:T(8,128)S(1)}, u32[]{:S(2)}, u32[]{:S(2)}) collective-permute-start(f32[128,256]{1,0:T(8,128)S(1)} %add.12), channel_id=1, source_target_pairs={{0,4},{2,6},{4,0},{6,2},{1,5},{3,7},{5,1},{7,3},{8,12},{10,14},{12... | collective-permute-start | bytes 393224 | tf_op jit(solution)/shard_map/ppermute | solution.py:506
  16.9 2.1 %collective-permute-start.4 = (f32[128,256]{1,0:T(8,128)S(1)}, f32[128,256]{1,0:T(8,128)S(1)}, u32[]{:S(2)}, u32[]{:S(2)}) collective-permute-start(f32[128,256]{1,0:T(8,128)S(1)} %add_add_fusion.refs_0_), channel_id=1, source_target_pairs={{0,1},{1,0},{2,3},{3,2},{4,5},{5,4},{6,7},{7,6},{8,9},{9,8},{10,11... | collective-permute-start | bytes 393224 | tf_op jit(solution)/shard_map/ppermute | solution.py:506
  19.0 23.5 %copy-start = (bf16[1024,256]{1,0:T(8,128)(2,1)S(1)}, bf16[1024,256]{1,0:T(8,128)(2,1)}, u32[]{:S(2)}) copy-start(bf16[1024,256]{1,0:T(8,128)(2,1)} %refs_22_.1) | copy-start | bytes 1572868
  47.4 15.4 %collective-permute-start.5 = (f32[320,256]{1,0:T(8,128)S(1)}, f32[320,256]{1,0:T(8,128)S(1)}, u32[]{:S(2)}, u32[]{:S(2)}) collective-permute-start(f32[320,256]{1,0:T(8,128)S(1)} %bitcast.23), channel_id=1, source_target_pairs={{0,64},{64,128},{128,192},{192,0},{1,65},{65,129},{129,193},{193,1... | collective-permute-start | bytes 983048 | tf_op jit(solution)/shard_map/ppermute | solution.py:506
  49.6 16.6 %collective-permute-start.6 = (f32[320,256]{1,0:T(8,128)S(1)}, f32[320,256]{1,0:T(8,128)S(1)}, u32[]{:S(2)}, u32[]{:S(2)}) collective-permute-start(f32[320,256]{1,0:T(8,128)S(1)} %bitcast.22), channel_id=1, source_target_pairs={{0,192},{64,0},{128,64},{192,128},{1,193},{65,1},{129,65},{193,129... | collective-permute-start | bytes 983048 | tf_op jit(solution)/shard_map/ppermute | solution.py:506
  49.6 16.6 %collective-permute-start.7 = (f32[320,256]{1,0:T(8,128)S(1)}, f32[320,256]{1,0:T(8,128)S(1)}, u32[]{:S(2)}, u32[]{:S(2)}) collective-permute-start(f32[320,256]{1,0:T(8,128)S(1)} %bitcast.21), channel_id=1, source_target_pairs={{0,128},{64,192},{128,0},{192,64},{1,129},{65,193},{129,1},{193,65... | collective-permute-start | bytes 983048 | tf_op jit(solution)/shard_map/ppermute | solution.py:506
  81.0 17.1 %copy-start.5 = (bf16[256,256]{1,0:T(8,128)(2,1)S(1)}, bf16[256,256]{1,0:T(8,128)(2,1)}, u32[]{:S(2)}) copy-start(bf16[256,256]{1,0:T(8,128)(2,1)} %constant.5.clone.refs_0_) | copy-start | bytes 393220
  94.7 7.9 %collective-permute-start.10 = (f32[320,256]{1,0:T(8,128)S(1)}, f32[320,256]{1,0:T(8,128)S(1)}, u32[]{:S(2)}, u32[]{:S(2)}) collective-permute-start(f32[320,256]{1,0:T(8,128)S(1)} %bitcast.12), channel_id=1, source_target_pairs={{0,64},{64,128},{128,192},{192,0},{1,65},{65,129},{129,193},{193,1... | collective-permute-start | bytes 983048 | tf_op jit(solution)/shard_map/ppermute | solution.py:506
  95.3 13.3 %collective-permute-start.9 = (f32[320,256]{1,0:T(8,128)S(1)}, f32[320,256]{1,0:T(8,128)S(1)}, u32[]{:S(2)}, u32[]{:S(2)}) collective-permute-start(f32[320,256]{1,0:T(8,128)S(1)} %bitcast.13), channel_id=1, source_target_pairs={{0,192},{64,0},{128,64},{192,128},{1,193},{65,1},{129,65},{193,129... | collective-permute-start | bytes 983048 | tf_op jit(solution)/shard_map/ppermute | solution.py:506
  96.8 11.8 %collective-permute-start.8 = (f32[320,256]{1,0:T(8,128)S(1)}, f32[320,256]{1,0:T(8,128)S(1)}, u32[]{:S(2)}, u32[]{:S(2)}) collective-permute-start(f32[320,256]{1,0:T(8,128)S(1)} %bitcast.14), channel_id=1, source_target_pairs={{0,128},{64,192},{128,0},{192,64},{1,129},{65,193},{129,1},{193,65... | collective-permute-start | bytes 983048 | tf_op jit(solution)/shard_map/ppermute | solution.py:506

commit v6 on v5

--- a/solution.py
+++ b/solution.py
@@ -214,15 +214,12 @@
 
 def last_effects(a_h, a_l, b_h, b_l, m):
     m = m[...]
-    for level in range(FIRST, 8):
-        m_cut = cut(m)
-        if level > FIRST:
-            yield from put(0, level - FIRST - 1, m_cut)
-        a_cut = (a_h[level], a_l[level], m.shape[0])
-        n_cut = cut(mul(a_cut, m_cut))
-        yield from put(2, level - FIRST, n_cut)
-        m = m + mul(n_cut, (b_h[level], b_l[level]))
-    yield from put(4, None, cut(m))
+    a_cut = (a_h[FIRST], a_l[FIRST], m.shape[0])
+    n_cut = cut(mul(a_cut, cut(m)))
+    yield from put(2, 0, n_cut)
+    m = m + mul(n_cut, (b_h[FIRST], b_l[FIRST]))
+    yield from put(0, 0, cut(m))
+    yield 4, None, m
 
 
 def information_part(order, noise_precision, emission, observations):
@@ -320,8 +317,7 @@
     a_big_l,
     lead_h,
     lead_l,
-    m_h,
-    m_l,
+    m,
     b_big_h,
     b_big_l,
     sub_ends,
@@ -342,6 +338,9 @@
 ):
     block = lax.axis_index("y") * N_Z + lax.axis_index("z")
     width = shown.shape[1]
+    m = m[...]
+    n_cut = cut(mul((a_h[7], a_l[7], m.shape[0]), cut(m)))
+    m_whole = cut(m + mul(n_cut, (b_h[7], b_l[7])))
     gathered = gathered[...]
     after = gathered[:, 0]
     index = row_index(after)
@@ -350,7 +349,7 @@
         before = jnp.where(index >= by, roll(after, by), 0.0)
         after = after + mul(cut(before), at([(a_big_h, a_big_l)], level))
     enter = jnp.where(index >= 1, roll(after, 1), 0.0)
-    follow = gathered[:, 1] + mul(cut(enter), (m_h[...], m_l[...]))
+    follow = gathered[:, 1] + mul(cut(enter), m_whole[:2])
     final = after - mul(cut(after), at([(lead_h, lead_l)], 4))
     follow = jnp.where(index < BLOCKS - 1, roll(follow, -1), final)
     for level in range(5):
@@ -367,7 +366,8 @@
 
     def children(enter, follow, level):
         enter = cut(enter)
-        first = mul(enter, at([(n_h, n_l), (n_last_h, n_last_l)], level)) + mul(cut(follow), at([(b_h, b_l)], level))
+        n_level = n_cut[:2] if level == 7 else at([(n_h, n_l), (n_last_h, n_last_l)], level)
+        first = mul(enter, n_level) + mul(cut(follow), at([(b_h, b_l)], level))
         return mul(enter, at([(a_h, a_l)], level)), first
 
     enter, follow = picked(enter), picked(follow)
@@ -555,7 +555,7 @@
     lead, a_cut, b_cut, m_cut, n_cut, a_big, b_big = (known[i : i + 2] for i in range(0, 14, 2))
     late = call(
         last_effects,
-        stack(7 - FIRST) + stack(8 - FIRST) + [(square, BF16)] * 2,
+        stack(1) * 2 + [(square, F32)],
         *a_cut,
         *b_cut,
         known[14],

time: 111 us -> 110 us (level)
  transfers between devices with their start and end apart: 11 -> 11, of which waited for: 5 -> 6; matrix products, arithmetic and copies ran while one was open for 1% -> 1% of each run, Pallas kernels for 10% -> 10%
where the time goes in v6:
time: 110 us
  blocking collectives  46.7 us (42%)
  Pallas kernels  25.1 us (23%)
  waiting for transfers between devices  23.2 us (21%)
  starting transfers between devices  12.7 us (12%)
    pallas_call x10, Pallas kernels, call(): pl.pallas_call(kernel, out_shape=[(pltpu.HBM if i in sent else pltpu.VMEM...  25.1 us
    ppermute x11, waiting for transfers between devices, shift(): lax.ppermute(value, axis, [(i, (i + by) % count) for i in range(count)])  23.2 us
    all_to_all x1, blocking collectives, local(): gathered = lax.all_to_all(ends, ('y', 'z'), 0, 0)  19.5 us
    all_to_all x1, blocking collectives, local(): whole = lax.all_to_all(spread, 'z', 0, 0)  13.7 us
    all_to_all x1, blocking collectives, local(): payload = lax.all_to_all(payload, 'z', 0, 0)  13.6 us
    ppermute x11, starting transfers between devices, shift(): lax.ppermute(value, axis, [(i, (i + by) % count) for i in range(count)])  12.7 us
  transfers between devices with their start and end apart: 11, of which 6 were waited for; matrix products, arithmetic and copies ran while one was open for 1% of the time, Pallas kernels for 10%

profile of v6, /device:TPU:24, one launch (start us, length us, event | category | flops | bytes accessed | tf_op | source)
XLA Modules:
  0.0 109.5 jit_solution(7995870479344133967)
XLA Ops:
  0.7 2.5 %information_part.1 = (f32[128,256]{1,0:T(8,128)S(1)}, f32[128,256]{1,0:T(8,128)S(1)}, bf16[256,1024]{1,0:T(8,128)(2,1)S(1)}) custom-call(bf16[256,256]{1,0:T(8,128)(2,1)} %constant.4.clone.refs_0_, f32[1,1024]{1,0:T(1,128)} %bitcast.24, bf16[1024,256]{1,0:T(8,128)(2,1)} %refs_21_.1, bf16[256,1024]{1,0:T(8,128)(2,1)} %refs_3_.2), custom_call_target="tpu_custom_call" | custom-call | tf_op jit(solution)/shard_map/information_part/pallas_call | solution.py:93
  3.2 0.0 copy-start.1
  3.2 0.1 collective-permute-start
  3.3 1.3 %collective-permute-done = f32[128,256]{1,0:T(8,128)S(1)} collective-permute-done((f32[128,256]{1,0:T(8,128)S(1)}, f32[128,256]{1,0:T(8,128)S(1)}, u32[]{:S(2)}, u32[]{:S(2)}) %collective-permute-start) | collective-permute-done | bytes 131104 | tf_op jit(solution)/shard_map/ppermute | solution.py:506
  4.7 2.8 %collective-permute-start.3 = (f32[128,256]{1,0:T(8,128)S(1)}, f32[128,256]{1,0:T(8,128)S(1)}, u32[]{:S(2)}, u32[]{:S(2)}) collective-permute-start(f32[128,256]{1,0:T(8,128)S(1)} %add.12), channel_id=1, source_target_pairs={{0,6},{2,0},{4,2},{6,4},{1,7},{3,1},{5,3},{7,5},{8,14},{10,8},{12,... | collective-permute-start | bytes 393224 | tf_op jit(solution)/shard_map/ppermute | solution.py:506
  7.5 0.0 collective-permute-start.2
  7.5 2.3 %collective-permute-start.1 = (f32[128,256]{1,0:T(8,128)S(1)}, f32[128,256]{1,0:T(8,128)S(1)}, u32[]{:S(2)}, u32[]{:S(2)}) collective-permute-start(f32[128,256]{1,0:T(8,128)S(1)} %add.12), channel_id=1, source_target_pairs={{0,4},{2,6},{4,0},{6,2},{1,5},{3,7},{5,1},{7,3},{8,12},{10,14},{12... | collective-permute-start | bytes 393224 | tf_op jit(solution)/shard_map/ppermute | solution.py:506
  9.8 7.0 %powers.1 = (bf16[5,256,256]{2,1,0:T(8,128)(2,1)S(1)}, bf16[5,256,256]{2,1,0:T(8,128)(2,1)S(1)}, bf16[8,256,256]{2,1,0:T(8,128)(2,1)S(1)}, bf16[8,256,256]{2,1,0...) custom-call(f32[256,256]{1,0:T(8,128)S(1)} %copy-done.1, ...), custom_call_target="tpu_custom_call" | custom-call | tf_op jit(solution)/shard_map/powers/pallas_call | solution.py:93
  16.9 0.1 collective-permute-start.4
  17.0 1.2 %last_effects.1 = (bf16[1,256,256]{2,1,0:T(8,128)(2,1)S(1)}, bf16[1,256,256]{2,1,0:T(8,128)(2,1)S(1)}, bf16[1,256,256]{2,1,0:T(8,128)(2,1)S(1)}, bf16[1,256,256]{2,1,0:T(8,128)(2,1)S(1)}, f32[256,256]{1,0:T(8,128)S(1)}) custom-call(bf16[8,256,256]{2,1,0:T(8,128)(2,1)S(1)} %get-tuple-element.90.refs_0_.refs_10_, ...), custom_call_target="tpu_custom_call" | custom-call | tf_op jit(solution)/shard_map/last_effects/pallas_call | solution.py:93
  18.2 0.1 collective-permute-done.4.refs_1_
  18.4 4.0 %block_tree.1 = (f32[32,2,256]{2,1,0:T(2,128)S(1)}, f32[256,256]{1,0:T(8,128)S(1)}, f32[248,256]{1,0:T(8,128)S(1)}, f32[248,256]{1,0:T(8,128)S(1)}, f32[24,256]{1,0:T(8,128)S(1)}, /*index=5*/f32[24,256]{1,0:T(8,128)S(1)}) custom-call(f32[128,256]{1,0:T(8,128)S(1)} %add_add_fusion.refs_0_, f32[128,256]{1,0:T(8,128)S(1)} %collective-permute-done.4.refs_1_, ...), custom_call_target="tpu_custom_call" | custom-call | tf_op jit(solution)/shard_map/block_tree/pallas_call | solution.py:93
  22.4 19.5 %all_to_all.15.refs_0_ = f32[32,2,256]{2,1,0:T(2,128)S(1)} all-to-all(f32[32,2,256]{2,1,0:T(2,128)S(1)} %get-tuple-element.101), channel_id=1, replica_groups=mesh['y'=4,'z'=8,'x'=4,'core'=2] {'y','z'}, dimensions={0} | all-to-all | bytes 131072 | tf_op jit(solution)/shard_map/all_to_all | solution.py:585
  41.9 5.2 %states_and_sums.1 = (f32[256,256]{1,0:T(8,128)S(1)}, f32[8,40,256]{2,1,0:T(8,128)S(1)}, f32[8,40,256]{2,1,0:T(8,128)S(1)}, f32[8,40,256]{2,1,0:T(8,128)S(1)}, f32[8,40,256]{2,1,0:T(8,128)S(1)}) custom-call(f32[32,2,256]{2,1,0:T(2,128)S(1)} %all_to_all.15.refs_0_, bf16[5,256,256]{2,1,0:T(8,128)(2,1)S(1)} %get-tuple-element.102.refs_1_, ...), custom_call_target="tpu_custom_call" | custom-call | tf_op jit(solution)/shard_map/states_and_sums/pallas_call | solution.py:93
  47.1 2.1 %collective-permute-start.5 = (f32[320,256]{1,0:T(8,128)S(1)}, f32[320,256]{1,0:T(8,128)S(1)}, u32[]{:S(2)}, u32[]{:S(2)}) collective-permute-start(f32[320,256]{1,0:T(8,128)S(1)} %bitcast.23), channel_id=1, source_target_pairs={{0,64},{64,128},{128,192},{192,0},{1,65},{65,129},{129,193},{193,1... | collective-permute-start | bytes 983048 | tf_op jit(solution)/shard_map/ppermute | solution.py:506
  49.3 2.1 %collective-permute-start.7 = (f32[320,256]{1,0:T(8,128)S(1)}, f32[320,256]{1,0:T(8,128)S(1)}, u32[]{:S(2)}, u32[]{:S(2)}) collective-permute-start(f32[320,256]{1,0:T(8,128)S(1)} %bitcast.21), channel_id=1, source_target_pairs={{0,128},{64,192},{128,0},{192,64},{1,129},{65,193},{129,1},{193,65... | collective-permute-start | bytes 983048 | tf_op jit(solution)/shard_map/ppermute | solution.py:506
  51.3 11.0 %collective-permute-done.5 = f32[320,256]{1,0:T(8,128)S(1)} collective-permute-done((f32[320,256]{1,0:T(8,128)S(1)}, f32[320,256]{1,0:T(8,128)S(1)}, u32[]{:S(2)}, u32[]{:S(2)}) %collective-permute-start.5) | collective-permute-done | bytes 327712 | tf_op jit(solution)/shard_map/ppermute | solution.py:506
  62.4 3.4 %collective-permute-done.6 = f32[320,256]{1,0:T(8,128)S(1)} collective-permute-done((f32[320,256]{1,0:T(8,128)S(1)}, f32[320,256]{1,0:T(8,128)S(1)}, u32[]{:S(2)}, u32[]{:S(2)}) %collective-permute-start.6) | collective-permute-done | bytes 327712 | tf_op jit(solution)/shard_map/ppermute | solution.py:506
  65.8 0.6 add_chunks.1
  66.4 13.6 %all_to_all.16.refs_0_ = f32[8,40,256]{2,1,0:T(8,128)S(1)} all-to-all(f32[8,40,256]{2,1,0:T(8,128)S(1)} %add_chunks.1), channel_id=1, replica_groups=mesh['y'=4,'z'=8,'x'=4,'core'=2] {'z'}, dimensions={0} | all-to-all | bytes 655360 | tf_op jit(solution)/shard_map/all_to_all | solution.py:612
  80.0 0.6 add_pieces.1
  80.6 0.0 copy-start.5
  80.6 13.7 %all_to_all.17.refs_0_ = f32[8,40,256]{2,1,0:T(8,128)S(1)} all-to-all(f32[8,40,256]{2,1,0:T(8,128)S(1)} %add_pieces.1), channel_id=1, replica_groups=mesh['y'=4,'z'=8,'x'=4,'core'=2] {'z'}, dimensions={0} | all-to-all | bytes 655360 | tf_op jit(solution)/shard_map/all_to_all | solution.py:614
  94.3 0.3 collective-permute-start.10
  94.6 1.7 %collective-permute-start.9 = (f32[320,256]{1,0:T(8,128)S(1)}, f32[320,256]{1,0:T(8,128)S(1)}, u32[]{:S(2)}, u32[]{:S(2)}) collective-permute-start(f32[320,256]{1,0:T(8,128)S(1)} %bitcast.13), channel_id=1, source_target_pairs={{0,192},{64,0},{128,64},{192,128},{1,193},{65,1},{129,65},{193,129... | collective-permute-start | bytes 983048 | tf_op jit(solution)/shard_map/ppermute | solution.py:506
  96.3 1.1 %collective-permute-start.8 = (f32[320,256]{1,0:T(8,128)S(1)}, f32[320,256]{1,0:T(8,128)S(1)}, u32[]{:S(2)}, u32[]{:S(2)}) collective-permute-start(f32[320,256]{1,0:T(8,128)S(1)} %bitcast.14), channel_id=1, source_target_pairs={{0,128},{64,192},{128,0},{192,64},{1,129},{65,193},{129,1},{193,65... | collective-permute-start | bytes 983048 | tf_op jit(solution)/shard_map/ppermute | solution.py:506
  97.4 0.8 in_time_order.1
  98.3 0.7 copy.15
  99.0 2.9 %collective-permute-done.10 = f32[320,256]{1,0:T(8,128)S(1)} collective-permute-done((f32[320,256]{1,0:T(8,128)S(1)}, f32[320,256]{1,0:T(8,128)S(1)}, u32[]{:S(2)}, u32[]{:S(2)}) %collective-permute-start.10) | collective-permute-done | bytes 327712 | tf_op jit(solution)/shard_map/ppermute | solution.py:506
  101.9 1.4 %first_blocks.1 = (f32[1024,256]{1,0:T(8,128)}, f32[256,256]{1,0:T(8,128)S(1)}, f32[32,256]{1,0:T(8,128)S(1)}) custom-call(f32[8,40,256]{2,1,0:T(8,128)S(1)} %all_to_all.17.refs_0_, f32[8,40,256]{2,1,0:T(8,128)S(1)} %bitcast.15), custom_call_target="tpu_custom_call" | custom-call | tf_op jit(solution)/shard_map/first_blocks/pallas_call | solution.py:93
  103.3 4.5 %collective-permute-done.9 = f32[320,256]{1,0:T(8,128)S(1)} collective-permute-done((f32[320,256]{1,0:T(8,128)S(1)}, f32[320,256]{1,0:T(8,128)S(1)}, u32[]{:S(2)}, u32[]{:S(2)}) %collective-permute-start.9) | collective-permute-done | bytes 327712 | tf_op jit(solution)/shard_map/ppermute | solution.py:506
  107.7 1.6 %last_blocks.1 = (f32[1024,256]{1,0:T(8,128)}, f32[256,256]{1,0:T(8,128)}, f32[1,1024]{1,0:T(1,128)}) custom-call(f32[8,40,256]{2,1,0:T(8,128)S(1)} %bitcast.20, f32[8,40,256]{2,1,0:T(8,128)S(1)} %bitcast.19, f32[1024,256]{1,0:T(8,128)} %get-tuple-element.122.refs_2_, f32[256,256]{1,0:T(8,128)S(1)} %get-tuple-element.123.refs_3_, ...), custom_call_target="tpu_custom_call", output_to_operand_aliasing={{0}: (2, {})} | custom-call | tf_op jit(solution)/shard_map/last_blocks/pallas_call | solution.py:93
  (18 shorter events, 0.1 us)
Async XLA Ops:
  0.6 9.2 %copy-start.2 = (f32[256,256]{1,0:T(8,128)S(1)}, f32[256,256]{1,0:T(8,128)}, u32[]{:S(2)}) copy-start(f32[256,256]{1,0:T(8,128)} %refs_1_.1) | copy-start | bytes 786436
  0.6 9.2 %copy-start.3 = (f32[256,256]{1,0:T(8,128)S(1)}, f32[256,256]{1,0:T(8,128)}, u32[]{:S(2)}) copy-start(f32[256,256]{1,0:T(8,128)} %refs_2_.3) | copy-start | bytes 786436
  0.7 9.2 %copy-start.4 = (f32[256,256]{1,0:T(8,128)S(1)}, f32[256,256]{1,0:T(8,128)}, u32[]{:S(2)}) copy-start(f32[256,256]{1,0:T(8,128)} %refs_3_.3) | copy-start | bytes 786436
  3.2 6.6 %copy-start.1 = (f32[256,256]{1,0:T(8,128)S(1)}, f32[256,256]{1,0:T(8,128)}, u32[]{:S(2)}) copy-start(f32[256,256]{1,0:T(8,128)} %refs_0_.3) | copy-start | bytes 786436
  3.2 1.4 %collective-permute-start = (f32[128,256]{1,0:T(8,128)S(1)}, f32[128,256]{1,0:T(8,128)S(1)}, u32[]{:S(2)}, u32[]{:S(2)}) collective-permute-start(f32[128,256]{1,0:T(8,128)S(1)} %get-tuple-element.67), channel_id=1, source_target_pairs={{0,1},{1,0},{2,3},{3,2},{4,5},{5,4},{6,7},{7,6},{8,9},{9,8},{10,11... | collective-permute-start | bytes 393224 | tf_op jit(solution)/shard_map/ppermute | solution.py:506
  4.7 12.2 %collective-permute-start.3 = (f32[128,256]{1,0:T(8,128)S(1)}, f32[128,256]{1,0:T(8,128)S(1)}, u32[]{:S(2)}, u32[]{:S(2)}) collective-permute-start(f32[128,256]{1,0:T(8,128)S(1)} %add.12), channel_id=1, source_target_pairs={{0,6},{2,0},{4,2},{6,4},{1,7},{3,1},{5,3},{7,5},{8,14},{10,8},{12,... | collective-permute-start | bytes 393224 | tf_op jit(solution)/shard_map/ppermute | solution.py:506
  7.5 9.4 %collective-permute-start.2 = (f32[128,256]{1,0:T(8,128)S(1)}, f32[128,256]{1,0:T(8,128)S(1)}, u32[]{:S(2)}, u32[]{:S(2)}) collective-permute-start(f32[128,256]{1,0:T(8,128)S(1)} %add.12), channel_id=1, source_target_pairs={{0,2},{2,4},{4,6},{6,0},{1,3},{3,5},{5,7},{7,1},{8,10},{10,12},{12... | collective-permute-start | bytes 393224 | tf_op jit(solution)/shard_map/ppermute | solution.py:506
  7.5 9.4 %collective-permute-start.1 = (f32[128,256]{1,0:T(8,128)S(1)}, f32[128,256]{1,0:T(8,128)S(1)}, u32[]{:S(2)}, u32[]{:S(2)}) collective-permute-start(f32[128,256]{1,0:T(8,128)S(1)} %add.12), channel_id=1, source_target_pairs={{0,4},{2,6},{4,0},{6,2},{1,5},{3,7},{5,1},{7,3},{8,12},{10,14},{12... | collective-permute-start | bytes 393224 | tf_op jit(solution)/shard_map/ppermute | solution.py:506
  16.9 1.4 %collective-permute-start.4 = (f32[128,256]{1,0:T(8,128)S(1)}, f32[128,256]{1,0:T(8,128)S(1)}, u32[]{:S(2)}, u32[]{:S(2)}) collective-permute-start(f32[128,256]{1,0:T(8,128)S(1)} %add_add_fusion.refs_0_), channel_id=1, source_target_pairs={{0,1},{1,0},{2,3},{3,2},{4,5},{5,4},{6,7},{7,6},{8,9},{9,8},{10,11... | collective-permute-start | bytes 393224 | tf_op jit(solution)/shard_map/ppermute | solution.py:506
  18.4 23.5 %copy-start = (bf16[1024,256]{1,0:T(8,128)(2,1)S(1)}, bf16[1024,256]{1,0:T(8,128)(2,1)}, u32[]{:S(2)}) copy-start(bf16[1024,256]{1,0:T(8,128)(2,1)} %refs_21_.1) | copy-start | bytes 1572868
  47.1 15.3 %collective-permute-start.5 = (f32[320,256]{1,0:T(8,128)S(1)}, f32[320,256]{1,0:T(8,128)S(1)}, u32[]{:S(2)}, u32[]{:S(2)}) collective-permute-start(f32[320,256]{1,0:T(8,128)S(1)} %bitcast.23), channel_id=1, source_target_pairs={{0,64},{64,128},{128,192},{192,0},{1,65},{65,129},{129,193},{193,1... | collective-permute-start | bytes 983048 | tf_op jit(solution)/shard_map/ppermute | solution.py:506
  49.3 16.5 %collective-permute-start.6 = (f32[320,256]{1,0:T(8,128)S(1)}, f32[320,256]{1,0:T(8,128)S(1)}, u32[]{:S(2)}, u32[]{:S(2)}) collective-permute-start(f32[320,256]{1,0:T(8,128)S(1)} %bitcast.22), channel_id=1, source_target_pairs={{0,192},{64,0},{128,64},{192,128},{1,193},{65,1},{129,65},{193,129... | collective-permute-start | bytes 983048 | tf_op jit(solution)/shard_map/ppermute | solution.py:506
  49.3 16.5 %collective-permute-start.7 = (f32[320,256]{1,0:T(8,128)S(1)}, f32[320,256]{1,0:T(8,128)S(1)}, u32[]{:S(2)}, u32[]{:S(2)}) collective-permute-start(f32[320,256]{1,0:T(8,128)S(1)} %bitcast.21), channel_id=1, source_target_pairs={{0,128},{64,192},{128,0},{192,64},{1,129},{65,193},{129,1},{193,65... | collective-permute-start | bytes 983048 | tf_op jit(solution)/shard_map/ppermute | solution.py:506
  80.6 16.9 %copy-start.5 = (bf16[256,256]{1,0:T(8,128)(2,1)S(1)}, bf16[256,256]{1,0:T(8,128)(2,1)}, u32[]{:S(2)}) copy-start(bf16[256,256]{1,0:T(8,128)(2,1)} %constant.5.clone.refs_0_) | copy-start | bytes 393220
  94.3 7.6 %collective-permute-start.10 = (f32[320,256]{1,0:T(8,128)S(1)}, f32[320,256]{1,0:T(8,128)S(1)}, u32[]{:S(2)}, u32[]{:S(2)}) collective-permute-start(f32[320,256]{1,0:T(8,128)S(1)} %bitcast.12), channel_id=1, source_target_pairs={{0,64},{64,128},{128,192},{192,0},{1,65},{65,129},{129,193},{193,1... | collective-permute-start | bytes 983048 | tf_op jit(solution)/shard_map/ppermute | solution.py:506
  94.6 13.2 %collective-permute-start.9 = (f32[320,256]{1,0:T(8,128)S(1)}, f32[320,256]{1,0:T(8,128)S(1)}, u32[]{:S(2)}, u32[]{:S(2)}) collective-permute-start(f32[320,256]{1,0:T(8,128)S(1)} %bitcast.13), channel_id=1, source_target_pairs={{0,192},{64,0},{128,64},{192,128},{1,193},{65,1},{129,65},{193,129... | collective-permute-start | bytes 983048 | tf_op jit(solution)/shard_map/ppermute | solution.py:506
  96.3 11.4 %collective-permute-start.8 = (f32[320,256]{1,0:T(8,128)S(1)}, f32[320,256]{1,0:T(8,128)S(1)}, u32[]{:S(2)}, u32[]{:S(2)}) collective-permute-start(f32[320,256]{1,0:T(8,128)S(1)} %bitcast.14), channel_id=1, source_target_pairs={{0,128},{64,192},{128,0},{192,64},{1,129},{65,193},{129,1},{193,65... | collective-permute-start | bytes 983048 | tf_op jit(solution)/shard_map/ppermute | solution.py:506
